TPU v7x, 32 devices: a whole 2x2x4 slice. The times are simulated.
32 devices in a mesh: seq: 16 (over z, y, core), mp: 2 (over x).
Axes of the slice: x: 2, y: 2, z: 4, core: 2. Of those that a mesh axis runs over, the one named last changes fastest.
Arguments:
- patches: bfloat16 [4096, 64], P('seq'), may hold values from -6 to 6
- clip_shape: int32 [8, 3], replicated, may hold values from 1 to 16, as said below
- shard_counts: int32 [16], replicated, may hold values from 1 to 256, as said below
- patch_weight: bfloat16 [64, 2560], P(None, 'mp'), may hold values from -3 to 3
- patch_bias: float32 [2560], P('mp'), may hold values from -6 to 6
- time_mod: float32 [8, 2, 2560], P(None, None, 'mp'), may hold values from -6 to 6
- block_mod: float32 [2, 2560], P(None, 'mp'), may hold values from -4 to 4
- w_query: bfloat16 [2560, 2560], P('seq', 'mp'), may hold values from -0.47434165 to 0.47434165
- query_bias: float32 [2560], P('mp'), may hold values from -4 to 4
- w_keyvalue: bfloat16 [2560, 5120], P('seq', 'mp'), may hold values from -0.47434165 to 0.47434165
- keyvalue_bias: float32 [5120], P('mp'), may hold values from -6 to 6
- norm_gain: float32 [2, 2560], P(None, 'mp'), may hold values from 1 to 2
Outputs:
- attention: bfloat16 [4096, 2560], P('seq', 'mp')
Inputs may be any that keep to these rules, and one draw needn't show every extreme that they name: `clip_shape`: clip c lies on shards 2 c to 2 c + 1. Frames run from 1 to 2, patch rows from 8 to 16, patch columns from 8 to 16; some clip has 2 frames of 16 by 16 patches. `shard_counts`: the counts of clip c's 2 shards add up to the product of clip_shape[c].
All inputs are finite; a program needn't handle non-finite values.
Results may differ from a plain program's by a relative error of at most 0.0063.
Values may be sent and summed in bfloat16 or wider, within the bound.
No kernel may reach another device: no remote copies, remote signals or barrier semaphores. Data moves between devices by JAX's collectives and lax.ppermute only.
A program may use at most 128 MiB of HBM per device.

v0:
```python
import math

import jax
import jax.numpy as jnp
from jax import lax
from jax.sharding import PartitionSpec as P

D = 2560
HEADS = 20
HD = 128
GROUP = 2


EPSILON = 1e-06


def partner_2(value, axis, apart):
    mask = 2**apart
    pairs = [(source, source ^ mask) for source in range(lax.axis_size(axis))]
    return lax.ppermute(value, axis, pairs)


def token_places(group_counts, member_ids, slot_ids, shape_row):
    before = jnp.cumsum(group_counts) - group_counts
    lookup = jnp.arange(GROUP, dtype=jnp.int32)[None, :] == member_ids[:, None]
    offset = jnp.sum(jnp.where(lookup, before[None, :], 0), axis=1)
    holding = jnp.sum(jnp.where(lookup, group_counts[None, :], 0), axis=1)
    position = offset + slot_ids
    plane_size = shape_row[1] * shape_row[2]
    frame_pos = position // plane_size
    row_pos = position // shape_row[2] % shape_row[1]
    col_pos = position % shape_row[2]
    return (slot_ids < holding, frame_pos, row_pos, col_pos)


def rotary_tables(frame_pos, row_pos, col_pos):
    other_pairs = HD // 6
    frame_pairs = HD // 2 - 2 * other_pairs
    pair_id = jnp.arange(HD, dtype=jnp.int32) // 2
    in_frame = pair_id < frame_pairs
    in_row = jnp.logical_and(pair_id >= frame_pairs, pair_id < frame_pairs + other_pairs)
    within = jnp.where(
        in_frame,
        pair_id,
        jnp.where(in_row, pair_id - frame_pairs, pair_id - frame_pairs - other_pairs),
    ).astype(jnp.float32)
    axis_span = jnp.where(in_frame, 2.0 * frame_pairs, 2.0 * other_pairs).astype(jnp.float32)
    inverse = jnp.exp(-(2.0 * within / axis_span) * math.log(10000.0))
    position = jnp.where(
        in_frame[None, :],
        frame_pos[:, None],
        jnp.where(in_row[None, :], row_pos[:, None], col_pos[:, None]),
    ).astype(jnp.float32)
    angles = position * inverse[None, :]
    return (jnp.cos(angles), jnp.sin(angles))


def rotate_pairs(values, cosine_table, sine_table):
    parity = jnp.arange(HD, dtype=jnp.int32) % 2 == 0
    partner = jnp.where(parity, -jnp.roll(values, -1, axis=-1), jnp.roll(values, 1, axis=-1))
    return values * cosine_table[:, None, :] + partner * sine_table[:, None, :]


def modulate_rows(embedded, row_sums, squares, modulation):
    average = row_sums / D
    variance = squares / D - average * average
    normed = (embedded - average[:, None]) * lax.rsqrt(variance[:, None] + EPSILON)
    return (normed * (1.0 + modulation[1]) + modulation[0]).astype(jnp.bfloat16)


def finish_heads(raw_rows, squares, scale_gain, cosine_table, sine_table):
    normed = raw_rows * lax.rsqrt(squares[:, None] / (HEADS * HD) + EPSILON) * scale_gain
    return rotate_pairs(normed.reshape(raw_rows.shape[0], -1, HD), cosine_table, sine_table).astype(
        jnp.bfloat16
    )


def contract(left_rows, pieces):
    return jnp.dot(left_rows, pieces, preferred_element_type=jnp.float32)


def split_pairs(pair_acc, keyvalue_bias, heads_here):
    tokens = pair_acc.shape[0]
    pair_raw = (pair_acc + keyvalue_bias).reshape(tokens, heads_here, 2, HD)
    key_raw = pair_raw[:, :, 0].reshape(tokens, heads_here * HD)
    value_rows = pair_raw[:, :, 1].reshape(tokens, heads_here * HD).astype(jnp.bfloat16)
    return (key_raw, value_rows)


def count_of(group_counts, source):
    return jnp.sum(jnp.where(jnp.arange(GROUP, dtype=jnp.int32) == source, group_counts, 0))


def gather_group(key_rows, value_rows, member):
    tokens = value_rows.shape[0]
    blocks = jnp.stack([key_rows.reshape(tokens, -1), value_rows])
    sources = [member]
    partner = partner_2(blocks, "seq", 0)
    blocks = jnp.concatenate([blocks, partner], axis=1)
    sources = sources + [jnp.bitwise_xor(source, 1 << 0) for source in sources]
    return (blocks, sources)


def attend_rows(queries, all_keys, all_values, key_valid):
    scores = jnp.einsum(
        "qhd,khd->hqk", queries, all_keys, preferred_element_type=jnp.float32
    ) * HD ** (-0.5)
    weights = jnp.where(key_valid[None, None, :], jnp.exp(scores), 0.0)
    totals = jnp.sum(weights, axis=-1)
    numerator = jnp.einsum(
        "hqk,khd->qhd", weights.astype(jnp.bfloat16), all_values, preferred_element_type=jnp.float32
    )
    return numerator / jnp.transpose(totals)[:, :, None]


def shards(
    patches,
    clip_shape,
    shard_counts,
    patch_weight,
    patch_bias,
    time_mod,
    block_mod,
    w_query,
    query_bias,
    w_keyvalue,
    keyvalue_bias,
    norm_gain,
):
    tokens = patches.shape[0]
    heads_here = w_query.shape[1] // HD
    seq_index = lax.axis_index("seq")
    clip_id = seq_index // GROUP
    member = seq_index % GROUP
    group_counts = lax.dynamic_slice_in_dim(shard_counts, clip_id * GROUP, GROUP, 0)
    shape_row = lax.dynamic_index_in_dim(clip_shape, clip_id, 0, keepdims=False)
    slot_ids = jnp.arange(tokens, dtype=jnp.int32)
    is_valid, frame_pos, row_pos, col_pos = token_places(
        group_counts, jnp.full((tokens,), member, jnp.int32), slot_ids, shape_row
    )
    modulation = lax.dynamic_index_in_dim(time_mod, clip_id, 0, keepdims=False) + block_mod
    full_weight = lax.all_gather(patch_weight, "mp", axis=1, tiled=True)
    full_bias, full_mod = (
        lax.all_gather(patch_bias, "mp", axis=0, tiled=True),
        lax.all_gather(modulation, "mp", axis=1, tiled=True),
    )
    embedded = jnp.dot(patches, full_weight, preferred_element_type=jnp.float32) + full_bias
    hidden = modulate_rows(
        embedded, jnp.sum(embedded, axis=1), jnp.sum(embedded * embedded, axis=1), full_mod
    )
    cosine_table, sine_table = rotary_tables(frame_pos, row_pos, col_pos)
    query_acc = contract(hidden, lax.all_gather(w_query, "seq", axis=0, tiled=True))
    pair_acc = contract(hidden, lax.all_gather(w_keyvalue, "seq", axis=0, tiled=True))
    query_raw = query_acc + query_bias
    key_raw, value_rows = split_pairs(pair_acc, keyvalue_bias, heads_here)
    query_squares, key_squares = lax.psum(
        (jnp.sum(query_raw * query_raw, axis=1), jnp.sum(key_raw * key_raw, axis=1)), "mp"
    )
    queries = finish_heads(query_raw, query_squares, norm_gain[0], cosine_table, sine_table)
    key_rows = finish_heads(key_raw, key_squares, norm_gain[1], cosine_table, sine_table)
    blocks, sources = gather_group(key_rows, value_rows, member)
    key_valid = jnp.concatenate([slot_ids < count_of(group_counts, source) for source in sources])
    all_keys = blocks[0].reshape(-1, heads_here, HD)
    all_values = blocks[1].reshape(-1, heads_here, HD)
    result = attend_rows(queries, all_keys, all_values, key_valid)
    result = jnp.where(is_valid[:, None, None], result, 0.0)
    return result.reshape(tokens, heads_here * HD).astype(jnp.bfloat16)


def solution(mesh):
    return jax.shard_map(
        shards,
        mesh=mesh,
        in_specs=(
            P("seq", None),
            P(),
            P(),
            P(None, "mp"),
            P("mp"),
            P(None, None, "mp"),
            P(None, "mp"),
            P("seq", "mp"),
            P("mp"),
            P("seq", "mp"),
            P("mp"),
            P(None, "mp"),
        ),
        out_specs=P("seq", "mp"),
        check_vma=False,
    )
```

profile of v0, /device:TPU:17, one launch (start us, length us, event | category | flops | bytes accessed | tf_op | source)
XLA Modules:
  0.0 240.5 jit_solution(5319323107325425394)
XLA Ops:
  13.1 3.2 %all-gather = f32[2,1,1280]{2,1,0:T(1,128)S(1)} all-gather(f32[1,1,1280]{2,1,0:T(1,128)S(1)} %reshape.431), channel_id=1, replica_groups=mesh['seq'=16,'mp'=2] {'mp'}, dimensions={0}, use_global_device_ids=true | all-gather | bytes 15360 | tf_op jit(solution)/shard_map/all_gather | solution.py:144
  19.3 3.6 %all_gather.17 = f32[2,2560]{1,0:T(2,128)S(1)} all-gather(f32[2,1280]{1,0:T(2,128)S(1)} %bitcast_add_fusion), channel_id=1, replica_groups=mesh['seq'=16,'mp'=2] {'mp'}, dimensions={1}, use_global_device_ids=true | all-gather | bytes 30720 | tf_op jit(solution)/shard_map/all_gather | solution.py:145
  22.9 5.1 %all_gather.15 = bf16[64,2560]{1,0:T(8,128)(2,1)S(1)} all-gather(bf16[64,1280]{1,0:T(8,128)(2,1)S(1)} %copy-done.9), channel_id=1, replica_groups=mesh['seq'=16,'mp'=2] {'mp'}, dimensions={1}, use_global_device_ids=true | all-gather | bytes 491520 | tf_op jit(solution)/shard_map/all_gather | solution.py:142
  32.3 41.8 %all-gather.6.cloned.1.call-done = bf16[2560,1280]{1,0:T(8,128)(2,1)} async-done(((bf16[160,1280]{1,0:T(8,128)(2,1)}), bf16[2560,1280]{1,0:T(8,128)(2,1)}) %all-gather.6.cloned.1.call-update) | async-done | bytes 6553616 | tf_op jit(solution)/shard_map/all_gather | solution.py:152
  74.1 5.9 %multiply_reduce_fusion.1 = (f32[256]{0:T(256)S(1)}, f32[256,1280]{1,0:T(8,128)}) fusion(f32[1280]{0:T(1024)S(1)} %copy-done.14, bf16[2560,1280]{1,0:T(8,128)(2,1)} %all-gather.6.cloned.1.call-done, f32[256,2560]{1,0:T(8,128)S(1)} %get-tuple-element.37, f32[2560]{0:T(1024)S(1)} %get-tuple-element.8, f32[2560]{0:T(1024)S(1)} %get-tuple-element.7, ...), kind=kOutput, calls=%fused_computation.33 | convolution fusion | flops 1681981184 | bytes 10514432 | tf_op jit(solution)/shard_map/dot_general | solution.py:79
  80.0 98.5 %all-gather.4.cloned.1.call-done = bf16[2560,2560]{1,0:T(8,128)(2,1)} async-done(((bf16[160,2560]{1,0:T(8,128)(2,1)}), bf16[2560,2560]{1,0:T(8,128)(2,1)}) %all-gather.4.cloned.1.call-update) | async-done | bytes 13107216 | tf_op jit(solution)/shard_map/all_gather | solution.py:153
  178.6 9.8 %convolution_add_fusion.1 = f32[256,2560]{1,0:T(8,128)} fusion(bf16[2560,2560]{1,0:T(8,128)(2,1)} %all-gather.4.cloned.1.call-done, f32[2560]{0:T(1024)S(1)} %copy-done.13, f32[256,2560]{1,0:T(8,128)S(1)} %get-tuple-element.37, f32[2560]{0:T(1024)S(1)} %get-tuple-element.8, f32[2560]{0:T(1024)S(1)} %get-tuple-element.7, f32[256]{0:T(256)S(1)} %get-tuple-element.36, ...), kind=kOutput, calls=%fused_computation.4 | convolution fusion | flops 3359375360 | bytes 18382848 | tf_op jit(solution)/shard_map/dot_general | solution.py:79
  188.4 3.3 %reshape.427 = f32[256,10,2,128]{3,2,1,0:T(2,128)S(1)} reshape(f32[256,2560]{1,0:T(8,128)} %convolution_add_fusion.1) | data formatting | bytes 5242880 | tf_op jit(solution)/shard_map/reshape | solution.py:84
  191.7 1.5 copy-done.2
  193.2 2.4 %slice.89 = bf16[256,10,1,128]{3,2,1,0:T(2,128)(2,1)} slice(f32[256,10,2,128]{3,2,1,0:T(2,128)S(1)} %reshape.427), slice={[0:256], [0:10], [1:2], [0:128]} | slice | bytes 1310720 | tf_op jit(solution)/shard_map/slice | solution.py:86
  195.6 2.6 %slice.84 = f32[256,10,1,128]{3,2,1,0:T(1,128)S(1)} slice(f32[256,10,2,128]{3,2,1,0:T(2,128)} %copy-done.2), slice={[0:256], [0:10], [0:1], [0:128]} | slice | bytes 2621440 | tf_op jit(solution)/shard_map/slice | solution.py:85
  198.4 4.0 %all-reduce = (f32[256]{0:T(256)S(1)}, f32[256]{0:T(256)S(1)}) all-reduce(f32[256]{0:T(256)S(1)} %multiply_reduce_fusion.2, f32[256]{0:T(256)S(1)} %get-tuple-element.38), channel_id=1, replica_groups=mesh['seq'=16,'mp'=2] {'mp'}, use_global_device_ids=true, to_apply=%region_4.5 | all-reduce | flops 512 | bytes 4096 | tf_op jit(solution)/shard_map/psum | solution.py:156
  202.6 1.9 fusion.37
  204.5 1.9 fusion.38
  206.4 2.2 copy.42
  209.5 3.3 %pad_maximum_fusion.1 = f32[256,10,128]{2,0,1:T(8,128)} fusion(f32[256,10,127]{2,0,1:T(8,128)} %get-tuple-element.25, f32[256,10,1]{2,0,1:T(8,128)} %get-tuple-element.27), kind=kLoop, calls=%fused_computation.15 | loop fusion | flops 327680 | bytes 2621440 | tf_op jit(solution)/shard_map/jit(_roll_static)/concatenate | solution.py:60
  212.8 3.0 %copy.44 = f32[256,10,128]{0,2,1:T(8,128)} copy(f32[256,10,128]{2,0,1:T(8,128)} %pad_maximum_fusion.1) | data formatting | bytes 2621440 | tf_op jit(solution)/shard_map/jit(_roll_static)/concatenate | solution.py:60
  215.8 1.5 maximum_negate_fusion
  217.3 2.9 %copy.43 = f32[256,10,128]{0,2,1:T(8,128)} copy(f32[256,10,128]{2,0,1:T(8,128)} %maximum_negate_fusion) | data formatting | bytes 2621440 | tf_op jit(solution)/shard_map/neg | solution.py:60
  220.2 2.1 fusion.15
  223.5 1.4 collective-permute-start
  226.2 1.7 copy.46
  228.2 1.5 pad_maximum_fusion
  229.9 1.6 fusion
  (69 shorter events, 15.8 us)
Async XLA Ops:
  6.5 23.0 %copy-start = (bf16[256,64]{0,1:T(8,128)(2,1)S(1)}, bf16[256,64]{0,1:T(8,128)(2,1)}, u32[]{:S(2)}) copy-start(bf16[256,64]{0,1:T(8,128)(2,1)} %param.12) | copy-start | bytes 98308
  6.5 9.8 %copy-start.12 = (s32[16]{0:T(128)S(1)}, s32[16]{0:T(128)}, u32[]{:S(2)}) copy-start(s32[16]{0:T(128)} %param.14) | copy-start | bytes 196
  6.5 12.0 %copy-start.10 = (f32[2,1280]{1,0:T(2,128)S(1)}, f32[2,1280]{1,0:T(2,128)}, u32[]{:S(2)}) copy-start(f32[2,1280]{1,0:T(2,128)} %param.18) | copy-start | bytes 30724
  6.5 16.3 %copy-start.9 = (bf16[64,1280]{1,0:T(8,128)(2,1)S(1)}, bf16[64,1280]{1,0:T(8,128)(2,1)}, u32[]{:S(2)}) copy-start(bf16[64,1280]{1,0:T(8,128)(2,1)} %param.15) | copy-start | bytes 491524
  6.5 22.7 %copy-start.11 = (f32[2,1280]{1,0:T(2,128)S(1)}, f32[2,1280]{1,0:T(2,128)}, u32[]{:S(2)}) copy-start(f32[2,1280]{1,0:T(2,128)} %param.23) | copy-start | bytes 30724
  6.5 67.5 %all-gather.6.cloned.1.call-start = ((), (), s32[]{:S(2)}) async-start(), calls=%async_computation.1 | async-start | bytes 6963200 | tf_op jit(solution)/shard_map/all_gather | solution.py:152
  7.3 171.3 %all-gather.4.cloned.1.call-start = ((), (), s32[]{:S(2)}) async-start(), calls=%async_computation | async-start | bytes 13926400 | tf_op jit(solution)/shard_map/all_gather | solution.py:153
  29.5 44.6 %copy-start.14 = (f32[1280]{0:T(1024)S(1)}, f32[1280]{0:T(1024)}, u32[]{:S(2)}) copy-start(f32[1280]{0:T(1024)} %param.20) | copy-start | bytes 15364
  74.1 104.5 %copy-start.13 = (f32[2560]{0:T(1024)S(1)}, f32[2560]{0:T(1024)}, u32[]{:S(2)}) copy-start(f32[2560]{0:T(1024)} %param.22) | copy-start | bytes 30724
  191.7 1.5 copy-start.2
  206.4 2.2 copy-start.3
  212.8 3.0 %copy-start.4 = (f32[256,10,127]{2,0,1:T(8,128)S(1)}, f32[256,10,127]{2,0,1:T(8,128)}, u32[]{:S(2)}) copy-start(f32[256,10,127]{2,0,1:T(8,128)} %get-tuple-element.24) | copy-start | bytes 3901444
  212.8 3.0 %copy-start.5 = (f32[256,10,1]{2,0,1:T(8,128)S(1)}, f32[256,10,1]{2,0,1:T(8,128)}, u32[]{:S(2)}) copy-start(f32[256,10,1]{2,0,1:T(8,128)} %get-tuple-element.26) | copy-start | bytes 30724
  217.3 2.9 %copy-start.6 = (f32[256,10,1,128]{0,3,1,2:T(8,128)S(1)}, f32[256,10,1,128]{0,3,1,2:T(8,128)}, u32[]{:S(2)}) copy-start(f32[256,10,1,128]{0,3,1,2:T(8,128)} %copy.42) | copy-start | bytes 3932164
  217.3 2.9 %copy-start.8 = (f32[256,128]{0,1:T(8,128)S(1)}, f32[256,128]{0,1:T(8,128)}, u32[]{:S(2)}) copy-start(f32[256,128]{0,1:T(8,128)} %get-tuple-element.29) | copy-start | bytes 393220
  222.3 2.6 %copy-start.7 = (f32[256,1280]{1,0:T(8,128)S(1)}, f32[256,1280]{1,0:T(8,128)}, u32[]{:S(2)}) copy-start(f32[256,1280]{1,0:T(8,128)} %get-tuple-element.39) | copy-start | bytes 3932164
  223.5 4.7 %collective-permute-start = (bf16[2,256,1280]{1,2,0:T(8,128)(2,1)}, bf16[2,256,1280]{1,2,0:T(8,128)(2,1)}, u32[]{:S(2)}, u32[]{:S(2)}) collective-permute-start(bf16[2,256,1280]{1,2,0:T(8,128)(2,1)} %pad_maximum_fusion.2), channel_id=1, source_target_pairs={{0,2},{2,0},{4,6},{6,4},{8,10},{10,8},{12,14},{14,12},{16,18},{18,... | collective-permute-start | bytes 3932168 | tf_op jit(solution)/shard_map/ppermute | solution.py:20
  231.6 2.1 copy-start.1
Sparse Core Ops, SparseCore 0:
  9.7 64.3 all-gather.5
  76.4 102.1 all-gather.3
where the time goes:
time: 244 us; the launch traced here: 241 us
  waiting for transfers between devices  142 us (58%)
  local copies, waits for them, and re-layouts  28 us (11%)
  matrix products  19.1 us (8%)
  between operations  18 us (7%)
  other arithmetic  16.4 us (7%)
  blocking collectives  15.8 us (6%)
    all_gather x1, waiting for transfers between devices, shards(): lax.all_gather(w_keyvalue, 'seq', axis=0, tiled=True)  98.5 us
    all_gather x1, waiting for transfers between devices, shards(): lax.all_gather(w_query, 'seq', axis=0, tiled=True)  41.8 us
    dot_general x2, matrix products, contract(): return jnp.dot(left_rows, pieces, preferred_element_type=jnp.float32)  15.7 us
    all_gather x1, blocking collectives, shards(): full_weight = lax.all_gather(patch_weight, 'mp', axis=1, tiled=True)  5.06 us
  transfers between devices with their start and end apart: 3, of which 2 were waited for; matrix products, arithmetic and copies ran while one was open for 7% of the time, Pallas kernels for 0%

commit v1 on v0

v1 whole, which is shorter than its diff:
```python
import functools
import math

import jax
import jax.numpy as jnp
from jax import lax
from jax.experimental import pallas as pl
from jax.experimental.pallas import tpu as pltpu
from jax.sharding import PartitionSpec as P

D = 2560
HEADS = 20
HD = 128
GROUP = 2
EPSILON = 1e-06

BLOCKS = 4
WIRE = 72
STEP = 80
VMEM_LIMIT = 48 * 1024 * 1024
F32 = jnp.float32
BF16 = jnp.bfloat16


def params():
    return pltpu.CompilerParams(vmem_limit_bytes=VMEM_LIMIT)


def vmem():
    return pl.BlockSpec(memory_space=pltpu.VMEM)


def smem():
    return pl.BlockSpec(memory_space=pltpu.SMEM)


def swap_bits(value, mask):
    count = lax.axis_size("seq")
    return lax.ppermute(value, "seq", [(source, source ^ mask) for source in range(count)])


def exact_pieces(values, pieces):
    found = []
    for _ in range(pieces):
        piece = values.astype(BF16)
        found.append(piece)
        values = values - piece.astype(F32)
    return found


def chip_block():
    return lax.rem(lax.div(lax.axis_index("seq"), 2), BLOCKS)


def pack_kernel(wq_ref, wkv_ref, *out_refs):
    mine = chip_block()
    wide = out_refs[0].shape[1]
    query_cols, pair_cols = wq_ref.shape[1], wkv_ref.shape[1]
    for flip in range(BLOCKS):
        for block in range(BLOCKS):

            @pl.when(jnp.bitwise_xor(mine, flip) == block)
            def _(flip=flip, block=block):
                first, last = block * wide, (block + 1) * wide
                spans = [
                    (wq_ref, 0, query_cols),
                    (wkv_ref, query_cols, query_cols + pair_cols),
                    (None, query_cols + pair_cols, BLOCKS * wide),
                ]
                for ref, low, high in spans:
                    start, stop = max(first, low), min(last, high)
                    if start >= stop:
                        continue
                    here = pl.ds(start - first, stop - start)
                    if ref is None:
                        out_refs[flip][:, here] = jnp.zeros((wq_ref.shape[0], stop - start), BF16)
                    else:
                        out_refs[flip][:, here] = ref[:, pl.ds(start - low, stop - start)]


def pack_weights(w_query, w_keyvalue):
    rows = w_query.shape[0]
    wide = -(-(w_query.shape[1] + w_keyvalue.shape[1]) // (BLOCKS * HD)) * HD
    return pl.pallas_call(
        pack_kernel,
        out_shape=[jax.ShapeDtypeStruct((rows, wide), BF16)] * BLOCKS,
        in_specs=[vmem()] * 2,
        out_specs=[vmem()] * BLOCKS,
        compiler_params=params(),
        name="pack_weights",
    )(w_query, w_keyvalue)


def modulated_kernel(clips_sent, whole_ref, part_ref, mods_ref, high_ref, low_ref):
    place = lax.axis_index("seq")
    rest, core = lax.div(place, 4), lax.rem(place, 2)
    total = jnp.zeros((72, 1), F32)
    for shard in range(whole_ref.shape[0]):
        total = total + jnp.sum(whole_ref[shard, 0:72], axis=1, keepdims=True)
    centred = part_ref[...] - total * (1.0 / D)
    row = lax.broadcasted_iota(jnp.int32, (STEP - 64, centred.shape[1]), 0)
    for flip in range(clips_sent):
        clip = jnp.bitwise_xor(rest, flip) * 2 + core
        mods = mods_ref[clip]
        shift, scale = mods[0:1], 1.0 + mods[1:2]
        patch_rows = centred[0:64] * scale
        extra = jnp.where(row == 0, centred[64:65] * scale, jnp.where(row == 1, shift, 0.0))
        for start, values in ((0, patch_rows), (64, extra)):
            high, low = exact_pieces(values, 2)
            here = pl.ds(flip * STEP + start, values.shape[0])
            high_ref[here] = high
            low_ref[here] = low


def modulated_rows(whole, part, mods, clips_sent):
    shape = jax.ShapeDtypeStruct((clips_sent * STEP, part.shape[1]), BF16)
    return pl.pallas_call(
        functools.partial(modulated_kernel, clips_sent),
        out_shape=[shape, shape],
        in_specs=[vmem()] * 3,
        out_specs=[vmem()] * 2,
        compiler_params=params(),
        name="modulated_rows",
    )(whole, part, mods)


def product_kernel(clips_sent, *refs):
    high_ref, low_ref = refs[:2]
    piece_refs = refs[2 : 2 + 2 * BLOCKS]
    out_refs = refs[2 + 2 * BLOCKS : 2 + 2 * BLOCKS + clips_sent]
    weight, sems = refs[2 + 2 * BLOCKS + clips_sent :]
    rows = piece_refs[0].shape[0]
    core = lax.rem(lax.axis_index("seq"), 2)
    mine = chip_block()
    copies = []
    for order in range(2 * BLOCKS):
        flip, other = order // 2, order % 2
        source = jnp.bitwise_xor(mine, flip) * 2 + jnp.bitwise_xor(core, other)
        here = pl.ds(pl.multiple_of(source * rows, 16), rows)
        copies.append(
            pltpu.make_async_copy(piece_refs[order], weight.at[here], sems.at[order])
        )
    for copy in copies:
        copy.start()
    for copy in copies:
        copy.wait()
    wide = weight.shape[1]
    tile = 256
    for start in range(0, wide, tile):
        columns = pl.ds(start, tile)
        block = weight[:, columns]
        total = jnp.dot(high_ref[...], block, preferred_element_type=F32)
        total = total + jnp.dot(low_ref[...], block, preferred_element_type=F32)
        for flip in range(clips_sent):
            base = flip * STEP
            ends = total[base + 64 : base + 72]
            first = ends.astype(BF16).astype(F32)
            ends = first + pltpu.roll(ends - first, 2, 0)
            out_refs[flip][:, columns] = jnp.concatenate(
                [total[base : base + 64], ends], axis=0
            ).astype(BF16)


def product_rows(high, low, pieces, clips_sent):
    rows, wide = pieces[0].shape
    return pl.pallas_call(
        functools.partial(product_kernel, clips_sent),
        out_shape=[jax.ShapeDtypeStruct((WIRE, wide), BF16)] * clips_sent,
        in_specs=[vmem()] * 2 + [pl.BlockSpec(memory_space=pl.ANY)] * len(pieces),
        out_specs=[vmem()] * clips_sent,
        scratch_shapes=[
            pltpu.VMEM((2 * BLOCKS * rows, wide), BF16),
            pltpu.SemaphoreType.DMA((2 * BLOCKS,)),
        ],
        compiler_params=params(),
        name="product_rows",
    )(high, low, *pieces)


def split_ends(ends, row):
    ends = jnp.where(row < 2, ends + pltpu.roll(ends, 6, 0), 0.0)
    first = ends.astype(BF16).astype(F32)
    return first + pltpu.roll(ends - first, 2, 0)


def sum_kernel(*refs):
    in_refs, out_ref = refs[:-1], refs[-1]
    own = lax.rem(lax.div(lax.axis_index("seq"), 4), 2)
    row = lax.broadcasted_iota(jnp.int32, (8, out_ref.shape[2]), 0)
    for parity in range(2):
        total = in_refs[parity][...].astype(F32)
        for ref in in_refs[parity + 2 :: 2]:
            total = total + ref[...].astype(F32)
        ends = split_ends(total[64:72], row)
        out_ref[jnp.bitwise_xor(own, parity)] = jnp.concatenate([total[0:64], ends], axis=0).astype(
            BF16
        )


def sum_rows(arrived):
    return pl.pallas_call(
        sum_kernel,
        out_shape=jax.ShapeDtypeStruct((2,) + arrived[0].shape, BF16),
        in_specs=[vmem()] * len(arrived),
        out_specs=vmem(),
        compiler_params=params(),
        name="sum_rows",
    )(*arrived)


def gram_kernel(heads_here, mine_ref, other_ref, bias_q_ref, bias_kv_ref, rows_ref, gram_ref):
    core = lax.rem(lax.axis_index("seq"), 2)
    wide = mine_ref.shape[2]
    for half in range(2):
        for ref, owner in ((mine_ref, core), (other_ref, 1 - core)):
            start = pl.multiple_of((half * 2 + owner) * wide, HD)
            rows_ref[:, pl.ds(start, wide)] = ref[half]
    spans = ((0, bias_q_ref), (bias_q_ref.shape[1], bias_kv_ref))
    for start, bias_ref in spans:
        here = pl.ds(start, bias_ref.shape[1])
        row = lax.broadcasted_iota(jnp.int32, (8, bias_ref.shape[1]), 0)
        block = rows_ref[64:WIRE, here].astype(F32)
        block = block + jnp.where(row == 1, bias_ref[...], 0.0)
        block = split_ends(block, row)
        block = block + jnp.where(row == 4, pltpu.roll(block, 3, 0), 0.0)
        rows_ref[64:WIRE, here] = block.astype(BF16)
    contract = (((1,), (1,)), ((), ()))
    queries = rows_ref[:, pl.ds(0, heads_here * HD)]
    gram_ref[0] = lax.dot_general(queries, queries, contract, preferred_element_type=F32)
    keys = jnp.concatenate(
        [rows_ref[:, pl.ds((heads_here + 2 * head) * HD, HD)] for head in range(heads_here)], axis=1
    )
    gram_ref[1] = lax.dot_general(keys, keys, contract, preferred_element_type=F32)


def gram_rows(mine, other, bias_q, bias_kv, heads_here):
    wide = mine.shape[2]
    return pl.pallas_call(
        functools.partial(gram_kernel, heads_here),
        out_shape=[
            jax.ShapeDtypeStruct((WIRE, BLOCKS * wide), BF16),
            jax.ShapeDtypeStruct((2, WIRE, WIRE), F32),
        ],
        in_specs=[vmem()] * 4,
        out_specs=[vmem()] * 2,
        compiler_params=params(),
        name="gram_rows",
    )(mine, other, bias_q, bias_kv)


def spread_kernel(mine_ref, other_ref, whole_ref, left_ref, turned_ref, spread_ref):
    tokens = mine_ref.shape[0]
    shards = whole_ref.shape[0]
    for part, ref in enumerate((mine_ref, other_ref)):
        rows = ref[...]
        pieces = []
        for shard in range(shards):
            weight = whole_ref[shard, 0:64].astype(BF16)
            pieces.append(
                jnp.dot(rows, weight, preferred_element_type=F32) + whole_ref[shard, 64:65]
            )
        average = sum(jnp.sum(piece, axis=1, keepdims=True) for piece in pieces) * (1.0 / D)
        squares = sum(
            jnp.sum((piece - average) * (piece - average), axis=1, keepdims=True)
            for piece in pieces
        )
        spread = jnp.sqrt(squares * (1.0 / D) + EPSILON)
        spread = jnp.broadcast_to(spread, (tokens, HD))
        first = spread.astype(BF16).astype(F32)
        lane = lax.broadcasted_iota(jnp.int32, (tokens, HD), 1)
        extra = jnp.where(
            (lane == 64) | (lane == 66),
            1.0,
            jnp.where(
                (lane == 65) | (lane == 67), first, jnp.where(lane == 68, spread - first, 0.0)
            ),
        )
        patch = jnp.concatenate([rows.astype(F32), jnp.zeros((tokens, HD - 64), F32)], axis=1)
        left = jnp.where(lane < 64, patch, extra)
        here = pl.ds(part * tokens, tokens)
        left_ref[here] = left.astype(BF16)
        turned_ref[:, here] = left.T.astype(BF16)
        spread_ref[here] = spread


def spread_rows(mine, other, whole):
    tokens = mine.shape[0]
    return pl.pallas_call(
        spread_kernel,
        out_shape=[
            jax.ShapeDtypeStruct((2 * tokens, HD), BF16),
            jax.ShapeDtypeStruct((HD, 2 * tokens), BF16),
            jax.ShapeDtypeStruct((2 * tokens, HD), F32),
        ],
        in_specs=[vmem()] * 3,
        out_specs=[vmem()] * 3,
        compiler_params=params(),
        name="spread_rows",
    )(mine, other, whole)


def heads_kernel(
    heads_here, left_ref, rows_ref, spread_ref, cosine_ref, sine_ref, gain_ref, q_ref, k_ref, v_ref
):
    tokens = q_ref.shape[0]
    left = left_ref[:, 0:WIRE]
    inverse = 1.0 / spread_ref[...]
    cosine, sine = cosine_ref[...], sine_ref[...]
    even = lax.broadcasted_iota(jnp.int32, cosine.shape, 1) % 2 == 0
    sine_even, sine_odd = jnp.where(even, -sine, 0.0), jnp.where(even, 0.0, sine)

    def rotate(values, count):
        back, ahead = pltpu.roll(values, HD - 1, 1), pltpu.roll(values, 1, 1)
        turned = values * cosine[:count] + back * sine_even[:count] + ahead * sine_odd[:count]
        return turned.astype(BF16)

    for head in range(heads_here):
        own = pl.ds(head * HD, HD)
        key_cols = pl.ds((heads_here + 2 * head) * HD, HD)
        value_cols = pl.ds((heads_here + 2 * head + 1) * HD, HD)
        query = jnp.dot(left[:tokens], rows_ref[:, own], preferred_element_type=F32)
        q_ref[:, own] = rotate(query * gain_ref[0:1, own], tokens)
        key = jnp.dot(left, rows_ref[:, key_cols], preferred_element_type=F32)
        k_ref[:, own] = rotate(key * gain_ref[1:2, own], 2 * tokens)
        value = jnp.dot(left, rows_ref[:, value_cols], preferred_element_type=F32)
        v_ref[:, own] = (value * inverse).astype(BF16)


def heads_rows(left, rows, spread, cosine, sine, gains, heads_here):
    both = left.shape[0]
    wide = heads_here * HD
    return pl.pallas_call(
        functools.partial(heads_kernel, heads_here),
        out_shape=[
            jax.ShapeDtypeStruct((both // 2, wide), BF16),
            jax.ShapeDtypeStruct((both, wide), BF16),
            jax.ShapeDtypeStruct((both, wide), BF16),
        ],
        in_specs=[vmem()] * 6,
        out_specs=[vmem()] * 3,
        compiler_params=params(),
        name="heads_rows",
    )(left, rows, spread, cosine, sine, gains)


def attend_kernel(
    heads_step,
    counts_ref,
    q_ref,
    k_ref,
    v_ref,
    left_ref,
    turned_ref,
    gram_ref,
    gram_other_ref,
    out_ref,
    query_scale,
    key_scale,
):
    tokens = q_ref.shape[0]
    place = lax.axis_index("seq")
    count_own = counts_ref[place]
    count_other = counts_ref[jnp.bitwise_xor(place, 1)]

    @pl.when(pl.program_id(0) == 0)
    def _():
        left = left_ref[0:tokens, 0:WIRE]
        turned = turned_ref[0:WIRE]
        gram_q, gram_k = [
            exact_pieces((gram_ref[which] + gram_other_ref[which]) * (1.0 / D), 3)
            for which in range(2)
        ]
        spun_q = sum(jnp.dot(left, piece, preferred_element_type=F32) for piece in gram_q)
        wide_left = left_ref[0:tokens].astype(F32)
        square_q = jnp.sum(spun_q * wide_left[:, 0:WIRE], axis=1, keepdims=True)
        spread_q = wide_left[:, 65:66] + wide_left[:, 68:69]
        query_scale[...] = jnp.broadcast_to(
            lax.rsqrt(square_q + EPSILON * spread_q * spread_q), query_scale.shape
        )
        spun_k = sum(jnp.dot(piece, turned, preferred_element_type=F32) for piece in gram_k)
        wide_turned = turned.astype(F32)
        square_k = jnp.sum(spun_k * wide_turned, axis=0, keepdims=True)
        spread_k = wide_turned[65:66] + wide_turned[68:69]
        key_scale[...] = jnp.broadcast_to(
            lax.rsqrt(square_k + EPSILON * spread_k * spread_k) * (1.0 / math.sqrt(HD)),
            key_scale.shape,
        )

    slot = lax.broadcasted_iota(jnp.int32, (1, 2 * tokens), 1)
    valid = slot < jnp.where(slot < tokens, count_own, tokens + count_other)
    row = lax.broadcasted_iota(jnp.int32, (tokens, HD), 0)
    contract = (((1,), (1,)), ((), ()))
    for head in range(heads_step):
        own = pl.ds(head * HD, HD)
        scores = lax.dot_general(q_ref[:, own], k_ref[:, own], contract, preferred_element_type=F32)
        scores = scores * query_scale[:, 0:1] * key_scale[0:1]
        weights = jnp.where(valid, jnp.exp(scores), 0.0)
        totals = jnp.sum(weights, axis=1, keepdims=True)
        result = jnp.dot(weights.astype(BF16), v_ref[:, own], preferred_element_type=F32)
        out_ref[:, own] = jnp.where(row < count_own, result / totals, 0.0).astype(BF16)


def attend_rows(counts, queries, keys, values, left, turned, gram, gram_other):
    tokens, wide = queries.shape
    heads_step = 2
    width = heads_step * HD
    whole = lambda *shape: pl.BlockSpec(shape, lambda step: (0,) * len(shape))
    return pl.pallas_call(
        functools.partial(attend_kernel, heads_step),
        out_shape=jax.ShapeDtypeStruct((tokens, wide), BF16),
        grid=(wide // width,),
        in_specs=[
            smem(),
            pl.BlockSpec((tokens, width), lambda step: (0, step)),
            pl.BlockSpec((2 * tokens, width), lambda step: (0, step)),
            pl.BlockSpec((2 * tokens, width), lambda step: (0, step)),
            whole(*left.shape),
            whole(*turned.shape),
            whole(*gram.shape),
            whole(*gram.shape),
        ],
        out_specs=pl.BlockSpec((tokens, width), lambda step: (0, step)),
        scratch_shapes=[pltpu.VMEM((tokens, HD), F32), pltpu.VMEM((8, 2 * tokens), F32)],
        compiler_params=params(),
        name="attend_rows",
    )(counts, queries, keys, values, left, turned, gram, gram_other)


def token_places(group_counts, member_ids, slot_ids, shape_row):
    before = jnp.cumsum(group_counts) - group_counts
    lookup = jnp.arange(GROUP, dtype=jnp.int32)[None, :] == member_ids[:, None]
    offset = jnp.sum(jnp.where(lookup, before[None, :], 0), axis=1)
    position = offset + slot_ids
    plane_size = shape_row[1] * shape_row[2]
    frame_pos = position // plane_size
    row_pos = position // shape_row[2] % shape_row[1]
    col_pos = position % shape_row[2]
    return (frame_pos, row_pos, col_pos)


def rotary_tables(frame_pos, row_pos, col_pos):
    other_pairs = HD // 6
    frame_pairs = HD // 2 - 2 * other_pairs
    pair_id = jnp.arange(HD, dtype=jnp.int32) // 2
    in_frame = pair_id < frame_pairs
    in_row = jnp.logical_and(pair_id >= frame_pairs, pair_id < frame_pairs + other_pairs)
    within = jnp.where(
        in_frame,
        pair_id,
        jnp.where(in_row, pair_id - frame_pairs, pair_id - frame_pairs - other_pairs),
    ).astype(F32)
    axis_span = jnp.where(in_frame, 2.0 * frame_pairs, 2.0 * other_pairs).astype(F32)
    inverse = jnp.exp(-(2.0 * within / axis_span) * math.log(10000.0))
    position = jnp.where(
        in_frame[None, :],
        frame_pos[:, None],
        jnp.where(in_row[None, :], row_pos[:, None], col_pos[:, None]),
    ).astype(F32)
    angles = position * inverse[None, :]
    return (jnp.cos(angles), jnp.sin(angles))


def shards(
    patches,
    clip_shape,
    shard_counts,
    patch_weight,
    patch_bias,
    time_mod,
    block_mod,
    w_query,
    query_bias,
    w_keyvalue,
    keyvalue_bias,
    norm_gain,
):
    tokens = patches.shape[0]
    heads_here = w_query.shape[1] // HD
    count = lax.axis_size("seq")
    halves = lax.axis_size("mp")
    place = lax.axis_index("seq")
    clips = time_mod.shape[0]
    rows = w_query.shape[0]
    padded = -(-rows // 16) * 16
    clips_sent = count // 4

    def pad_rows(values):
        return values if rows == padded else jnp.pad(values, ((0, padded - rows), (0, 0)))

    packed = pack_weights(pad_rows(w_query), pad_rows(w_keyvalue))
    pieces = []
    for flip in range(BLOCKS):
        piece = packed[flip] if flip == 0 else swap_bits(packed[flip], 2 * flip)
        pieces += [piece, swap_bits(piece, 1)]

    mods = (time_mod + block_mod).reshape(2 * clips, -1)
    features = patch_bias.shape[0]
    bundle = jnp.concatenate(
        [patch_weight.astype(F32), patch_bias[None], jnp.zeros((7, features), F32), mods]
    )
    whole = lax.all_gather(bundle, "mp", axis=0)
    other_patches = swap_bits(patches, 1)
    span = 8 * rows
    first = place // 8 * span
    part = lax.dynamic_slice(
        whole, (first // features, 0, first % features), (1, whole.shape[1], span)
    )[0]
    if rows != padded:
        part = jnp.pad(part.reshape(-1, 8, rows), ((0, 0), (0, 0), (0, padded - rows)))
        part = part.reshape(whole.shape[1], 8 * padded)
    whole = whole[:, 0:72]
    high, low = modulated_rows(
        whole, part[0:72], part[72:].reshape(clips, 2, -1), clips_sent
    )
    left, turned, spread = spread_rows(patches, other_patches, whole)

    products = product_rows(high, low, pieces, clips_sent)
    arrived = []
    for flip in range(clips_sent):
        pairs = []
        for source in range(count):
            rest, second, core = source // 4, source // 2 % 2, source % 2
            pairs.append((source, (rest ^ flip) * 4 + core * 2 + second))
        arrived.append(lax.ppermute(products[flip], "seq", pairs))

    clip_id = place // GROUP
    member = place % GROUP
    group_counts = lax.dynamic_slice_in_dim(shard_counts, clip_id * GROUP, GROUP, 0)
    shape_row = lax.dynamic_index_in_dim(clip_shape, clip_id, 0, keepdims=False)
    slots = jnp.arange(2 * tokens, dtype=jnp.int32)
    members = jnp.bitwise_xor(slots // tokens, member)
    cosine, sine = rotary_tables(
        *token_places(group_counts, members, slots % tokens, shape_row)
    )

    mine = sum_rows(arrived)
    other = swap_bits(mine, 1)
    columns, gram = gram_rows(
        mine, other, query_bias[None], keyvalue_bias[None], heads_here
    )
    gram_other = lax.ppermute(gram, "mp", [(i, (i + 1) % halves) for i in range(halves)])
    queries, keys, values = heads_rows(left, columns, spread, cosine, sine, norm_gain, heads_here)
    return attend_rows(shard_counts, queries, keys, values, left, turned, gram, gram_other)


def solution(mesh):
    return jax.shard_map(
        shards,
        mesh=mesh,
        in_specs=(
            P("seq", None),
            P(),
            P(),
            P(None, "mp"),
            P("mp"),
            P(None, None, "mp"),
            P(None, "mp"),
            P("seq", "mp"),
            P("mp"),
            P("seq", "mp"),
            P("mp"),
            P(None, "mp"),
        ),
        out_specs=P("seq", "mp"),
        check_vma=False,
    )
```

time: 244 us -> 64.4 us (0.26); the launches traced: 241 us -> 63.4 us
  waiting for transfers between devices: 142 us -> 8.14 us
  local copies, waits for them, and re-layouts: 28 us -> 6.96 us
  matrix products: 19.1 us -> 0 us
  Pallas kernels: 0 us -> 14.3 us
  starting transfers between devices: 1.48 us -> 14.8 us
  other arithmetic: 16.4 us -> 3.14 us
  between operations: 18 us -> 4.89 us
  blocking collectives: 15.8 us -> 11.2 us
    all_gather x2 -> x0, waiting for transfers between devices: 140 us -> none  [the longest x1 98.5 us: shards(): lax.all_gather(w_keyvalue, 'seq', axis=0, tiled=True)]
    dot_general x5 -> x0, matrix products: 19.1 us -> none  [the longest x2 15.7 us: contract(): return jnp.dot(left_rows, pieces, preferred_element_type=jnp.float32)]
    pallas_call x0 -> x8, Pallas kernels: none -> 14.3 us  [the longest x1 5.31 us: attend_rows(): pl.pallas_call(functools.partial(attend_kernel, heads_step), out_shape=ja...]
    ppermute x1 -> x14, starting transfers between devices: 1.4 us -> 14.8 us  [the longest x4 7.26 us: shards(): arrived.append(lax.ppermute(products[flip], 'seq', pairs))]
    slice x9 -> x3, local copies, waits for them, and re-layouts: 11.5 us -> 1.97 us  [the longest x1 1.02 us: shards(): part[0:72]]
    ppermute x1 -> x14, waiting for transfers between devices: 0.01 us -> 8.14 us  [the longest x4 5.94 us: shards(): arrived.append(lax.ppermute(products[flip], 'seq', pairs))]
    concatenate x3 -> x1, other arithmetic: 4.8 us -> 0.1 us  [shards(): jnp.concatenate([patch_weight.astype(F32), patch_bias[None], jnp.zeros((7...]
    psum x1 -> x0, blocking collectives: 3.97 us -> none  [shards(): lax.psum((jnp.sum(query_raw * query_raw, axis=1), jnp.sum(key_raw * key_r...]
  transfers between devices with their start and end apart: 3 -> 14, of which waited for: 2 -> 6; matrix products, arithmetic and copies ran while one was open for 7% -> 10% of each run, Pallas kernels for 0% -> 14%
where the time goes in v1:
time: 64.4 us; the launch traced here: 63.4 us
  starting transfers between devices  14.8 us (23%)
  Pallas kernels  14.3 us (22%)
  blocking collectives  11.2 us (17%)
  waiting for transfers between devices  8.14 us (13%)
  local copies, waits for them, and re-layouts  6.96 us (11%)
  between operations  4.89 us (8%)
  other arithmetic  3.14 us (5%)
    all_gather x1, blocking collectives, shards(): whole = lax.all_gather(bundle, 'mp', axis=0)  11.2 us
    ppermute x4, starting transfers between devices, shards(): arrived.append(lax.ppermute(products[flip], 'seq', pairs))  7.26 us
    ppermute x9, starting transfers between devices, swap_bits(): lax.ppermute(value, 'seq', [(source, source ^ mask) for source in range(c...  6.24 us
    ppermute x4, waiting for transfers between devices, shards(): arrived.append(lax.ppermute(products[flip], 'seq', pairs))  5.94 us
    pallas_call x1, Pallas kernels, attend_rows(): pl.pallas_call(functools.partial(attend_kernel, heads_step), out_shape=ja...  5.31 us
    unnamed x26, local copies, waits for them, and re-layouts  4.04 us
    pallas_call x1, Pallas kernels, product_rows(): pl.pallas_call(functools.partial(product_kernel, clips_sent), out_shape=[...  2.78 us
    pallas_call x1, Pallas kernels, heads_rows(): pl.pallas_call(functools.partial(heads_kernel, heads_here), out_shape=[ja...  2.67 us
  transfers between devices with their start and end apart: 14, of which 6 were waited for; matrix products, arithmetic and copies ran while one was open for 10% of the time, Pallas kernels for 14%

profile of v1, /device:TPU:17, one launch (start us, length us, event | category | flops | bytes accessed | tf_op | source)
XLA Modules:
  0.0 63.4 jit_solution(13494468126941752513)
XLA Ops:
  0.0 0.9 %copy.16.mine_ref = bf16[256,64]{1,0:T(8,128)(2,1)S(1)} copy(bf16[256,64]{0,1:T(8,128)(2,1)} %param.12) | data formatting | bytes 65536 | tf_op args[0]
  1.7 1.1 %copy-done.1 = bf16[160,2560]{1,0:T(8,128)(2,1)S(1)} copy-done((bf16[160,2560]{1,0:T(8,128)(2,1)S(1)}, bf16[160,2560]{1,0:T(8,128)(2,1)}, u32[]{:S(2)}) %copy-start.1) | copy-done | bytes 819224
  2.8 1.0 %copy-done.2 = bf16[160,1280]{1,0:T(8,128)(2,1)S(1)} copy-done((bf16[160,1280]{1,0:T(8,128)(2,1)S(1)}, bf16[160,1280]{1,0:T(8,128)(2,1)}, u32[]{:S(2)}) %copy-start.2) | copy-done | bytes 409624
  3.8 1.0 %pack_weights.1 = (bf16[160,1024]{1,0:T(8,128)(2,1)S(1)}, bf16[160,1024]{1,0:T(8,128)(2,1)}, bf16[160,1024]{1,0:T(8,128)(2,1)}, bf16[160,1024]{1,0:T(8,128)(2,1)S(1)}) custom-call(bf16[160,1280]{1,0:T(8,128)(2,1)S(1)} %copy-done.2, bf16[160,2560]{1,0:T(8,128)(2,1)S(1)} %copy-done.1), custom_call_target="tpu_custom_call" | custom-call | tf_op jit(solution)/shard_map/pack_weights/pallas_call | solution.py:84
  4.8 1.2 %collective-permute-start.2 = (bf16[160,1024]{1,0:T(8,128)(2,1)}, bf16[160,1024]{1,0:T(8,128)(2,1)S(1)}, u32[]{:S(2)}, u32[]{:S(2)}) collective-permute-start(bf16[160,1024]{1,0:T(8,128)(2,1)} %get-tuple-element.27), channel_id=1, source_target_pairs={{0,4},{2,6},{4,0},{6,2},{8,12},{10,14},{12,8},{14,10},{16,20},{18,... | collective-permute-start | bytes 983048 | tf_op jit(solution)/shard_map/ppermute | solution.py:39
  6.1 1.3 %collective-permute-start.4 = (bf16[160,1024]{1,0:T(8,128)(2,1)}, bf16[160,1024]{1,0:T(8,128)(2,1)S(1)}, u32[]{:S(2)}, u32[]{:S(2)}) collective-permute-start(bf16[160,1024]{1,0:T(8,128)(2,1)} %get-tuple-element.28), channel_id=1, source_target_pairs={{0,8},{2,10},{4,12},{6,14},{8,0},{10,2},{12,4},{14,6},{16,24},{18,... | collective-permute-start | bytes 983048 | tf_op jit(solution)/shard_map/ppermute | solution.py:39
  7.8 11.2 %all-gather = f32[176,1280]{1,0:T(8,128)S(1)} all-gather(f32[88,1280]{1,0:T(8,128)S(1)} %pad_maximum_fusion), channel_id=2, replica_groups=mesh['seq'=16,'mp'=2] {'mp'}, dimensions={0}, use_global_device_ids=true | all-gather | bytes 1351680 | tf_op jit(solution)/shard_map/all_gather | solution.py:501
  19.0 0.9 %copy-done.5 = f32[176,1280]{1,0:T(8,128)} copy-done((f32[176,1280]{1,0:T(8,128)}, f32[176,1280]{1,0:T(8,128)S(1)}, u32[]{:S(2)}) %copy-start.5) | copy-done | bytes 901144
  20.0 1.0 %dynamic-slice_bitcast_fusion.part_ref = f32[72,1280]{1,0:T(8,128)S(1)} fusion(f32[2,88,1280]{2,1,0:T(8,128)} %bitcast.13, s32[]{:T(128)S(6)} %select_n.147), kind=kLoop, calls=%fused_computation.1 | loop fusion | bytes 737284 | tf_op jit(solution)/shard_map/slice | solution.py:513
  21.0 0.9 %constant_dynamic-slice_fusion.1 = f32[1,16,1280]{2,1,0:T(8,128)S(1)} fusion(f32[2,88,1280]{2,1,0:T(8,128)} %bitcast.14, s32[]{:T(128)S(6)} %select_n.147, s32[]{:T(128)S(6)} %add.122), kind=kLoop, calls=%fused_computation.36 | loop fusion | bytes 163848 | tf_op jit(solution)/shard_map/slice | solution.py:513
  23.5 2.3 %collective-permute-start.3 = (bf16[160,1024]{1,0:T(8,128)(2,1)S(1)}, bf16[160,1024]{1,0:T(8,128)(2,1)S(1)}, u32[]{:S(2)}, u32[]{:S(2)}) collective-permute-start(bf16[160,1024]{1,0:T(8,128)(2,1)S(1)} %collective-permute-done.2.refs_4_), channel_id=1, source_target_pairs={{0,2},{2,0},{4,6},{6,4},{8,10},{10,8},{12,14},{14,12},{16,18},{18,... | collective-permute-start | bytes 983048 | tf_op jit(solution)/shard_map/ppermute | solution.py:39
  27.9 2.8 %product_rows.1 = (bf16[72,1024]{1,0:T(8,128)(2,1)S(1)}, bf16[72,1024]{1,0:T(8,128)(2,1)S(1)}, bf16[72,1024]{1,0:T(8,128)(2,1)S(1)}, bf16[72,1024]{1,0:T(8,128)(2,1)S(1)}) custom-call(bf16[320,1280]{1,0:T(8,128)(2,1)S(1)} %get-tuple-element.24.refs_0_, bf16[320,1280]{1,0:T(8,128)(2,1)S(1)} %get-tuple-element.25.refs_1_, ...), custom_call_target="tpu_custom_call" | custom-call | tf_op jit(solution)/shard_map/product_rows/pallas_call | solution.py:166
  30.7 3.4 %collective-permute-start.8 = (bf16[72,1024]{1,0:T(8,128)(2,1)S(1)}, bf16[72,1024]{1,0:T(8,128)(2,1)S(1)}, u32[]{:S(2)}, u32[]{:S(2)}) collective-permute-start(bf16[72,1024]{1,0:T(8,128)(2,1)S(1)} %get-tuple-element.30), channel_id=1, source_target_pairs={{0,0},{2,4},{4,2},{6,6},{8,8},{10,12},{12,10},{14,14},{16,16},{18,... | collective-permute-start | bytes 442376 | tf_op jit(solution)/shard_map/ppermute | solution.py:524
  34.1 1.3 %collective-permute-start.9 = (bf16[72,1024]{1,0:T(8,128)(2,1)S(1)}, bf16[72,1024]{1,0:T(8,128)(2,1)S(1)}, u32[]{:S(2)}, u32[]{:S(2)}) collective-permute-start(bf16[72,1024]{1,0:T(8,128)(2,1)S(1)} %get-tuple-element.31), channel_id=1, source_target_pairs={{0,8},{2,12},{4,10},{6,14},{8,0},{10,4},{12,2},{14,6},{16,24},{18,... | collective-permute-start | bytes 442376 | tf_op jit(solution)/shard_map/ppermute | solution.py:524
  35.4 1.3 %collective-permute-start.10 = (bf16[72,1024]{1,0:T(8,128)(2,1)S(1)}, bf16[72,1024]{1,0:T(8,128)(2,1)S(1)}, u32[]{:S(2)}, u32[]{:S(2)}) collective-permute-start(bf16[72,1024]{1,0:T(8,128)(2,1)S(1)} %get-tuple-element.32), channel_id=1, source_target_pairs={{0,16},{2,20},{4,18},{6,22},{8,24},{10,28},{12,26},{14,30},{16,0},... | collective-permute-start | bytes 442376 | tf_op jit(solution)/shard_map/ppermute | solution.py:524
  36.7 1.3 %collective-permute-start.11 = (bf16[72,1024]{1,0:T(8,128)(2,1)S(1)}, bf16[72,1024]{1,0:T(8,128)(2,1)S(1)}, u32[]{:S(2)}, u32[]{:S(2)}) collective-permute-start(bf16[72,1024]{1,0:T(8,128)(2,1)S(1)} %get-tuple-element.33), channel_id=1, source_target_pairs={{0,24},{2,28},{4,26},{6,30},{8,16},{10,20},{12,18},{14,22},{16,8},... | collective-permute-start | bytes 442376 | tf_op jit(solution)/shard_map/ppermute | solution.py:524
  42.7 2.8 %collective-permute-done.10.refs_2_ = bf16[72,1024]{1,0:T(8,128)(2,1)S(1)} collective-permute-done((bf16[72,1024]{1,0:T(8,128)(2,1)S(1)}, bf16[72,1024]{1,0:T(8,128)(2,1)S(1)}, u32[]{:S(2)}, u32[]{:S(2)}) %collective-permute-start.10) | collective-permute-done | bytes 147488 | tf_op jit(solution)/shard_map/ppermute | solution.py:524
  45.5 3.2 %collective-permute-done.11.refs_3_ = bf16[72,1024]{1,0:T(8,128)(2,1)S(1)} collective-permute-done((bf16[72,1024]{1,0:T(8,128)(2,1)S(1)}, bf16[72,1024]{1,0:T(8,128)(2,1)S(1)}, u32[]{:S(2)}, u32[]{:S(2)}) %collective-permute-start.11) | collective-permute-done | bytes 147488 | tf_op jit(solution)/shard_map/ppermute | solution.py:524
  48.9 0.9 %add_select_fusion.3 = (s32[512]{0:T(512)S(1)}, s32[512]{0:T(512)S(1)}, s32[512]{0:T(512)S(1)}) fusion(s32[]{:T(128)S(6)} %mul.39, s32[]{:T(128)S(6)} %sign.66, s32[512]{0:T(512)S(1)} %fusion.2, pred[]{:T(512)S(6)} %lt.85, s32[]{:T(128)S(6)} %select_n.160, pred[]{:T(512)S(6)} %lt.83, s32[]{:T(128)S(6)} %select_n.158, s32[]{:T(128)} %bitcast.5, s32[]{:T(128)S(6)} %sign.67), kind=kLoop, calls=%fused_computation.18 | loop fusion | flops 18432 | bytes 8218 | tf_op jit(solution)/shard_map/jit(floor_divide)/jit(_where)/select_n | solution.py:435
  50.8 1.3 %collective-permute-start.13 = (f32[2,72,72]{2,1,0:T(8,128)S(1)}, f32[2,72,72]{2,1,0:T(8,128)S(1)}, u32[]{:S(2)}, u32[]{:S(2)}) collective-permute-start(f32[2,72,72]{2,1,0:T(8,128)S(1)} %get-tuple-element.40.gram_ref), channel_id=1, source_target_pairs={{0,1},{1,0},{2,3},{3,2},{4,5},{5,4},{6,7},{7,6},{8,9},{9,8},{10,11... | collective-permute-start | bytes 124424 | tf_op jit(solution)/shard_map/ppermute | solution.py:541
  52.0 1.7 %fusion = (f32[512,128]{1,0:T(8,128)S(1)}, f32[512,128]{1,0:T(8,128)S(1)}) fusion(f32[128]{0:T(128)S(1)} %multiply_exponential_fusion, s32[512]{0:T(512)S(1)} %get-tuple-element.44, s32[512]{0:T(512)S(1)} %get-tuple-element.45, s32[512]{0:T(512)S(1)} %get-tuple-element.43, pred[128]{0:T(512)(128)(4,1)S(1)} %get-tuple-element.48, ...), kind=kLoop, calls=%fused_computation.3 | loop fusion | flops 262144 | bytes 531200 | tf_op jit(solution)/shard_map/sin | solution.py:460
  53.7 1.7 %spread_rows.1 = (bf16[512,128]{1,0:T(8,128)(2,1)S(1)}, bf16[128,512]{1,0:T(8,128)(2,1)S(1)}, f32[512,128]{1,0:T(8,128)S(1)}) custom-call(bf16[256,64]{1,0:T(8,128)(2,1)S(1)} %copy.16.mine_ref, bf16[256,64]{1,0:T(8,128)(2,1)S(1)} %collective-permute-done.other_ref, f32[2,72,1280]{2,1,0:T(8,128)S(1)} %slice.30.whole_ref), custom_call_target="tpu_custom_call" | custom-call | tf_op jit(solution)/shard_map/spread_rows/pallas_call | solution.py:288
  55.4 2.7 %heads_rows.1 = (bf16[256,1280]{1,0:T(8,128)(2,1)S(1)}, bf16[512,1280]{1,0:T(8,128)(2,1)S(1)}, bf16[512,1280]{1,0:T(8,128)(2,1)S(1)}) custom-call(bf16[512,128]{1,0:T(8,128)(2,1)S(1)} %get-tuple-element.23.left_ref, bf16[72,4096]{1,0:T(8,128)(2,1)S(1)} %get-tuple-element.34.rows_ref, f32[512,128]{1,0:T(8,128)S(1)} %get-tuple-element.35.spread_ref, ...), custom_call_target="tpu_custom_call" | custom-call | tf_op jit(solution)/shard_map/heads_rows/pallas_call | solution.py:332
  58.1 5.3 %attend_rows.1 = bf16[256,1280]{1,0:T(8,128)(2,1)} custom-call(s32[16]{0:T(128)S(1)} %copy-done.4, bf16[256,1280]{1,0:T(8,128)(2,1)S(1)} %get-tuple-element.36.q_ref, bf16[512,1280]{1,0:T(8,128)(2,1)S(1)} %get-tuple-element.37.k_ref, bf16[512,1280]{1,0:T(8,128)(2,1)S(1)} %get-tuple-element.38.v_ref, bf16[512,128]{1,0:T(8,128)(2,1)S(1)} %get-tuple-element.23.left_ref, ...), custom_call_target="tpu_custom_call" | custom-call | tf_op jit(solution)/shard_map/attend_rows/pallas_call | solution.py:408
  (63 shorter events, 6.1 us)
Async XLA Ops:
  0.0 22.8 %copy-start = (s32[8,3]{0,1:T(4,128)S(1)}, s32[8,3]{0,1:T(4,128)}, u32[]{:S(2)}) copy-start(s32[8,3]{0,1:T(4,128)} %param.13) | copy-start | bytes 292
  0.0 7.5 %copy-start.7 = (f32[8,2,1280]{2,1,0:T(2,128)S(1)}, f32[8,2,1280]{2,1,0:T(2,128)}, u32[]{:S(2)}) copy-start(f32[8,2,1280]{2,1,0:T(2,128)} %param.17) | copy-start | bytes 245764
  0.0 7.5 %copy-start.9 = (f32[2,1280]{1,0:T(2,128)S(1)}, f32[2,1280]{1,0:T(2,128)}, u32[]{:S(2)}) copy-start(f32[2,1280]{1,0:T(2,128)} %param.18) | copy-start | bytes 30724
  0.9 52.8 %collective-permute-start = (bf16[256,64]{1,0:T(8,128)(2,1)S(1)}, bf16[256,64]{1,0:T(8,128)(2,1)S(1)}, u32[]{:S(2)}, u32[]{:S(2)}) collective-permute-start(bf16[256,64]{1,0:T(8,128)(2,1)S(1)} %copy.16.mine_ref), channel_id=1, source_target_pairs={{0,2},{2,0},{4,6},{6,4},{8,10},{10,8},{12,14},{14,12},{16,18},{18,... | collective-permute-start | bytes 98312 | tf_op jit(solution)/shard_map/ppermute | solution.py:39
  1.7 1.1 %copy-start.1 = (bf16[160,2560]{1,0:T(8,128)(2,1)S(1)}, bf16[160,2560]{1,0:T(8,128)(2,1)}, u32[]{:S(2)}) copy-start(bf16[160,2560]{1,0:T(8,128)(2,1)} %wkv_ref.1) | copy-start | bytes 2457604
  3.8 3.8 %copy-start.10 = (f32[1280]{0:T(1024)S(1)}, f32[1280]{0:T(1024)}, u32[]{:S(2)}) copy-start(f32[1280]{0:T(1024)} %param.16) | copy-start | bytes 15364
  3.8 3.8 %copy-start.6 = (bf16[64,1280]{1,0:T(8,128)(2,1)S(1)}, bf16[64,1280]{1,0:T(8,128)(2,1)}, u32[]{:S(2)}) copy-start(bf16[64,1280]{1,0:T(8,128)(2,1)} %param.15) | copy-start | bytes 491524
  4.8 21.5 %collective-permute-start.1 = (bf16[160,1024]{1,0:T(8,128)(2,1)S(1)}, bf16[160,1024]{1,0:T(8,128)(2,1)S(1)}, u32[]{:S(2)}, u32[]{:S(2)}) collective-permute-start(bf16[160,1024]{1,0:T(8,128)(2,1)S(1)} %get-tuple-element.26.refs_2_), channel_id=1, source_target_pairs={{0,2},{2,0},{4,6},{6,4},{8,10},{10,8},{12,14},{14,12},{16,18},{18,... | collective-permute-start | bytes 983048 | tf_op jit(solution)/shard_map/ppermute | solution.py:39
  4.8 18.6 %collective-permute-start.2 = (bf16[160,1024]{1,0:T(8,128)(2,1)}, bf16[160,1024]{1,0:T(8,128)(2,1)S(1)}, u32[]{:S(2)}, u32[]{:S(2)}) collective-permute-start(bf16[160,1024]{1,0:T(8,128)(2,1)} %get-tuple-element.27), channel_id=1, source_target_pairs={{0,4},{2,6},{4,0},{6,2},{8,12},{10,14},{12,8},{14,10},{16,20},{18,... | collective-permute-start | bytes 983048 | tf_op jit(solution)/shard_map/ppermute | solution.py:39
  6.1 19.7 %collective-permute-start.4 = (bf16[160,1024]{1,0:T(8,128)(2,1)}, bf16[160,1024]{1,0:T(8,128)(2,1)S(1)}, u32[]{:S(2)}, u32[]{:S(2)}) collective-permute-start(bf16[160,1024]{1,0:T(8,128)(2,1)} %get-tuple-element.28), channel_id=1, source_target_pairs={{0,8},{2,10},{4,12},{6,14},{8,0},{10,2},{12,4},{14,6},{16,24},{18,... | collective-permute-start | bytes 983048 | tf_op jit(solution)/shard_map/ppermute | solution.py:39
  7.3 18.5 %collective-permute-start.6 = (bf16[160,1024]{1,0:T(8,128)(2,1)S(1)}, bf16[160,1024]{1,0:T(8,128)(2,1)S(1)}, u32[]{:S(2)}, u32[]{:S(2)}) collective-permute-start(bf16[160,1024]{1,0:T(8,128)(2,1)S(1)} %get-tuple-element.29), channel_id=1, source_target_pairs={{0,12},{2,14},{4,8},{6,10},{8,4},{10,6},{12,0},{14,2},{16,28},{18,... | collective-permute-start | bytes 983048 | tf_op jit(solution)/shard_map/ppermute | solution.py:39
  19.0 3.0 %copy-start.4 = (s32[16]{0:T(128)S(1)}, s32[16]{0:T(128)}, u32[]{:S(2)}) copy-start(s32[16]{0:T(128)} %counts_ref.1) | copy-start | bytes 196
  23.5 3.5 %collective-permute-start.3 = (bf16[160,1024]{1,0:T(8,128)(2,1)S(1)}, bf16[160,1024]{1,0:T(8,128)(2,1)S(1)}, u32[]{:S(2)}, u32[]{:S(2)}) collective-permute-start(bf16[160,1024]{1,0:T(8,128)(2,1)S(1)} %collective-permute-done.2.refs_4_), channel_id=1, source_target_pairs={{0,2},{2,0},{4,6},{6,4},{8,10},{10,8},{12,14},{14,12},{16,18},{18,... | collective-permute-start | bytes 983048 | tf_op jit(solution)/shard_map/ppermute | solution.py:39
  25.7 1.7 %collective-permute-start.5 = (bf16[160,1024]{1,0:T(8,128)(2,1)S(1)}, bf16[160,1024]{1,0:T(8,128)(2,1)S(1)}, u32[]{:S(2)}, u32[]{:S(2)}) collective-permute-start(bf16[160,1024]{1,0:T(8,128)(2,1)S(1)} %collective-permute-done.4.refs_6_), channel_id=1, source_target_pairs={{0,2},{2,0},{4,6},{6,4},{8,10},{10,8},{12,14},{14,12},{16,18},{18,... | collective-permute-start | bytes 983048 | tf_op jit(solution)/shard_map/ppermute | solution.py:39
  25.8 2.1 %collective-permute-start.7 = (bf16[160,1024]{1,0:T(8,128)(2,1)S(1)}, bf16[160,1024]{1,0:T(8,128)(2,1)S(1)}, u32[]{:S(2)}, u32[]{:S(2)}) collective-permute-start(bf16[160,1024]{1,0:T(8,128)(2,1)S(1)} %collective-permute-done.6.refs_8_), channel_id=1, source_target_pairs={{0,2},{2,0},{4,6},{6,4},{8,10},{10,8},{12,14},{14,12},{16,18},{18,... | collective-permute-start | bytes 983048 | tf_op jit(solution)/shard_map/ppermute | solution.py:39
  27.9 13.4 %copy-start.11 = (f32[1280]{0:T(1024)S(1)}, f32[1280]{0:T(1024)}, u32[]{:S(2)}) copy-start(f32[1280]{0:T(1024)} %param.20) | copy-start | bytes 15364
  27.9 13.4 %copy-start.8 = (f32[2560]{0:T(1024)S(1)}, f32[2560]{0:T(1024)}, u32[]{:S(2)}) copy-start(f32[2560]{0:T(1024)} %param.22) | copy-start | bytes 30724
  30.7 12.0 %collective-permute-start.8 = (bf16[72,1024]{1,0:T(8,128)(2,1)S(1)}, bf16[72,1024]{1,0:T(8,128)(2,1)S(1)}, u32[]{:S(2)}, u32[]{:S(2)}) collective-permute-start(bf16[72,1024]{1,0:T(8,128)(2,1)S(1)} %get-tuple-element.30), channel_id=1, source_target_pairs={{0,0},{2,4},{4,2},{6,6},{8,8},{10,12},{12,10},{14,14},{16,16},{18,... | collective-permute-start | bytes 442376 | tf_op jit(solution)/shard_map/ppermute | solution.py:524
  34.1 8.6 %collective-permute-start.9 = (bf16[72,1024]{1,0:T(8,128)(2,1)S(1)}, bf16[72,1024]{1,0:T(8,128)(2,1)S(1)}, u32[]{:S(2)}, u32[]{:S(2)}) collective-permute-start(bf16[72,1024]{1,0:T(8,128)(2,1)S(1)} %get-tuple-element.31), channel_id=1, source_target_pairs={{0,8},{2,12},{4,10},{6,14},{8,0},{10,4},{12,2},{14,6},{16,24},{18,... | collective-permute-start | bytes 442376 | tf_op jit(solution)/shard_map/ppermute | solution.py:524
  35.4 10.1 %collective-permute-start.10 = (bf16[72,1024]{1,0:T(8,128)(2,1)S(1)}, bf16[72,1024]{1,0:T(8,128)(2,1)S(1)}, u32[]{:S(2)}, u32[]{:S(2)}) collective-permute-start(bf16[72,1024]{1,0:T(8,128)(2,1)S(1)} %get-tuple-element.32), channel_id=1, source_target_pairs={{0,16},{2,20},{4,18},{6,22},{8,24},{10,28},{12,26},{14,30},{16,0},... | collective-permute-start | bytes 442376 | tf_op jit(solution)/shard_map/ppermute | solution.py:524
  36.7 12.0 %collective-permute-start.11 = (bf16[72,1024]{1,0:T(8,128)(2,1)S(1)}, bf16[72,1024]{1,0:T(8,128)(2,1)S(1)}, u32[]{:S(2)}, u32[]{:S(2)}) collective-permute-start(bf16[72,1024]{1,0:T(8,128)(2,1)S(1)} %get-tuple-element.33), channel_id=1, source_target_pairs={{0,24},{2,28},{4,26},{6,30},{8,16},{10,20},{12,18},{14,22},{16,8},... | collective-permute-start | bytes 442376 | tf_op jit(solution)/shard_map/ppermute | solution.py:524
  42.7 12.7 %copy-start.3 = (f32[2,1280]{1,0:T(2,128)S(1)}, f32[2,1280]{1,0:T(2,128)}, u32[]{:S(2)}) copy-start(f32[2,1280]{1,0:T(2,128)} %gain_ref.1) | copy-start | bytes 30724
  48.8 1.6 %collective-permute-start.12 = (bf16[2,72,1024]{2,1,0:T(8,128)(2,1)S(1)}, bf16[2,72,1024]{2,1,0:T(8,128)(2,1)S(1)}, u32[]{:S(2)}, u32[]{:S(2)}) collective-permute-start(bf16[2,72,1024]{2,1,0:T(8,128)(2,1)S(1)} %sum_rows.1.mine_ref), channel_id=1, source_target_pairs={{0,2},{2,0},{4,6},{6,4},{8,10},{10,8},{12,14},{14,12},{16,18},{18,... | collective-permute-start | bytes 884744 | tf_op jit(solution)/shard_map/ppermute | solution.py:39
  50.8 7.4 %collective-permute-start.13 = (f32[2,72,72]{2,1,0:T(8,128)S(1)}, f32[2,72,72]{2,1,0:T(8,128)S(1)}, u32[]{:S(2)}, u32[]{:S(2)}) collective-permute-start(f32[2,72,72]{2,1,0:T(8,128)S(1)} %get-tuple-element.40.gram_ref), channel_id=1, source_target_pairs={{0,1},{1,0},{2,3},{3,2},{4,5},{5,4},{6,7},{7,6},{8,9},{9,8},{10,11... | collective-permute-start | bytes 124424 | tf_op jit(solution)/shard_map/ppermute | solution.py:541
  (2 other events, 1.9 us)

commit v2 on v0

v2 whole, which is shorter than its diff:
```python
import functools
import math

import jax
import jax.numpy as jnp
from jax import lax
from jax.experimental import pallas as pl
from jax.experimental.pallas import tpu as pltpu
from jax.sharding import PartitionSpec as P

D = 2560
HEADS = 20
HD = 128
GROUP = 2
EPSILON = 1e-06

BLOCKS = 4
WIRE = 72
STEP = 80
VMEM_LIMIT = 24 * 1024 * 1024
F32 = jnp.float32
BF16 = jnp.bfloat16


def params():
    return pltpu.CompilerParams(vmem_limit_bytes=VMEM_LIMIT)


def vmem():
    return pl.BlockSpec(memory_space=pltpu.VMEM)


def smem():
    return pl.BlockSpec(memory_space=pltpu.SMEM)


def swap_bits(value, mask):
    count = lax.axis_size("seq")
    return lax.ppermute(value, "seq", [(source, source ^ mask) for source in range(count)])


def exact_pieces(values, pieces):
    found = []
    for _ in range(pieces):
        piece = values.astype(BF16)
        found.append(piece)
        values = values - piece.astype(F32)
    return found


def block_chunks(chunks):
    whole = chunks // BLOCKS
    assert chunks - BLOCKS * whole == BLOCKS // 2
    return whole, BLOCKS * whole


def block_spans(block, chunks):
    whole, shared = block_chunks(chunks)
    return (block * whole * HD, whole * HD), ((shared + block // 2) * HD, HD)


def chip_block():
    return lax.rem(lax.div(lax.axis_index("seq"), 2), BLOCKS)


def after(value, *ready):
    anywhere = pl.BlockSpec(memory_space=pl.ANY)
    return pl.pallas_call(
        lambda *refs: None,
        out_shape=jax.ShapeDtypeStruct(value.shape, value.dtype),
        in_specs=[anywhere] * (1 + len(ready)),
        out_specs=anywhere,
        input_output_aliases={0: 0},
        compiler_params=pltpu.CompilerParams(vmem_limit_bytes=1024 * 1024),
        name="after",
    )(value, *ready)


def prepare_kernel(
    weight_ref, bias_ref, time_ref, block_ref, patches_ref, ready_ref, bundle_ref, copy_ref, mods
):
    clips = time_ref.shape[0]
    bundle_ref[0:64] = weight_ref[...]
    row = lax.broadcasted_iota(jnp.int32, (16, bundle_ref.shape[1]), 0)
    pieces = exact_pieces(bias_ref[...], 3)
    bundle_ref[64:80] = sum(
        jnp.where(row == which, piece.astype(F32), 0.0) for which, piece in enumerate(pieces)
    ).astype(BF16)
    for clip in range(clips):
        mods[pl.ds(2 * clip, 2)] = time_ref[clip] + block_ref[...]
    for which, piece in enumerate(exact_pieces(mods[...], 2)):
        bundle_ref[pl.ds(80 + 2 * clips * which, 2 * clips)] = piece
    copy_ref[...] = patches_ref[...]


def prepare_rows(weight, bias, time_mod, block_mod, patches, ready):
    clips, _, features = time_mod.shape
    return pl.pallas_call(
        prepare_kernel,
        out_shape=[
            jax.ShapeDtypeStruct((80 + 4 * clips, features), BF16),
            jax.ShapeDtypeStruct(patches.shape, BF16),
        ],
        in_specs=[vmem()] * 5 + [pl.BlockSpec(memory_space=pl.ANY)],
        out_specs=[vmem()] * 2,
        scratch_shapes=[pltpu.VMEM((2 * clips, features), F32)],
        compiler_params=params(),
        name="prepare_rows",
    )(weight, bias, time_mod, block_mod, patches, ready)


def bundle_bias(ref):
    return jnp.sum(ref[64:80].astype(F32), axis=0, keepdims=True)


def pack_kernel(wq_ref, wkv_ref, *refs):
    out_refs, (shared, sems, shared_sem) = refs[:-3], refs[-3:]
    rows, query_cols = wq_ref.shape
    chunks = (query_cols + wkv_ref.shape[1]) // HD
    whole, first_shared = block_chunks(chunks)
    mine = chip_block()

    def chunk_of(chunk):
        if chunk * HD < query_cols:
            return wq_ref.at[:, pl.ds(chunk * HD, HD)]
        return wkv_ref.at[:, pl.ds(chunk * HD - query_cols, HD)]

    copies = [
        pltpu.make_async_copy(chunk_of(first_shared + which), shared.at[which], shared_sem.at[which])
        for which in range(BLOCKS // 2)
    ]
    for copy in copies:
        copy.start()
    for flip in range(1, BLOCKS + 1):
        flip = flip % BLOCKS
        for block in range(BLOCKS):

            @pl.when(jnp.bitwise_xor(mine, flip) == block)
            def _(flip=flip, block=block):
                for chunk in range(whole):
                    pltpu.make_async_copy(
                        chunk_of(block * whole + chunk),
                        out_refs[flip].at[pl.ds(chunk * rows, rows)],
                        sems.at[flip],
                    ).start()

    for copy in copies:
        copy.wait()
    lane = lax.broadcasted_iota(jnp.int32, (rows // 2, HD), 1)
    for flip in range(BLOCKS):
        block = jnp.bitwise_xor(mine, flip)
        values = shared[lax.div(block, 2)].astype(F32)
        above, below = values[: rows // 2], values[rows // 2 :]
        even = jnp.where(lane < HD // 2, above, pltpu.roll(below, HD // 2, 1))
        odd = jnp.where(lane < HD // 2, pltpu.roll(above, HD // 2, 1), below)
        found = jnp.where(lax.rem(block, 2) == 0, even, odd)
        out_refs[flip][pl.ds(whole * rows, rows // 2)] = found.astype(BF16)
    for flip in range(BLOCKS):
        here = out_refs[flip].at[pl.ds(0, whole * rows)]
        pltpu.make_async_copy(here, here, sems.at[flip]).wait()


def pack_weights(w_query, w_keyvalue):
    rows = w_query.shape[0]
    whole, _ = block_chunks((w_query.shape[1] + w_keyvalue.shape[1]) // HD)
    return pl.pallas_call(
        pack_kernel,
        out_shape=[jax.ShapeDtypeStruct((whole * rows + rows // 2, HD), BF16)] * BLOCKS,
        in_specs=[pl.BlockSpec(memory_space=pltpu.HBM)] * 2,
        out_specs=[vmem()] * BLOCKS,
        scratch_shapes=[
            pltpu.VMEM((BLOCKS // 2, rows, HD), BF16),
            pltpu.SemaphoreType.DMA((BLOCKS,)),
            pltpu.SemaphoreType.DMA((BLOCKS // 2,)),
        ],
        compiler_params=params(),
        name="pack_weights",
    )(*[pltpu.with_memory_space_constraint(w, pltpu.HBM) for w in (w_query, w_keyvalue)])


def reorder_blocks(values, low):
    for bit in (2, 1, 0):
        count = 8 >> bit
        size = values.shape[1] // count
        blocks = [values[:, j * size : (j + 1) * size] for j in range(count)]
        swapped = jnp.concatenate([blocks[j ^ 1] for j in range(count)], axis=1)
        values = jnp.where(jnp.bitwise_and(low, 1 << bit) != 0, swapped, values)
    return values


def modulated_kernel(
    clips_sent, span, own_ref, other_ref, own_part_ref, other_part_ref, rows_ref, part
):
    place = lax.axis_index("seq")
    rest, core = lax.div(place, 4), lax.rem(place, 2)
    mods_rows = (own_ref.shape[0] - 80) // 2
    total = jnp.sum(own_ref[0:64].astype(F32), axis=1, keepdims=True)
    total = total + jnp.sum(other_ref[0:64].astype(F32), axis=1, keepdims=True)
    total_bias = jnp.sum(bundle_bias(own_ref) + bundle_bias(other_ref), axis=1, keepdims=True)
    owner = lax.div(lax.div(place, 8) * span, own_ref.shape[1])

    def unbundled(ref):
        mods = ref[80 : 80 + mods_rows].astype(F32) + ref[80 + mods_rows :].astype(F32)
        bias = jnp.broadcast_to(bundle_bias(ref), (8, mods.shape[1]))
        return jnp.concatenate([ref[0:64].astype(F32), bias, mods], axis=0)

    @pl.when(owner == lax.axis_index("mp"))
    def _():
        part[...] = unbundled(own_part_ref)

    @pl.when(owner != lax.axis_index("mp"))
    def _():
        part[...] = unbundled(other_part_ref)

    part[...] = reorder_blocks(part[...], jnp.bitwise_and(place, 7))
    centred = part[0:64] - total * (1.0 / D)
    centred_bias = part[64:65] - total_bias * (1.0 / D)
    row = lax.broadcasted_iota(jnp.int32, (STEP - 64, centred.shape[1]), 0)
    for flip in range(clips_sent):
        clip = jnp.bitwise_xor(rest, flip) * 2 + jnp.bitwise_xor(core, flip % 2)
        eight = part[pl.ds(pl.multiple_of(72 + 8 * lax.div(clip, 4), 8), 8)]
        first = 2 * lax.rem(clip, 4)
        shift = jnp.sum(jnp.where(row[:8] == first, eight, 0.0), axis=0, keepdims=True)
        scale = 1.0 + jnp.sum(jnp.where(row[:8] == first + 1, eight, 0.0), axis=0, keepdims=True)
        patch_rows = centred * scale
        extra = jnp.where(row == 0, centred_bias * scale, jnp.where(row == 1, shift, 0.0))
        rows_ref[pl.ds(flip * STEP, 64)] = patch_rows.astype(BF16)
        rows_ref[pl.ds(flip * STEP + 64, STEP - 64)] = extra.astype(BF16)


def modulated_rows(own, other, own_part, other_part, clips_sent, span):
    return pl.pallas_call(
        functools.partial(modulated_kernel, clips_sent, span),
        out_shape=jax.ShapeDtypeStruct((clips_sent * STEP, own_part.shape[1]), BF16),
        in_specs=[vmem()] * 4,
        out_specs=vmem(),
        scratch_shapes=[pltpu.VMEM((72 + (own.shape[0] - 80) // 2, own_part.shape[1]), F32)],
        compiler_params=params(),
        name="modulated_rows",
    )(own, other, own_part, other_part)


def free_lanes(lane, odd):
    return jnp.where(odd == 1, 0, HD // 2) == HD // 2 * lax.div(lane, HD // 2)


def doubled(values, lane, second):
    turned = pltpu.roll(values, HD // 2, 1)
    return jnp.where((lane < HD // 2) == (not second), values, turned)


def piece_chunks(refs, rows):
    whole = refs[0].shape[0] // rows
    for chunk in range(whole):
        yield jnp.concatenate([ref[pl.ds(chunk * rows, rows)] for ref in refs], axis=0)
    parts = []
    for ref in refs:
        half = ref[pl.ds(whole * rows, rows // 2)]
        parts += [half, pltpu.roll(half.astype(F32), HD // 2, 1).astype(BF16)]
    yield jnp.concatenate(parts, axis=0)


def piece_products(rows_here, refs, rows):
    chunks = list(piece_chunks(refs, rows))
    for chunk in range(0, len(chunks), 2):
        block = jnp.concatenate(chunks[chunk : chunk + 2], axis=1)
        yield chunk, jnp.dot(rows_here, block, preferred_element_type=F32)


def early_kernel(order, rows, rows_ref, *refs):
    out_ref = refs[-1]
    refs = [refs[order.index(block)] for block in sorted(order)]
    for chunk, total in piece_products(rows_ref[:, 0 : len(refs) * rows], refs, rows):
        out_ref[:, pl.ds(chunk * HD, 2 * HD)] = total


def early_rows(rows_here, pieces, rows):
    wide = (pieces[0].shape[0] // rows + 1) * HD
    return pl.pallas_call(
        functools.partial(early_kernel, list(pieces), rows),
        out_shape=jax.ShapeDtypeStruct((rows_here.shape[0], wide), F32),
        in_specs=[vmem()] * (1 + len(pieces)),
        out_specs=vmem(),
        compiler_params=params(),
        name="early_rows",
    )(rows_here, *pieces.values())


def product_kernel(clips_sent, order, rows, rows_ref, early_ref, *refs):
    refs, out_refs = refs[: len(order)], refs[len(order) :]
    refs = [refs[order.index(block)] for block in sorted(order)]
    done = rows_ref.shape[1] - len(order) * rows
    wide = early_ref.shape[1]
    tile = 2 * HD
    lane = lax.broadcasted_iota(jnp.int32, (8, HD), 1)
    row = lax.broadcasted_iota(jnp.int32, (8, HD), 0)
    odd = lax.rem(chip_block(), 2)
    ends = [[] for _ in range(clips_sent)]
    for first_chunk, total in piece_products(rows_ref[:, done:], refs, rows):
        start = first_chunk * HD
        columns = pl.ds(start, tile)
        total = total + early_ref[:, columns]
        for flip in range(clips_sent):
            base = flip * STEP
            for chunk in range(0, tile, HD):
                end = total[base + 64 : base + 72, chunk : chunk + HD]
                first = end.astype(BF16).astype(F32)
                end = first + pltpu.roll(end - first, 2, 0)
                low = doubled(end, lane, False)
                high = low if start + chunk + HD == wide else doubled(end, lane, True)
                ends[flip].append(jnp.where(row < 4, low, pltpu.roll(high, 4, 0)))
            patch_rows = total[base : base + 64]
            if start + tile == wide:
                wide_lane = lax.broadcasted_iota(jnp.int32, (64, HD), 1)
                last = jnp.where(
                    free_lanes(wide_lane, odd),
                    jnp.concatenate(ends[flip], axis=0),
                    doubled(patch_rows[:, tile - HD :], wide_lane, False),
                )
                patch_rows = jnp.concatenate([patch_rows[:, : tile - HD], last], axis=1)
            out_refs[flip][:, columns] = patch_rows.astype(BF16)


def product_rows(rows_here, early, pieces, clips_sent, rows):
    return pl.pallas_call(
        functools.partial(product_kernel, clips_sent, list(pieces), rows),
        out_shape=[jax.ShapeDtypeStruct((64, early.shape[1]), BF16)] * clips_sent,
        in_specs=[vmem()] * (2 + len(pieces)),
        out_specs=[vmem()] * clips_sent,
        compiler_params=params(),
        name="product_rows",
    )(rows_here, early, *pieces.values())


def split_ends(ends, row):
    ends = jnp.where(row < 2, ends + pltpu.roll(ends, 6, 0), 0.0)
    first = ends.astype(BF16).astype(F32)
    return first + pltpu.roll(ends - first, 2, 0)


def near_core(half):
    place = lax.axis_index("seq")
    core, low = lax.rem(place, 2), lax.rem(lax.div(place, 4), 2)
    return jnp.bitwise_xor(core, jnp.bitwise_xor(low, half))


def sum_kernel(flips, query_cols, pair_cols, *refs):
    in_refs, bias_ref = refs[: len(flips)], refs[len(flips)]
    out_ref, gram_ref, gram_sent_ref = refs[-3:]
    wide = out_ref.shape[2] - HD
    chunks = wide // HD
    own = lax.rem(lax.div(lax.axis_index("seq"), 4), 2)
    row = lax.broadcasted_iota(jnp.int32, (8, wide), 0)
    lane = lax.broadcasted_iota(jnp.int32, (1, wide), 1)
    chunk_lane = lax.broadcasted_iota(jnp.int32, (64, HD), 1)
    contract = (((1,), (1,)), ((), ()))
    grams = [jnp.zeros((WIRE, WIRE), F32)] * 2
    for parity in range(2):
        half = jnp.bitwise_xor(own, parity)
        odd = near_core(half)
        total = sum(ref[...].astype(F32) for ref, flip in zip(in_refs, flips) if flip % 2 == parity)
        last = total[:, wide - HD :]
        free = free_lanes(chunk_lane, odd)
        kept = jnp.where(free, last, pltpu.roll(last, HD // 2, 1))
        ends = []
        for chunk in range(chunks):
            eight = kept[8 * chunk : 8 * chunk + 8]
            ends.append(jnp.where(chunk_lane[:8] < HD // 2, eight, pltpu.roll(eight, 4, 0)))
        ends[-1] = kept[64 - 8 :]
        ends = jnp.where(row < 4, jnp.concatenate(ends, axis=1), 0.0)
        first = pl.multiple_of((half * 2 + odd) * wide, HD)
        ends = ends + jnp.where(row == 1, bias_ref[:, pl.ds(first, wide)], 0.0)
        ends = split_ends(ends, row)
        ends = ends + jnp.where(row == 4, pltpu.roll(ends, 3, 0), 0.0)
        rows = jnp.concatenate([total, ends], axis=0).astype(BF16)
        out_ref[half, :, 0:wide] = rows
        column = lane + (half * 2 + odd) * (wide - HD)
        tail = lane - (wide - HD)
        in_tail = tail >= 0
        column = jnp.where(in_tail, tail + BLOCKS * (wide - HD) + half * HD, column)
        held = jnp.logical_or(lane < wide - HD, lax.div(tail, HD // 2) == odd)
        pair = column - query_cols
        is_key = (pair >= 0) & (lax.rem(pair, 2 * HD) < HD)
        for which, keep in enumerate((pair < 0, is_key)):
            keep = jnp.where(keep, 1.0, 0.0) * jnp.where(held, 1.0, 0.0)
            kept = jnp.where(keep > 0.0, rows.astype(F32), 0.0).astype(BF16)
            grams[which] += lax.dot_general(kept, kept, contract, preferred_element_type=F32)
    row = lax.broadcasted_iota(jnp.int32, (WIRE, WIRE), 0)
    column = lax.broadcasted_iota(jnp.int32, (WIRE, WIRE), 1)
    both = jnp.where(
        row < column, 2.0 * grams[0], jnp.where(row == column, grams[0], 2.0 * grams[1])
    )
    diagonal = jnp.sum(jnp.where(row == column, grams[1], 0.0), axis=1, keepdims=True)
    gram_ref[:, 0:WIRE] = both
    gram_ref[:, WIRE:] = jnp.broadcast_to(diagonal, (WIRE, HD - WIRE))
    gram_sent_ref[...] = gram_ref[...].astype(BF16)
    for place, piece in enumerate(exact_pieces(gram_ref[...], 2)):
        out_ref[place, :, pl.ds(wide, HD)] = piece


def gram_halves(gram):
    row = lax.broadcasted_iota(jnp.int32, (WIRE, WIRE), 0)
    column = lax.broadcasted_iota(jnp.int32, (WIRE, WIRE), 1)
    both = gram[:, 0:WIRE]
    queries = jnp.where(row <= column, both, 0.0)
    keys = jnp.where(row > column, both, jnp.where(row == column, gram[:, WIRE : WIRE + 1], 0.0))
    return queries, keys


def sum_rows(arrived, bias, query_cols, pair_cols, ready):
    wide = next(iter(arrived.values())).shape[1]
    anywhere = pl.BlockSpec(memory_space=pl.ANY)
    return pl.pallas_call(
        functools.partial(sum_kernel, list(arrived), query_cols, pair_cols),
        out_shape=[
            jax.ShapeDtypeStruct((2, WIRE, wide + HD), BF16),
            jax.ShapeDtypeStruct((WIRE, HD), F32),
            jax.ShapeDtypeStruct((WIRE, HD), BF16),
        ],
        in_specs=[vmem()] * (len(arrived) + 1) + [anywhere] * len(ready),
        out_specs=[vmem()] * 3,
        compiler_params=params(),
        name="sum_rows",
    )(*arrived.values(), bias, *ready)


def rotary_tables(shape_ref, counts_ref, tokens):
    place = lax.axis_index("seq")
    clip, member = lax.div(place, GROUP), lax.rem(place, GROUP)
    height, width = shape_ref[clip, 1], shape_ref[clip, 2]
    first_count = counts_ref[clip * GROUP]
    slot = lax.broadcasted_iota(jnp.int32, (GROUP * tokens, HD), 0)
    own = slot < tokens
    offset = jnp.where(own, member * first_count, (1 - member) * first_count - tokens)
    position = (slot + offset).astype(F32)

    def quotient(values, divisor):
        return jnp.floor((values + 0.5) / divisor.astype(F32))

    line = quotient(position, width)
    frame = quotient(position, height * width)
    row = line - frame * height.astype(F32)
    column = position - line * width.astype(F32)

    other_pairs = HD // 6
    frame_pairs = HD // 2 - 2 * other_pairs
    lane = lax.broadcasted_iota(jnp.int32, (1, HD), 1)
    pair = lax.rem(lane, HD // 2)
    in_frame = pair < frame_pairs
    in_row = pair < frame_pairs + other_pairs
    before = jnp.where(in_frame, 0, jnp.where(in_row, frame_pairs, frame_pairs + other_pairs))
    span = jnp.where(in_frame, 2.0 * frame_pairs, 2.0 * other_pairs)
    inverse = jnp.exp(-(2.0 * (pair - before).astype(F32) / span) * math.log(10000.0))
    angles = jnp.where(in_frame, frame, jnp.where(in_row, row, column)) * inverse
    return jnp.cos(angles), jnp.sin(angles) * jnp.where(lane < HD // 2, -1.0, 1.0)


def pairs_apart():
    source = lax.broadcasted_iota(jnp.int32, (HD, HD), 0)
    lane = lax.broadcasted_iota(jnp.int32, (HD, HD), 1)
    wanted = 2 * lax.rem(lane, HD // 2) + lax.div(lane, HD // 2)
    return jnp.where(source == wanted, 1.0, 0.0).astype(BF16)


def spread_kernel(
    shape_ref,
    counts_ref,
    mine_ref,
    other_ref,
    here_ref,
    there_ref,
    gain_ref,
    bias_q_ref,
    bias_kv_ref,
    ready_ref,
    left_ref,
    turned_ref,
    spread_ref,
    cosine_ref,
    sine_ref,
    gain_apart_ref,
    bias_ref,
):
    tokens = mine_ref.shape[0]
    query_cols, pair_cols = bias_q_ref.shape[1], bias_kv_ref.shape[1]
    place = 0
    for block in range(BLOCKS):
        for first, size in block_spans(block, (query_cols + pair_cols) // HD):
            for ref, low in ((bias_q_ref, 0), (bias_kv_ref, query_cols)):
                start, stop = max(first, low), min(first + size, low + ref.shape[1])
                if start < stop:
                    here = pl.ds(place + start - first, stop - start)
                    values = ref[:, pl.ds(start - low, stop - start)]
                    bias_ref[:, here] = jnp.broadcast_to(values, (8, stop - start))
            place += size
    apart = pairs_apart()
    for head in range(gain_ref.shape[1] // HD):
        own = pl.ds(head * HD, HD)
        for which in range(2):
            gain = jnp.broadcast_to(gain_ref[which : which + 1, own], (8, HD))
            gain_apart_ref[which, :, own] = sum(
                jnp.dot(piece, apart, preferred_element_type=F32)
                for piece in exact_pieces(gain, 3)
            )
    cosine_ref[...], sine_ref[...] = rotary_tables(shape_ref, counts_ref, tokens)
    for part, ref in enumerate((mine_ref, other_ref)):
        rows = ref[...]
        pieces = []
        for half_ref in (here_ref, there_ref):
            pieces.append(
                jnp.dot(rows, half_ref[0:64], preferred_element_type=F32) + bundle_bias(half_ref)
            )
        average = sum(jnp.sum(piece, axis=1, keepdims=True) for piece in pieces) * (1.0 / D)
        squares = sum(
            jnp.sum((piece - average) * (piece - average), axis=1, keepdims=True)
            for piece in pieces
        )
        spread = jnp.sqrt(squares * (1.0 / D) + EPSILON)
        spread = jnp.broadcast_to(spread, (tokens, HD))
        first = spread.astype(BF16).astype(F32)
        lane = lax.broadcasted_iota(jnp.int32, (tokens, HD), 1)
        extra = jnp.where(
            (lane == 64) | (lane == 66),
            1.0,
            jnp.where(
                (lane == 65) | (lane == 67), first, jnp.where(lane == 68, spread - first, 0.0)
            ),
        )
        patch = jnp.concatenate([rows.astype(F32), jnp.zeros((tokens, HD - 64), F32)], axis=1)
        left = jnp.where(lane < 64, patch, extra)
        here = pl.ds(part * tokens, tokens)
        left_ref[here] = left.astype(BF16)
        turned_ref[:, here] = left.T.astype(BF16)
        spread_ref[here] = spread


def spread_rows(clip_shape, shard_counts, mine, other, here, there, gains, biases, ready):
    tokens = mine.shape[0]
    return pl.pallas_call(
        spread_kernel,
        out_shape=[
            jax.ShapeDtypeStruct((2 * tokens, HD), BF16),
            jax.ShapeDtypeStruct((HD, 2 * tokens), BF16),
        ]
        + [jax.ShapeDtypeStruct((2 * tokens, HD), F32)] * 3
        + [jax.ShapeDtypeStruct((2, 8, gains.shape[1]), F32)]
        + [jax.ShapeDtypeStruct((8, BLOCKS * ready.shape[1]), F32)],
        in_specs=[smem()] * 2 + [vmem()] * 7 + [pl.BlockSpec(memory_space=pl.ANY)],
        out_specs=[vmem()] * 7,
        compiler_params=params(),
        name="spread_rows",
    )(clip_shape, shard_counts, mine, other, here, there, gains, *biases, ready)


def heads_kernel(
    heads_here,
    counts_ref,
    left_ref,
    mine_ref,
    theirs_ref,
    spread_ref,
    cosine_ref,
    sine_ref,
    gain_ref,
    q_ref,
    k_ref,
    v_ref,
    rows,
):
    tokens = q_ref.shape[0]
    whole, shared = block_chunks(3 * heads_here)
    lane = lax.broadcasted_iota(jnp.int32, (WIRE, HD), 1)
    for half in range(2):
        near = near_core(half)
        for ref, core in ((mine_ref, near), (theirs_ref, 1 - near)):
            for chunk in range(whole):
                columns = ref[half, :, chunk * HD : (chunk + 1) * HD]
                rows[(half * 2 + core) * whole + chunk, 0:WIRE] = columns
        last = pl.ds(whole * HD, HD)
        mine, theirs = mine_ref[half, :, last].astype(F32), theirs_ref[half, :, last].astype(F32)
        columns = jnp.where(free_lanes(lane, near), theirs, mine)
        rows[shared + half, 0:WIRE] = columns.astype(BF16)
    place = lax.axis_index("seq")
    count_own, count_other = counts_ref[place], counts_ref[jnp.bitwise_xor(place, 1)]
    slot = lax.broadcasted_iota(jnp.int32, (2 * tokens, HD), 0)
    valid = slot < jnp.where(slot < tokens, count_own, tokens + count_other)
    left = left_ref[:, 0:WIRE]
    inverse = jnp.where(valid, 1.0 / spread_ref[...], 0.0)
    turned = list(range(heads_here)) + [heads_here + 2 * head for head in range(heads_here)]
    together = jnp.concatenate([rows[chunk] for chunk in turned], axis=0)
    together = jnp.dot(together, pairs_apart(), preferred_element_type=F32).astype(BF16)

    def projected(first, second, count):
        weight = jnp.concatenate([first, second], axis=1)
        found = jnp.dot(left[:count], weight, preferred_element_type=F32)
        return found[:, :HD], found[:, HD:]

    def rotated(values, gain, count):
        values = values * gain
        return values * cosine_ref[:count] + pltpu.roll(values, HD // 2, 1) * sine_ref[:count]

    def apart(index):
        return together[index * STEP : index * STEP + WIRE]

    for head in range(0, heads_here, 2):
        pair = (head, head + 1)
        for turn, found in zip(pair, projected(*[apart(turn) for turn in pair], tokens)):
            own = pl.ds(turn * HD, HD)
            q_ref[:, own] = rotated(found, gain_ref[0, 0:1, own], tokens)
        weights = [apart(heads_here + turn) for turn in pair]
        for turn, found in zip(pair, projected(*weights, 2 * tokens)):
            own = pl.ds(turn * HD, HD)
            k_ref[:, own] = rotated(found, gain_ref[1, 0:1, own], 2 * tokens).astype(BF16)
        weights = [rows[heads_here + 2 * turn + 1, 0:WIRE] for turn in pair]
        for turn, found in zip(pair, projected(*weights, 2 * tokens)):
            v_ref[:, pl.ds(turn * HD, HD)] = (found * inverse).astype(BF16)


def heads_rows(counts, left, mine, theirs, spread, cosine, sine, gains, heads_here):
    both = left.shape[0]
    wide = heads_here * HD
    return pl.pallas_call(
        functools.partial(heads_kernel, heads_here),
        out_shape=[
            jax.ShapeDtypeStruct((both // 2, wide), F32),
            jax.ShapeDtypeStruct((both, wide), BF16),
            jax.ShapeDtypeStruct((both, wide), BF16),
        ],
        in_specs=[smem()] + [vmem()] * 7,
        out_specs=[vmem()] * 3,
        scratch_shapes=[pltpu.VMEM((3 * heads_here, STEP, HD), BF16)],
        compiler_params=params(),
        name="heads_rows",
    )(counts, left, mine, theirs, spread, cosine, sine, gains)


def attend_kernel(
    heads_here, counts_ref, q_ref, k_ref, v_ref, left_ref, turned_ref, theirs_ref, *refs
):
    gram_refs, (out_ref, found, sems) = refs[:-3], refs[-3:]
    tokens = q_ref.shape[0]
    place = lax.axis_index("seq")
    count_own, count_other = counts_ref[place], counts_ref[jnp.bitwise_xor(place, 1)]

    left = left_ref[0:tokens, 0:WIRE]
    turned = turned_ref[0:WIRE]
    last = theirs_ref.shape[2] - HD
    gram = sum(ref[...].astype(F32) for ref in gram_refs)
    for place in range(2):
        gram = gram + theirs_ref[place, :, last:].astype(F32)
    gram = gram * (1.0 / D)
    gram_q, gram_k = [exact_pieces(values, 2) for values in gram_halves(gram)]
    spun_q = sum(jnp.dot(left, piece, preferred_element_type=F32) for piece in gram_q)
    wide_left = left_ref[0:tokens].astype(F32)
    square_q = jnp.sum(spun_q * wide_left[:, 0:WIRE], axis=1, keepdims=True)
    spread_q = wide_left[:, 65:66] + wide_left[:, 68:69]
    scale_q = lax.rsqrt(square_q + EPSILON * spread_q * spread_q) * (
        math.log2(math.e) / math.sqrt(HD)
    )
    scale_q = jnp.broadcast_to(scale_q, (tokens, HD))
    spun_k = sum(jnp.dot(piece, turned, preferred_element_type=F32) for piece in gram_k)
    wide_turned = turned.astype(F32)
    square_k = jnp.sum(spun_k * wide_turned, axis=0, keepdims=True)
    spread_k = wide_turned[65:66] + wide_turned[68:69]
    scale_k = lax.rsqrt(square_k + EPSILON * spread_k * spread_k)
    slot = lax.broadcasted_iota(jnp.int32, (1, 2 * tokens), 1)
    valid = slot < jnp.where(slot < tokens, count_own, tokens + count_other)
    scale_k = jnp.where(valid, scale_k, 0.0)

    slot = lax.broadcasted_iota(jnp.int32, (2 * tokens, HD), 0)
    valid = slot < jnp.where(slot < tokens, count_own, tokens + count_other)
    ones = jnp.where(valid, 1.0, 0.0).astype(BF16)
    row = lax.broadcasted_iota(jnp.int32, (tokens, HD), 0)
    contract = (((1,), (1,)), ((), ()))

    def scores_of(head):
        own = pl.ds(head * HD, HD)
        query = (q_ref[:, own] * scale_q).astype(BF16)
        return lax.dot_general(query, k_ref[:, own], contract, preferred_element_type=F32)

    copies = []
    scores = scores_of(0)
    for head in range(heads_here):
        own = pl.ds(head * HD, HD)
        later = scores_of(head + 1) if head + 1 < heads_here else None
        weights = jnp.exp2(scores * scale_k).astype(BF16)
        values = jnp.concatenate([v_ref[:, own], ones], axis=1)
        result = jnp.dot(weights, values, preferred_element_type=F32)
        result = result[:, 0:HD] / result[:, HD:]
        found[:, own] = jnp.where(row < count_own, result, 0.0).astype(BF16)
        copies.append(pltpu.make_async_copy(found.at[:, own], out_ref.at[:, own], sems.at[head]))
        copies[-1].start()
        scores = later
    for copy in copies:
        copy.wait()


def attend_rows(counts, queries, keys, values, left, turned, theirs, grams):
    heads_here = queries.shape[1] // HD
    return pl.pallas_call(
        functools.partial(attend_kernel, heads_here),
        out_shape=jax.ShapeDtypeStruct(queries.shape, BF16),
        in_specs=[smem()] + [vmem()] * (6 + len(grams)),
        out_specs=pl.BlockSpec(memory_space=pl.ANY),
        scratch_shapes=[
            pltpu.VMEM(queries.shape, BF16),
            pltpu.SemaphoreType.DMA((heads_here,)),
        ],
        compiler_params=params(),
        name="attend_rows",
    )(counts, queries, keys, values, left, turned, theirs, *grams)


def shards(
    patches,
    clip_shape,
    shard_counts,
    patch_weight,
    patch_bias,
    time_mod,
    block_mod,
    w_query,
    query_bias,
    w_keyvalue,
    keyvalue_bias,
    norm_gain,
):
    tokens = patches.shape[0]
    heads_here = w_query.shape[1] // HD
    count = lax.axis_size("seq")
    halves = lax.axis_size("mp")
    place = lax.axis_index("seq")
    clips = time_mod.shape[0]
    rows = w_query.shape[0]
    padded = -(-rows // 16) * 16
    clips_sent = count // 4

    def pad_rows(values):
        return values if rows == padded else jnp.pad(values, ((0, padded - rows), (0, 0)))

    packed = pack_weights(pad_rows(w_query), pad_rows(w_keyvalue))
    pieces = [packed[0]] + [swap_bits(packed[flip], 2 * flip) for flip in range(1, BLOCKS)]
    first_swapped = swap_bits(packed[0], 1)

    features = patch_bias.shape[0]
    own, own_patches = prepare_rows(
        patch_weight, patch_bias[None], time_mod, block_mod, patches, first_swapped
    )
    other = lax.ppermute(own, "mp", [(i, (i + 1) % halves) for i in range(halves)])
    other_patches = swap_bits(own_patches, 1)
    span = 8 * rows

    def group_part(values):
        if span == features and rows == padded:
            return values
        values = lax.dynamic_slice_in_dim(values, place // 8 * span % features, span, 1)
        values = jnp.pad(
            values.reshape(-1, 8, rows), ((0, 0), (0, 0), (0, padded - rows))
        )
        return values.reshape(-1, 8 * padded)

    rows_here = modulated_rows(
        own, other, group_part(own), group_part(other), clips_sent, span
    )
    placed = {0: packed[0], 1: first_swapped}
    for flip in reversed(range(1, BLOCKS)):
        piece = after(pieces[flip], rows_here, other_patches)
        placed[2 * flip], placed[2 * flip + 1] = piece, swap_bits(piece, 1)
    first = {order: placed.pop(order) for order in (6, 4, 5, 2, 3, 0, 1)}
    early = early_rows(rows_here, first, padded)

    products = product_rows(rows_here, early, placed, clips_sent, padded)
    arrived = {}
    for flip in reversed(range(clips_sent)):
        pairs = []
        for source in range(count):
            rest, second, core = source // 4, source // 2 % 2, source % 2
            turn = flip % 2
            pairs.append((source, (rest ^ flip) * 4 + (core ^ turn) * 2 + (second ^ turn)))
        arrived[flip] = lax.ppermute(products[flip], "seq", pairs)
    biases = (query_bias[None], keyvalue_bias[None])
    left, turned, spread, cosine, sine, gains, bias = spread_rows(
        clip_shape,
        shard_counts,
        own_patches,
        other_patches,
        own,
        other,
        norm_gain,
        biases,
        products[0],
    )

    mine, gram, gram_sent = sum_rows(arrived, bias, w_query.shape[1], w_keyvalue.shape[1], (left,))
    theirs = swap_bits(mine, 1)
    far_mp = [(i, (i + 1) % halves) for i in range(halves)]
    far_both = [
        (core * halves + i, (core ^ 1) * halves + j) for core in range(count) for i, j in far_mp
    ]
    grams = (
        gram,
        lax.ppermute(gram_sent, "mp", far_mp),
        lax.ppermute(gram_sent, ("seq", "mp"), far_both),
    )
    queries, keys, values = heads_rows(
        shard_counts, left, mine, theirs, spread, cosine, sine, gains, heads_here
    )
    return attend_rows(shard_counts, queries, keys, values, left, turned, theirs, grams)


def solution(mesh):
    return jax.shard_map(
        shards,
        mesh=mesh,
        in_specs=(
            P("seq", None),
            P(),
            P(),
            P(None, "mp"),
            P("mp"),
            P(None, None, "mp"),
            P(None, "mp"),
            P("seq", "mp"),
            P("mp"),
            P("seq", "mp"),
            P("mp"),
            P(None, "mp"),
        ),
        out_specs=P("seq", "mp"),
        check_vma=False,
    )
```

time: 244 us -> 46.2 us (0.19); the launches traced: 241 us -> 46 us
  waiting for transfers between devices: 142 us -> 13.3 us
  local copies, waits for them, and re-layouts: 28 us -> 1.02 us
  matrix products: 19.1 us -> 0 us
  between operations: 18 us -> 0.25 us
  other arithmetic: 16.4 us -> 0 us
  starting transfers between devices: 1.48 us -> 17.7 us
  blocking collectives: 15.8 us -> 0 us
  Pallas kernels: 0 us -> 13.8 us
    all_gather x2 -> x0, waiting for transfers between devices: 140 us -> none  [the longest x1 98.5 us: shards(): lax.all_gather(w_keyvalue, 'seq', axis=0, tiled=True)]
    dot_general x5 -> x0, matrix products: 19.1 us -> none  [the longest x2 15.7 us: contract(): return jnp.dot(left_rows, pieces, preferred_element_type=jnp.float32)]
    ppermute x1 -> x16, starting transfers between devices: 1.4 us -> 17.7 us  [the longest x9 8.26 us: swap_bits(): lax.ppermute(value, 'seq', [(source, source ^ mask) for source in range(c...]
    pallas_call x0 -> x12, Pallas kernels: none -> 13.8 us  [the longest x1 3.73 us: spread_rows(): pl.pallas_call(spread_kernel, out_shape=[jax.ShapeDtypeStruct((2 * tokens...]
    ppermute x1 -> x16, waiting for transfers between devices: 0.01 us -> 13.3 us  [the longest x4 5.41 us: shards(): arrived[flip] = lax.ppermute(products[flip], 'seq', pairs)]
    slice x10 -> x0, local copies, waits for them, and re-layouts: 12.1 us -> none  [the longest x2 4.82 us: split_pairs(): key_raw = pair_raw[:, :, 0].reshape(tokens, heads_here * HD)]
    all_gather x3 -> x0, blocking collectives: 11.8 us -> none  [the longest x1 5.06 us: shards(): full_weight = lax.all_gather(patch_weight, 'mp', axis=1, tiled=True)]
    concatenate x3 -> x0, other arithmetic: 4.8 us -> none  [the longest x1 3.28 us: rotate_pairs(): jnp.roll(values, 1, axis=-1)]
  transfers between devices with their start and end apart: 3 -> 16, of which waited for: 2 -> 5; matrix products, arithmetic and copies ran while one was open for 7% -> 2% of each run, Pallas kernels for 0% -> 17%
where the time goes in v2:
time: 46.2 us; the launch traced here: 46 us
  starting transfers between devices  17.7 us (38%)
  Pallas kernels  13.8 us (30%)
  waiting for transfers between devices  13.3 us (29%)
  local copies, waits for them, and re-layouts  1.02 us (2%)
    ppermute x9, starting transfers between devices, swap_bits(): lax.ppermute(value, 'seq', [(source, source ^ mask) for source in range(c...  8.26 us
    ppermute x4, starting transfers between devices, shards(): arrived[flip] = lax.ppermute(products[flip], 'seq', pairs)  6.41 us
    ppermute x4, waiting for transfers between devices, shards(): arrived[flip] = lax.ppermute(products[flip], 'seq', pairs)  5.41 us
    ppermute x1, waiting for transfers between devices, shards(): lax.ppermute(own, 'mp', [(i, (i + 1) % halves) for i in range(halves)])  5.04 us
    pallas_call x1, Pallas kernels, spread_rows(): pl.pallas_call(spread_kernel, out_shape=[jax.ShapeDtypeStruct((2 * tokens...  3.73 us
    pallas_call x1, Pallas kernels, attend_rows(): pl.pallas_call(functools.partial(attend_kernel, heads_here), out_shape=ja...  3.32 us
    ppermute x9, waiting for transfers between devices, swap_bits(): lax.ppermute(value, 'seq', [(source, source ^ mask) for source in range(c...  2.41 us
    pallas_call x1, Pallas kernels, heads_rows(): pl.pallas_call(functools.partial(heads_kernel, heads_here), out_shape=[ja...  2.26 us
  transfers between devices with their start and end apart: 16, of which 5 were waited for; matrix products, arithmetic and copies ran while one was open for 2% of the time, Pallas kernels for 17%

profile of v2, /device:TPU:17, one launch (start us, length us, event | category | flops | bytes accessed | tf_op | source)
XLA Modules:
  0.0 46.0 jit_solution(9697316856749032099)
XLA Ops:
  0.0 1.5 %pack_weights.1 = (bf16[1200,128]{1,0:T(8,128)(2,1)S(1)}, bf16[1200,128]{1,0:T(8,128)(2,1)S(1)}, bf16[1200,128]{1,0:T(8,128)(2,1)S(1)}, bf16[1200,128]{1,0:T(8,128)(2,1)S(1)}) custom-call(bf16[160,1280]{1,0:T(8,128)(2,1)} %wq_ref.1, bf16[160,2560]{1,0:T(8,128)(2,1)} %wkv_ref.1), custom_call_target="tpu_custom_call" | custom-call | tf_op jit(solution)/shard_map/pack_weights/pallas_call | solution.py:166
  1.6 0.7 %collective-permute-start = (bf16[1200,128]{1,0:T(8,128)(2,1)S(1)}, bf16[1200,128]{1,0:T(8,128)(2,1)S(1)}, u32[]{:S(2)}, u32[]{:S(2)}) collective-permute-start(bf16[1200,128]{1,0:T(8,128)(2,1)S(1)} %get-tuple-element.28.refs_5_), channel_id=1, source_target_pairs={{0,2},{2,0},{4,6},{6,4},{8,10},{10,8},{12,14},{14,12},{16,18},{18,... | collective-permute-start | bytes 921608 | tf_op jit(solution)/shard_map/ppermute | solution.py:39
  2.3 1.2 %collective-permute-start.6 = (bf16[1200,128]{1,0:T(8,128)(2,1)S(1)}, bf16[1200,128]{1,0:T(8,128)(2,1)S(1)}, u32[]{:S(2)}, u32[]{:S(2)}) collective-permute-start(bf16[1200,128]{1,0:T(8,128)(2,1)S(1)} %get-tuple-element.33), channel_id=1, source_target_pairs={{0,4},{2,6},{4,0},{6,2},{8,12},{10,14},{12,8},{14,10},{16,20},{18,... | collective-permute-start | bytes 921608 | tf_op jit(solution)/shard_map/ppermute | solution.py:39
  3.6 1.3 %collective-permute-start.4 = (bf16[1200,128]{1,0:T(8,128)(2,1)S(1)}, bf16[1200,128]{1,0:T(8,128)(2,1)S(1)}, u32[]{:S(2)}, u32[]{:S(2)}) collective-permute-start(bf16[1200,128]{1,0:T(8,128)(2,1)S(1)} %get-tuple-element.32), channel_id=1, source_target_pairs={{0,8},{2,10},{4,12},{6,14},{8,0},{10,2},{12,4},{14,6},{16,24},{18,... | collective-permute-start | bytes 921608 | tf_op jit(solution)/shard_map/ppermute | solution.py:39
  5.0 0.9 %copy.16.patches_ref = bf16[256,64]{1,0:T(8,128)(2,1)S(1)} copy(bf16[256,64]{0,1:T(8,128)(2,1)} %param.12) | data formatting | bytes 65536 | tf_op args[0]
  6.0 1.3 %collective-permute-start.2 = (bf16[112,1280]{1,0:T(8,128)(2,1)S(1)}, bf16[112,1280]{1,0:T(8,128)(2,1)S(1)}, u32[]{:S(2)}, u32[]{:S(2)}) collective-permute-start(bf16[112,1280]{1,0:T(8,128)(2,1)S(1)} %get-tuple-element.30.own_ref.own_part_ref.here_ref), channel_id=1, source_target_pairs={{0,1},{1,0},{2,3},{3,2},{4,5},{5,4},{6,7},{7,6},{8,9},{9,8},{10,11... | collective-permute-start | bytes 860168 | tf_op jit(solution)/shard_map/ppermute | solution.py:749
  7.3 1.2 %collective-permute-start.1 = (bf16[256,64]{1,0:T(8,128)(2,1)S(1)}, bf16[256,64]{1,0:T(8,128)(2,1)S(1)}, u32[]{:S(2)}, u32[]{:S(2)}) collective-permute-start(bf16[256,64]{1,0:T(8,128)(2,1)S(1)} %get-tuple-element.29.mine_ref), channel_id=1, source_target_pairs={{0,2},{2,0},{4,6},{6,4},{8,10},{10,8},{12,14},{14,12},{16,18},{18,... | collective-permute-start | bytes 98312 | tf_op jit(solution)/shard_map/ppermute | solution.py:39
  8.5 5.0 %collective-permute-done.2.other_ref.other_part_ref.there_ref = bf16[112,1280]{1,0:T(8,128)(2,1)S(1)} collective-permute-done((bf16[112,1280]{1,0:T(8,128)(2,1)S(1)}, bf16[112,1280]{1,0:T(8,128)(2,1)S(1)}, u32[]{:S(2)}, u32[]{:S(2)}) %collective-permute-start.2) | collective-permute-done | bytes 286752 | tf_op jit(solution)/shard_map/ppermute | solution.py:749
  13.5 0.8 %modulated_rows.1.refs_1_.rows_ref = bf16[320,1280]{1,0:T(8,128)(2,1)S(1)} custom-call(bf16[112,1280]{1,0:T(8,128)(2,1)S(1)} %get-tuple-element.30.own_ref.own_part_ref.here_ref, bf16[112,1280]{1,0:T(8,128)(2,1)S(1)} %collective-permute-done.2.other_ref.other_part_ref.there_ref, bf16[112,1280]{1,0:T(8,128)(2,1)S(1)} %get-tuple-element.30.own_ref.own_part_ref.here_ref, ...), custom_call_target="tpu_custom_call" | custom-call | tf_op jit(solution)/shard_map/modulated_rows/pallas_call | solution.py:232
  14.4 1.9 %collective-permute-start.7 = (bf16[1200,128]{1,0:T(8,128)(2,1)S(1)}, bf16[1200,128]{1,0:T(8,128)(2,1)S(1)}, u32[]{:S(2)}, u32[]{:S(2)}) collective-permute-start(bf16[1200,128]{1,0:T(8,128)(2,1)S(1)} %after.5.refs_3_), channel_id=1, source_target_pairs={{0,2},{2,0},{4,6},{6,4},{8,10},{10,8},{12,14},{14,12},{16,18},{18,... | collective-permute-start | bytes 921608 | tf_op jit(solution)/shard_map/ppermute | solution.py:39
  16.4 2.3 %collective-permute-done.3.refs_0_ = bf16[1200,128]{1,0:T(8,128)(2,1)S(1)} collective-permute-done((bf16[1200,128]{1,0:T(8,128)(2,1)S(1)}, bf16[1200,128]{1,0:T(8,128)(2,1)S(1)}, u32[]{:S(2)}, u32[]{:S(2)}) %collective-permute-start.3) | collective-permute-done | bytes 307232 | tf_op jit(solution)/shard_map/ppermute | solution.py:39
  18.6 1.2 %collective-permute-start.8 = (bf16[1200,128]{1,0:T(8,128)(2,1)S(1)}, bf16[1200,128]{1,0:T(8,128)(2,1)S(1)}, u32[]{:S(2)}, u32[]{:S(2)}) collective-permute-start(bf16[1200,128]{1,0:T(8,128)(2,1)S(1)} %after.3.refs_0_), channel_id=1, source_target_pairs={{0,2},{2,0},{4,6},{6,4},{8,10},{10,8},{12,14},{14,12},{16,18},{18,... | collective-permute-start | bytes 921608 | tf_op jit(solution)/shard_map/ppermute | solution.py:39
  19.8 1.0 %early_rows.1.early_ref = f32[320,1024]{1,0:T(8,128)S(1)} custom-call(bf16[320,1280]{1,0:T(8,128)(2,1)S(1)} %modulated_rows.1.refs_1_.rows_ref, bf16[1200,128]{1,0:T(8,128)(2,1)S(1)} %after.3.refs_0_, bf16[1200,128]{1,0:T(8,128)(2,1)S(1)} %after.4.refs_1_, bf16[1200,128]{1,0:T(8,128)(2,1)S(1)} %collective-permute-done.5.refs_2_, ...), custom_call_target="tpu_custom_call" | custom-call | tf_op jit(solution)/shard_map/early_rows/pallas_call | solution.py:279
  21.5 1.3 %collective-permute-start.10 = (bf16[64,1024]{1,0:T(8,128)(2,1)S(1)}, bf16[64,1024]{1,0:T(8,128)(2,1)S(1)}, u32[]{:S(2)}, u32[]{:S(2)}) collective-permute-start(bf16[64,1024]{1,0:T(8,128)(2,1)S(1)} %get-tuple-element.37), channel_id=1, source_target_pairs={{0,16},{2,20},{4,18},{6,22},{8,24},{10,28},{12,26},{14,30},{16,0},... | collective-permute-start | bytes 393224 | tf_op jit(solution)/shard_map/ppermute | solution.py:780
  22.8 1.3 %collective-permute-start.11 = (bf16[64,1024]{1,0:T(8,128)(2,1)S(1)}, bf16[64,1024]{1,0:T(8,128)(2,1)S(1)}, u32[]{:S(2)}, u32[]{:S(2)}) collective-permute-start(bf16[64,1024]{1,0:T(8,128)(2,1)S(1)} %get-tuple-element.38), channel_id=1, source_target_pairs={{0,14},{2,10},{4,12},{6,8},{8,6},{10,2},{12,4},{14,0},{16,30},{18,... | collective-permute-start | bytes 393224 | tf_op jit(solution)/shard_map/ppermute | solution.py:780
  24.1 2.5 %collective-permute-start.12 = (bf16[64,1024]{1,0:T(8,128)(2,1)S(1)}, bf16[64,1024]{1,0:T(8,128)(2,1)S(1)}, u32[]{:S(2)}, u32[]{:S(2)}) collective-permute-start(bf16[64,1024]{1,0:T(8,128)(2,1)S(1)} %get-tuple-element.34.ready_ref), channel_id=1, source_target_pairs={{0,0},{2,4},{4,2},{6,6},{8,8},{10,12},{12,10},{14,14},{16,16},{18,... | collective-permute-start | bytes 393224 | tf_op jit(solution)/shard_map/ppermute | solution.py:780
  26.6 1.3 %collective-permute-start.9 = (bf16[64,1024]{1,0:T(8,128)(2,1)S(1)}, bf16[64,1024]{1,0:T(8,128)(2,1)S(1)}, u32[]{:S(2)}, u32[]{:S(2)}) collective-permute-start(bf16[64,1024]{1,0:T(8,128)(2,1)S(1)} %get-tuple-element.36), channel_id=1, source_target_pairs={{0,30},{2,26},{4,28},{6,24},{8,22},{10,18},{12,20},{14,16},{16,14}... | collective-permute-start | bytes 393224 | tf_op jit(solution)/shard_map/ppermute | solution.py:780
  28.0 3.7 %spread_rows.1 = (bf16[512,128]{1,0:T(8,128)(2,1)S(1)}, bf16[128,512]{1,0:T(8,128)(2,1)S(1)}, f32[512,128]{1,0:T(8,128)S(1)}, f32[512,128]{1,0:T(8,128)S(1)}, f3...) custom-call(s32[8,3]{1,0:T(8,128)S(1)} %copy.17.shape_ref, s32[16]{0:T(128)S(1)} %copy-done.4, ...), custom_call_target="tpu_custom_call" | custom-call | tf_op jit(solution)/shard_map/spread_rows/pallas_call | solution.py:539
  31.8 5.4 %collective-permute-done.9.refs_0_ = bf16[64,1024]{1,0:T(8,128)(2,1)S(1)} collective-permute-done((bf16[64,1024]{1,0:T(8,128)(2,1)S(1)}, bf16[64,1024]{1,0:T(8,128)(2,1)S(1)}, u32[]{:S(2)}, u32[]{:S(2)}) %collective-permute-start.9) | collective-permute-done | bytes 131104 | tf_op jit(solution)/shard_map/ppermute | solution.py:780
  37.2 0.5 %sum_rows.1 = (bf16[2,72,1152]{2,1,0:T(8,128)(2,1)S(1)}, f32[72,128]{1,0:T(8,128)S(1)}, bf16[72,128]{1,0:T(8,128)(2,1)S(1)}) custom-call(bf16[64,1024]{1,0:T(8,128)(2,1)S(1)} %collective-permute-done.9.refs_0_, bf16[64,1024]{1,0:T(8,128)(2,1)S(1)} %collective-permute-done.10.refs_1_, bf16[64,1024]{1,0:T(8,128)(2,1)S(1)} %collective-permute-done.11.refs_2_, ...), custom_call_target="tpu_custom_call" | custom-call | tf_op jit(solution)/shard_map/sum_rows/pallas_call | solution.py:413
  37.7 0.5 %collective-permute-start.13 = (bf16[2,72,1152]{2,1,0:T(8,128)(2,1)S(1)}, bf16[2,72,1152]{2,1,0:T(8,128)(2,1)S(1)}, u32[]{:S(2)}, u32[]{:S(2)}) collective-permute-start(bf16[2,72,1152]{2,1,0:T(8,128)(2,1)S(1)} %get-tuple-element.40.mine_ref), channel_id=1, source_target_pairs={{0,2},{2,0},{4,6},{6,4},{8,10},{10,8},{12,14},{14,12},{16,18},{18,... | collective-permute-start | bytes 995336 | tf_op jit(solution)/shard_map/ppermute | solution.py:39
  38.2 1.2 %collective-permute-start.14 = (bf16[72,128]{1,0:T(8,128)(2,1)S(1)}, bf16[72,128]{1,0:T(8,128)(2,1)S(1)}, u32[]{:S(2)}, u32[]{:S(2)}) collective-permute-start(bf16[72,128]{1,0:T(8,128)(2,1)S(1)} %get-tuple-element.50), channel_id=1, source_target_pairs={{0,1},{1,0},{2,3},{3,2},{4,5},{5,4},{6,7},{7,6},{8,9},{9,8},{10,11... | collective-permute-start | bytes 55304 | tf_op jit(solution)/shard_map/ppermute | solution.py:802
  40.0 2.3 %heads_rows.1 = (f32[256,1280]{1,0:T(8,128)S(1)}, bf16[512,1280]{1,0:T(8,128)(2,1)S(1)}, bf16[512,1280]{1,0:T(8,128)(2,1)S(1)}) custom-call(s32[16]{0:T(128)S(1)} %copy-done.4, bf16[512,128]{1,0:T(8,128)(2,1)S(1)} %get-tuple-element.35.refs_5_.left_ref, bf16[2,72,1152]{2,1,0:T(8,128)(2,1)S(1)} %get-tuple-element.40.mine_ref, ...), custom_call_target="tpu_custom_call" | custom-call | tf_op jit(solution)/shard_map/heads_rows/pallas_call | solution.py:622
  42.7 3.3 %attend_rows.1 = bf16[256,1280]{1,0:T(8,128)(2,1)} custom-call(s32[16]{0:T(128)S(1)} %copy-done.4, f32[256,1280]{1,0:T(8,128)S(1)} %get-tuple-element.45.q_ref, bf16[512,1280]{1,0:T(8,128)(2,1)S(1)} %get-tuple-element.46.k_ref, bf16[512,1280]{1,0:T(8,128)(2,1)S(1)} %get-tuple-element.47.v_ref, bf16[512,128]{1,0:T(8,128)(2,1)S(1)} %get-tuple-element.35.refs_5_.left_ref, ...), custom_call_target="tpu_custom_call" | custom-call | tf_op jit(solution)/shard_map/attend_rows/pallas_call | solution.py:700
  (43 shorter events, 2.0 us)
Async XLA Ops:
  0.0 5.9 %copy-start = (bf16[64,1280]{1,0:T(8,128)(2,1)S(1)}, bf16[64,1280]{1,0:T(8,128)(2,1)}, u32[]{:S(2)}) copy-start(bf16[64,1280]{1,0:T(8,128)(2,1)} %weight_ref.1) | copy-start | bytes 491524
  0.0 5.9 %copy-start.1 = (f32[8,2,1280]{2,1,0:T(2,128)S(1)}, f32[8,2,1280]{2,1,0:T(2,128)}, u32[]{:S(2)}) copy-start(f32[8,2,1280]{2,1,0:T(2,128)} %time_ref.1) | copy-start | bytes 245764
  0.0 5.9 %copy-start.2 = (f32[2,1280]{1,0:T(2,128)S(1)}, f32[2,1280]{1,0:T(2,128)}, u32[]{:S(2)}) copy-start(f32[2,1280]{1,0:T(2,128)} %block_ref.1) | copy-start | bytes 30724
  1.6 4.3 %collective-permute-start = (bf16[1200,128]{1,0:T(8,128)(2,1)S(1)}, bf16[1200,128]{1,0:T(8,128)(2,1)S(1)}, u32[]{:S(2)}, u32[]{:S(2)}) collective-permute-start(bf16[1200,128]{1,0:T(8,128)(2,1)S(1)} %get-tuple-element.28.refs_5_), channel_id=1, source_target_pairs={{0,2},{2,0},{4,6},{6,4},{8,10},{10,8},{12,14},{14,12},{16,18},{18,... | collective-permute-start | bytes 921608 | tf_op jit(solution)/shard_map/ppermute | solution.py:39
  2.3 12.0 %collective-permute-start.6 = (bf16[1200,128]{1,0:T(8,128)(2,1)S(1)}, bf16[1200,128]{1,0:T(8,128)(2,1)S(1)}, u32[]{:S(2)}, u32[]{:S(2)}) collective-permute-start(bf16[1200,128]{1,0:T(8,128)(2,1)S(1)} %get-tuple-element.33), channel_id=1, source_target_pairs={{0,4},{2,6},{4,0},{6,2},{8,12},{10,14},{12,8},{14,10},{16,20},{18,... | collective-permute-start | bytes 921608 | tf_op jit(solution)/shard_map/ppermute | solution.py:39
  3.6 12.7 %collective-permute-start.4 = (bf16[1200,128]{1,0:T(8,128)(2,1)S(1)}, bf16[1200,128]{1,0:T(8,128)(2,1)S(1)}, u32[]{:S(2)}, u32[]{:S(2)}) collective-permute-start(bf16[1200,128]{1,0:T(8,128)(2,1)S(1)} %get-tuple-element.32), channel_id=1, source_target_pairs={{0,8},{2,10},{4,12},{6,14},{8,0},{10,2},{12,4},{14,6},{16,24},{18,... | collective-permute-start | bytes 921608 | tf_op jit(solution)/shard_map/ppermute | solution.py:39
  4.9 13.7 %collective-permute-start.3 = (bf16[1200,128]{1,0:T(8,128)(2,1)S(1)}, bf16[1200,128]{1,0:T(8,128)(2,1)S(1)}, u32[]{:S(2)}, u32[]{:S(2)}) collective-permute-start(bf16[1200,128]{1,0:T(8,128)(2,1)S(1)} %get-tuple-element.31), channel_id=1, source_target_pairs={{0,12},{2,14},{4,8},{6,10},{8,4},{10,6},{12,0},{14,2},{16,28},{18,... | collective-permute-start | bytes 921608 | tf_op jit(solution)/shard_map/ppermute | solution.py:39
  6.0 7.5 %collective-permute-start.2 = (bf16[112,1280]{1,0:T(8,128)(2,1)S(1)}, bf16[112,1280]{1,0:T(8,128)(2,1)S(1)}, u32[]{:S(2)}, u32[]{:S(2)}) collective-permute-start(bf16[112,1280]{1,0:T(8,128)(2,1)S(1)} %get-tuple-element.30.own_ref.own_part_ref.here_ref), channel_id=1, source_target_pairs={{0,1},{1,0},{2,3},{3,2},{4,5},{5,4},{6,7},{7,6},{8,9},{9,8},{10,11... | collective-permute-start | bytes 860168 | tf_op jit(solution)/shard_map/ppermute | solution.py:749
  7.3 7.1 %collective-permute-start.1 = (bf16[256,64]{1,0:T(8,128)(2,1)S(1)}, bf16[256,64]{1,0:T(8,128)(2,1)S(1)}, u32[]{:S(2)}, u32[]{:S(2)}) collective-permute-start(bf16[256,64]{1,0:T(8,128)(2,1)S(1)} %get-tuple-element.29.mine_ref), channel_id=1, source_target_pairs={{0,2},{2,0},{4,6},{6,4},{8,10},{10,8},{12,14},{14,12},{16,18},{18,... | collective-permute-start | bytes 98312 | tf_op jit(solution)/shard_map/ppermute | solution.py:39
  14.4 5.4 %collective-permute-start.7 = (bf16[1200,128]{1,0:T(8,128)(2,1)S(1)}, bf16[1200,128]{1,0:T(8,128)(2,1)S(1)}, u32[]{:S(2)}, u32[]{:S(2)}) collective-permute-start(bf16[1200,128]{1,0:T(8,128)(2,1)S(1)} %after.5.refs_3_), channel_id=1, source_target_pairs={{0,2},{2,0},{4,6},{6,4},{8,10},{10,8},{12,14},{14,12},{16,18},{18,... | collective-permute-start | bytes 921608 | tf_op jit(solution)/shard_map/ppermute | solution.py:39
  16.3 3.5 %collective-permute-start.5 = (bf16[1200,128]{1,0:T(8,128)(2,1)S(1)}, bf16[1200,128]{1,0:T(8,128)(2,1)S(1)}, u32[]{:S(2)}, u32[]{:S(2)}) collective-permute-start(bf16[1200,128]{1,0:T(8,128)(2,1)S(1)} %after.4.refs_1_), channel_id=1, source_target_pairs={{0,2},{2,0},{4,6},{6,4},{8,10},{10,8},{12,14},{14,12},{16,18},{18,... | collective-permute-start | bytes 921608 | tf_op jit(solution)/shard_map/ppermute | solution.py:39
  18.6 2.4 %collective-permute-start.8 = (bf16[1200,128]{1,0:T(8,128)(2,1)S(1)}, bf16[1200,128]{1,0:T(8,128)(2,1)S(1)}, u32[]{:S(2)}, u32[]{:S(2)}) collective-permute-start(bf16[1200,128]{1,0:T(8,128)(2,1)S(1)} %after.3.refs_0_), channel_id=1, source_target_pairs={{0,2},{2,0},{4,6},{6,4},{8,10},{10,8},{12,14},{14,12},{16,18},{18,... | collective-permute-start | bytes 921608 | tf_op jit(solution)/shard_map/ppermute | solution.py:39
  20.8 7.1 %copy-start.5 = (f32[2560]{0:T(1024)S(1)}, f32[2560]{0:T(1024)}, u32[]{:S(2)}) copy-start(f32[2560]{0:T(1024)} %param.22) | copy-start | bytes 30724
  20.8 7.1 %copy-start.7 = (f32[1280]{0:T(1024)S(1)}, f32[1280]{0:T(1024)}, u32[]{:S(2)}) copy-start(f32[1280]{0:T(1024)} %param.20) | copy-start | bytes 15364
  20.8 7.1 %copy-start.8 = (s32[8,3]{0,1:T(4,128)S(1)}, s32[8,3]{0,1:T(4,128)}, u32[]{:S(2)}) copy-start(s32[8,3]{0,1:T(4,128)} %param.13) | copy-start | bytes 292
  20.9 7.2 %copy-start.3 = (f32[2,1280]{1,0:T(2,128)S(1)}, f32[2,1280]{1,0:T(2,128)}, u32[]{:S(2)}) copy-start(f32[2,1280]{1,0:T(2,128)} %gain_ref.1) | copy-start | bytes 30724
  20.9 7.2 %copy-start.4 = (s32[16]{0:T(128)S(1)}, s32[16]{0:T(128)}, u32[]{:S(2)}) copy-start(s32[16]{0:T(128)} %counts_ref.5) | copy-start | bytes 196
  21.5 10.3 %collective-permute-start.10 = (bf16[64,1024]{1,0:T(8,128)(2,1)S(1)}, bf16[64,1024]{1,0:T(8,128)(2,1)S(1)}, u32[]{:S(2)}, u32[]{:S(2)}) collective-permute-start(bf16[64,1024]{1,0:T(8,128)(2,1)S(1)} %get-tuple-element.37), channel_id=1, source_target_pairs={{0,16},{2,20},{4,18},{6,22},{8,24},{10,28},{12,26},{14,30},{16,0},... | collective-permute-start | bytes 393224 | tf_op jit(solution)/shard_map/ppermute | solution.py:780
  22.8 9.0 %collective-permute-start.11 = (bf16[64,1024]{1,0:T(8,128)(2,1)S(1)}, bf16[64,1024]{1,0:T(8,128)(2,1)S(1)}, u32[]{:S(2)}, u32[]{:S(2)}) collective-permute-start(bf16[64,1024]{1,0:T(8,128)(2,1)S(1)} %get-tuple-element.38), channel_id=1, source_target_pairs={{0,14},{2,10},{4,12},{6,8},{8,6},{10,2},{12,4},{14,0},{16,30},{18,... | collective-permute-start | bytes 393224 | tf_op jit(solution)/shard_map/ppermute | solution.py:780
  24.1 7.7 %collective-permute-start.12 = (bf16[64,1024]{1,0:T(8,128)(2,1)S(1)}, bf16[64,1024]{1,0:T(8,128)(2,1)S(1)}, u32[]{:S(2)}, u32[]{:S(2)}) collective-permute-start(bf16[64,1024]{1,0:T(8,128)(2,1)S(1)} %get-tuple-element.34.ready_ref), channel_id=1, source_target_pairs={{0,0},{2,4},{4,2},{6,6},{8,8},{10,12},{12,10},{14,14},{16,16},{18,... | collective-permute-start | bytes 393224 | tf_op jit(solution)/shard_map/ppermute | solution.py:780
  26.6 10.6 %collective-permute-start.9 = (bf16[64,1024]{1,0:T(8,128)(2,1)S(1)}, bf16[64,1024]{1,0:T(8,128)(2,1)S(1)}, u32[]{:S(2)}, u32[]{:S(2)}) collective-permute-start(bf16[64,1024]{1,0:T(8,128)(2,1)S(1)} %get-tuple-element.36), channel_id=1, source_target_pairs={{0,30},{2,26},{4,28},{6,24},{8,22},{10,18},{12,20},{14,16},{16,14}... | collective-permute-start | bytes 393224 | tf_op jit(solution)/shard_map/ppermute | solution.py:780
  37.7 2.2 %collective-permute-start.13 = (bf16[2,72,1152]{2,1,0:T(8,128)(2,1)S(1)}, bf16[2,72,1152]{2,1,0:T(8,128)(2,1)S(1)}, u32[]{:S(2)}, u32[]{:S(2)}) collective-permute-start(bf16[2,72,1152]{2,1,0:T(8,128)(2,1)S(1)} %get-tuple-element.40.mine_ref), channel_id=1, source_target_pairs={{0,2},{2,0},{4,6},{6,4},{8,10},{10,8},{12,14},{14,12},{16,18},{18,... | collective-permute-start | bytes 995336 | tf_op jit(solution)/shard_map/ppermute | solution.py:39
  38.2 4.0 %collective-permute-start.14 = (bf16[72,128]{1,0:T(8,128)(2,1)S(1)}, bf16[72,128]{1,0:T(8,128)(2,1)S(1)}, u32[]{:S(2)}, u32[]{:S(2)}) collective-permute-start(bf16[72,128]{1,0:T(8,128)(2,1)S(1)} %get-tuple-element.50), channel_id=1, source_target_pairs={{0,1},{1,0},{2,3},{3,2},{4,5},{5,4},{6,7},{7,6},{8,9},{9,8},{10,11... | collective-permute-start | bytes 55304 | tf_op jit(solution)/shard_map/ppermute | solution.py:802
  39.5 3.2 %collective-permute-start.15 = (bf16[72,128]{1,0:T(8,128)(2,1)S(1)}, bf16[72,128]{1,0:T(8,128)(2,1)S(1)}, u32[]{:S(2)}, u32[]{:S(2)}) collective-permute-start(bf16[72,128]{1,0:T(8,128)(2,1)S(1)} %get-tuple-element.50), channel_id=1, source_target_pairs={{0,3},{1,2},{2,1},{3,0},{4,7},{5,6},{6,5},{7,4},{8,11},{9,10},{10,... | collective-permute-start | bytes 55304 | tf_op jit(solution)/shard_map/ppermute | solution.py:803
  (1 other events, 5.9 us)

commit v3 on v2

--- a/solution.py
+++ b/solution.py
@@ -189,7 +189,7 @@
 
 
 def modulated_kernel(
-    clips_sent, span, own_ref, other_ref, own_part_ref, other_part_ref, rows_ref, part
+    clips_sent, span, own_ref, other_ref, own_part_ref, other_part_ref, rows_ref, rest_ref, part
 ):
     place = lax.axis_index("seq")
     rest, core = lax.div(place, 4), lax.rem(place, 2)
@@ -224,16 +224,17 @@
         scale = 1.0 + jnp.sum(jnp.where(row[:8] == first + 1, eight, 0.0), axis=0, keepdims=True)
         patch_rows = centred * scale
         extra = jnp.where(row == 0, centred_bias * scale, jnp.where(row == 1, shift, 0.0))
-        rows_ref[pl.ds(flip * STEP, 64)] = patch_rows.astype(BF16)
-        rows_ref[pl.ds(flip * STEP + 64, STEP - 64)] = extra.astype(BF16)
+        for start, values in ((0, patch_rows), (64, extra)):
+            here = pl.ds(flip * STEP + start, values.shape[0])
+            rows_ref[here], rest_ref[here] = exact_pieces(values, 2)
 
 
 def modulated_rows(own, other, own_part, other_part, clips_sent, span):
     return pl.pallas_call(
         functools.partial(modulated_kernel, clips_sent, span),
-        out_shape=jax.ShapeDtypeStruct((clips_sent * STEP, own_part.shape[1]), BF16),
+        out_shape=[jax.ShapeDtypeStruct((clips_sent * STEP, own_part.shape[1]), BF16)] * 2,
         in_specs=[vmem()] * 4,
-        out_specs=vmem(),
+        out_specs=[vmem()] * 2,
         scratch_shapes=[pltpu.VMEM((72 + (own.shape[0] - 80) // 2, own_part.shape[1]), F32)],
         compiler_params=params(),
         name="modulated_rows",
@@ -260,33 +261,35 @@
     yield jnp.concatenate(parts, axis=0)
 
 
-def piece_products(rows_here, refs, rows):
+def piece_products(rows_here, rest_here, refs, rows):
     chunks = list(piece_chunks(refs, rows))
     for chunk in range(0, len(chunks), 2):
         block = jnp.concatenate(chunks[chunk : chunk + 2], axis=1)
-        yield chunk, jnp.dot(rows_here, block, preferred_element_type=F32)
-
-
-def early_kernel(order, rows, rows_ref, *refs):
+        total = jnp.dot(rows_here, block, preferred_element_type=F32)
+        yield chunk, total + jnp.dot(rest_here, block, preferred_element_type=F32)
+
+
+def early_kernel(order, rows, rows_ref, rest_ref, *refs):
     out_ref = refs[-1]
     refs = [refs[order.index(block)] for block in sorted(order)]
-    for chunk, total in piece_products(rows_ref[:, 0 : len(refs) * rows], refs, rows):
+    used = len(refs) * rows
+    for chunk, total in piece_products(rows_ref[:, :used], rest_ref[:, :used], refs, rows):
         out_ref[:, pl.ds(chunk * HD, 2 * HD)] = total
 
 
-def early_rows(rows_here, pieces, rows):
+def early_rows(rows_here, rest_here, pieces, rows):
     wide = (pieces[0].shape[0] // rows + 1) * HD
     return pl.pallas_call(
         functools.partial(early_kernel, list(pieces), rows),
         out_shape=jax.ShapeDtypeStruct((rows_here.shape[0], wide), F32),
-        in_specs=[vmem()] * (1 + len(pieces)),
+        in_specs=[vmem()] * (2 + len(pieces)),
         out_specs=vmem(),
         compiler_params=params(),
         name="early_rows",
-    )(rows_here, *pieces.values())
-
-
-def product_kernel(clips_sent, order, rows, rows_ref, early_ref, *refs):
+    )(rows_here, rest_here, *pieces.values())
+
+
+def product_kernel(clips_sent, order, rows, rows_ref, rest_ref, early_ref, *refs):
     refs, out_refs = refs[: len(order)], refs[len(order) :]
     refs = [refs[order.index(block)] for block in sorted(order)]
     done = rows_ref.shape[1] - len(order) * rows
@@ -296,7 +299,9 @@
     row = lax.broadcasted_iota(jnp.int32, (8, HD), 0)
     odd = lax.rem(chip_block(), 2)
     ends = [[] for _ in range(clips_sent)]
-    for first_chunk, total in piece_products(rows_ref[:, done:], refs, rows):
+    for first_chunk, total in piece_products(
+        rows_ref[:, done:], rest_ref[:, done:], refs, rows
+    ):
         start = first_chunk * HD
         columns = pl.ds(start, tile)
         total = total + early_ref[:, columns]
@@ -321,15 +326,15 @@
             out_refs[flip][:, columns] = patch_rows.astype(BF16)
 
 
-def product_rows(rows_here, early, pieces, clips_sent, rows):
+def product_rows(rows_here, rest_here, early, pieces, clips_sent, rows):
     return pl.pallas_call(
         functools.partial(product_kernel, clips_sent, list(pieces), rows),
         out_shape=[jax.ShapeDtypeStruct((64, early.shape[1]), BF16)] * clips_sent,
-        in_specs=[vmem()] * (2 + len(pieces)),
+        in_specs=[vmem()] * (3 + len(pieces)),
         out_specs=[vmem()] * clips_sent,
         compiler_params=params(),
         name="product_rows",
-    )(rows_here, early, *pieces.values())
+    )(rows_here, rest_here, early, *pieces.values())
 
 
 def split_ends(ends, row):
@@ -759,7 +764,7 @@
         )
         return values.reshape(-1, 8 * padded)
 
-    rows_here = modulated_rows(
+    rows_here, rest_here = modulated_rows(
         own, other, group_part(own), group_part(other), clips_sent, span
     )
     placed = {0: packed[0], 1: first_swapped}
@@ -767,9 +772,9 @@
         piece = after(pieces[flip], rows_here, other_patches)
         placed[2 * flip], placed[2 * flip + 1] = piece, swap_bits(piece, 1)
     first = {order: placed.pop(order) for order in (6, 4, 5, 2, 3, 0, 1)}
-    early = early_rows(rows_here, first, padded)
-
-    products = product_rows(rows_here, early, placed, clips_sent, padded)
+    early = early_rows(rows_here, rest_here, first, padded)
+
+    products = product_rows(rows_here, rest_here, early, placed, clips_sent, padded)
     arrived = {}
     for flip in reversed(range(clips_sent)):
         pairs = []

time: 46.2 us -> 47.1 us (1.019)
  Pallas kernels: 13.8 us -> 15 us
  waiting for transfers between devices: 13.3 us -> 12.5 us
    pallas_call x1, Pallas kernels: 1.02 us -> 1.87 us  [early_rows(): pl.pallas_call(functools.partial(early_kernel, list(pieces), rows), out_s...]
  transfers between devices with their start and end apart: 16 -> 16, of which waited for: 5 -> 4; matrix products, arithmetic and copies ran while one was open for 2% -> 2% of each run, Pallas kernels for 17% -> 19%
where the time goes in v3:
time: 47.1 us; the launch traced here: 46.9 us
  starting transfers between devices  18 us (38%)
  Pallas kernels  15 us (32%)
  waiting for transfers between devices  12.5 us (27%)
  local copies, waits for them, and re-layouts  1.02 us (2%)
    ppermute x9, starting transfers between devices, swap_bits(): lax.ppermute(value, 'seq', [(source, source ^ mask) for source in range(c...  8.62 us
    ppermute x4, starting transfers between devices, shards(): arrived[flip] = lax.ppermute(products[flip], 'seq', pairs)  6.41 us
    ppermute x4, waiting for transfers between devices, shards(): arrived[flip] = lax.ppermute(products[flip], 'seq', pairs)  5.05 us
    ppermute x1, waiting for transfers between devices, shards(): lax.ppermute(own, 'mp', [(i, (i + 1) % halves) for i in range(halves)])  5.04 us
    pallas_call x1, Pallas kernels, spread_rows(): pl.pallas_call(spread_kernel, out_shape=[jax.ShapeDtypeStruct((2 * tokens...  3.74 us
    pallas_call x1, Pallas kernels, attend_rows(): pl.pallas_call(functools.partial(attend_kernel, heads_here), out_shape=ja...  3.31 us
    pallas_call x1, Pallas kernels, heads_rows(): pl.pallas_call(functools.partial(heads_kernel, heads_here), out_shape=[ja...  2.26 us
    ppermute x9, waiting for transfers between devices, swap_bits(): lax.ppermute(value, 'seq', [(source, source ^ mask) for source in range(c...  2.03 us
  transfers between devices with their start and end apart: 16, of which 4 were waited for; matrix products, arithmetic and copies ran while one was open for 2% of the time, Pallas kernels for 19%

profile of v3, /device:TPU:17, one launch (start us, length us, event | category | flops | bytes accessed | tf_op | source)
XLA Modules:
  0.0 46.9 jit_solution(12944799077652679371)
XLA Ops:
  0.0 1.5 %pack_weights.1 = (bf16[1200,128]{1,0:T(8,128)(2,1)S(1)}, bf16[1200,128]{1,0:T(8,128)(2,1)S(1)}, bf16[1200,128]{1,0:T(8,128)(2,1)S(1)}, bf16[1200,128]{1,0:T(8,128)(2,1)S(1)}) custom-call(bf16[160,1280]{1,0:T(8,128)(2,1)} %wq_ref.1, bf16[160,2560]{1,0:T(8,128)(2,1)} %wkv_ref.1), custom_call_target="tpu_custom_call" | custom-call | tf_op jit(solution)/shard_map/pack_weights/pallas_call | solution.py:166
  1.6 0.7 %collective-permute-start = (bf16[1200,128]{1,0:T(8,128)(2,1)S(1)}, bf16[1200,128]{1,0:T(8,128)(2,1)S(1)}, u32[]{:S(2)}, u32[]{:S(2)}) collective-permute-start(bf16[1200,128]{1,0:T(8,128)(2,1)S(1)} %get-tuple-element.30.refs_5_), channel_id=1, source_target_pairs={{0,2},{2,0},{4,6},{6,4},{8,10},{10,8},{12,14},{14,12},{16,18},{18,... | collective-permute-start | bytes 921608 | tf_op jit(solution)/shard_map/ppermute | solution.py:39
  2.3 1.2 %collective-permute-start.6 = (bf16[1200,128]{1,0:T(8,128)(2,1)S(1)}, bf16[1200,128]{1,0:T(8,128)(2,1)S(1)}, u32[]{:S(2)}, u32[]{:S(2)}) collective-permute-start(bf16[1200,128]{1,0:T(8,128)(2,1)S(1)} %get-tuple-element.37), channel_id=1, source_target_pairs={{0,4},{2,6},{4,0},{6,2},{8,12},{10,14},{12,8},{14,10},{16,20},{18,... | collective-permute-start | bytes 921608 | tf_op jit(solution)/shard_map/ppermute | solution.py:39
  3.6 1.3 %collective-permute-start.4 = (bf16[1200,128]{1,0:T(8,128)(2,1)S(1)}, bf16[1200,128]{1,0:T(8,128)(2,1)S(1)}, u32[]{:S(2)}, u32[]{:S(2)}) collective-permute-start(bf16[1200,128]{1,0:T(8,128)(2,1)S(1)} %get-tuple-element.36), channel_id=1, source_target_pairs={{0,8},{2,10},{4,12},{6,14},{8,0},{10,2},{12,4},{14,6},{16,24},{18,... | collective-permute-start | bytes 921608 | tf_op jit(solution)/shard_map/ppermute | solution.py:39
  5.0 0.9 %copy.16.patches_ref = bf16[256,64]{1,0:T(8,128)(2,1)S(1)} copy(bf16[256,64]{0,1:T(8,128)(2,1)} %param.12) | data formatting | bytes 65536 | tf_op args[0]
  6.0 1.3 %collective-permute-start.2 = (bf16[112,1280]{1,0:T(8,128)(2,1)S(1)}, bf16[112,1280]{1,0:T(8,128)(2,1)S(1)}, u32[]{:S(2)}, u32[]{:S(2)}) collective-permute-start(bf16[112,1280]{1,0:T(8,128)(2,1)S(1)} %get-tuple-element.32.own_ref.own_part_ref.here_ref), channel_id=1, source_target_pairs={{0,1},{1,0},{2,3},{3,2},{4,5},{5,4},{6,7},{7,6},{8,9},{9,8},{10,11... | collective-permute-start | bytes 860168 | tf_op jit(solution)/shard_map/ppermute | solution.py:754
  7.3 1.2 %collective-permute-start.1 = (bf16[256,64]{1,0:T(8,128)(2,1)S(1)}, bf16[256,64]{1,0:T(8,128)(2,1)S(1)}, u32[]{:S(2)}, u32[]{:S(2)}) collective-permute-start(bf16[256,64]{1,0:T(8,128)(2,1)S(1)} %get-tuple-element.31.mine_ref), channel_id=1, source_target_pairs={{0,2},{2,0},{4,6},{6,4},{8,10},{10,8},{12,14},{14,12},{16,18},{18,... | collective-permute-start | bytes 98312 | tf_op jit(solution)/shard_map/ppermute | solution.py:39
  8.5 5.0 %collective-permute-done.2.other_ref.other_part_ref.there_ref = bf16[112,1280]{1,0:T(8,128)(2,1)S(1)} collective-permute-done((bf16[112,1280]{1,0:T(8,128)(2,1)S(1)}, bf16[112,1280]{1,0:T(8,128)(2,1)S(1)}, u32[]{:S(2)}, u32[]{:S(2)}) %collective-permute-start.2) | collective-permute-done | bytes 286752 | tf_op jit(solution)/shard_map/ppermute | solution.py:754
  13.5 1.1 %modulated_rows.1 = (bf16[320,1280]{1,0:T(8,128)(2,1)S(1)}, bf16[320,1280]{1,0:T(8,128)(2,1)S(1)}) custom-call(bf16[112,1280]{1,0:T(8,128)(2,1)S(1)} %get-tuple-element.32.own_ref.own_part_ref.here_ref, bf16[112,1280]{1,0:T(8,128)(2,1)S(1)} %collective-permute-done.2.other_ref.other_part_ref.there_ref, ...), custom_call_target="tpu_custom_call" | custom-call | tf_op jit(solution)/shard_map/modulated_rows/pallas_call | solution.py:233
  14.6 1.9 %collective-permute-start.7 = (bf16[1200,128]{1,0:T(8,128)(2,1)S(1)}, bf16[1200,128]{1,0:T(8,128)(2,1)S(1)}, u32[]{:S(2)}, u32[]{:S(2)}) collective-permute-start(bf16[1200,128]{1,0:T(8,128)(2,1)S(1)} %after.5.refs_3_), channel_id=1, source_target_pairs={{0,2},{2,0},{4,6},{6,4},{8,10},{10,8},{12,14},{14,12},{16,18},{18,... | collective-permute-start | bytes 921608 | tf_op jit(solution)/shard_map/ppermute | solution.py:39
  16.6 2.0 %collective-permute-done.3.refs_0_ = bf16[1200,128]{1,0:T(8,128)(2,1)S(1)} collective-permute-done((bf16[1200,128]{1,0:T(8,128)(2,1)S(1)}, bf16[1200,128]{1,0:T(8,128)(2,1)S(1)}, u32[]{:S(2)}, u32[]{:S(2)}) %collective-permute-start.3) | collective-permute-done | bytes 307232 | tf_op jit(solution)/shard_map/ppermute | solution.py:39
  18.6 1.2 %collective-permute-start.8 = (bf16[1200,128]{1,0:T(8,128)(2,1)S(1)}, bf16[1200,128]{1,0:T(8,128)(2,1)S(1)}, u32[]{:S(2)}, u32[]{:S(2)}) collective-permute-start(bf16[1200,128]{1,0:T(8,128)(2,1)S(1)} %after.3.refs_0_), channel_id=1, source_target_pairs={{0,2},{2,0},{4,6},{6,4},{8,10},{10,8},{12,14},{14,12},{16,18},{18,... | collective-permute-start | bytes 921608 | tf_op jit(solution)/shard_map/ppermute | solution.py:39
  19.8 1.9 %early_rows.1.early_ref = f32[320,1024]{1,0:T(8,128)S(1)} custom-call(bf16[320,1280]{1,0:T(8,128)(2,1)S(1)} %get-tuple-element.33.refs_1_.rows_ref, bf16[320,1280]{1,0:T(8,128)(2,1)S(1)} %get-tuple-element.34.rest_ref, bf16[1200,128]{1,0:T(8,128)(2,1)S(1)} %after.3.refs_0_, bf16[1200,128]{1,0:T(8,128)(2,1)S(1)} %after.4.refs_1_, ...), custom_call_target="tpu_custom_call" | custom-call | tf_op jit(solution)/shard_map/early_rows/pallas_call | solution.py:282
  21.7 0.6 %product_rows.1 = (bf16[64,1024]{1,0:T(8,128)(2,1)S(1)}, bf16[64,1024]{1,0:T(8,128)(2,1)S(1)}, bf16[64,1024]{1,0:T(8,128)(2,1)S(1)}, bf16[64,1024]{1,0:T(8,128)(2,1)S(1)}) custom-call(bf16[320,1280]{1,0:T(8,128)(2,1)S(1)} %get-tuple-element.33.refs_1_.rows_ref, bf16[320,1280]{1,0:T(8,128)(2,1)S(1)} %get-tuple-element.34.rest_ref, ...), custom_call_target="tpu_custom_call" | custom-call | tf_op jit(solution)/shard_map/product_rows/pallas_call | solution.py:330
  22.4 1.0 %collective-permute-start.10 = (bf16[64,1024]{1,0:T(8,128)(2,1)S(1)}, bf16[64,1024]{1,0:T(8,128)(2,1)S(1)}, u32[]{:S(2)}, u32[]{:S(2)}) collective-permute-start(bf16[64,1024]{1,0:T(8,128)(2,1)S(1)} %get-tuple-element.41), channel_id=1, source_target_pairs={{0,16},{2,20},{4,18},{6,22},{8,24},{10,28},{12,26},{14,30},{16,0},... | collective-permute-start | bytes 393224 | tf_op jit(solution)/shard_map/ppermute | solution.py:785
  23.3 1.3 %collective-permute-start.11 = (bf16[64,1024]{1,0:T(8,128)(2,1)S(1)}, bf16[64,1024]{1,0:T(8,128)(2,1)S(1)}, u32[]{:S(2)}, u32[]{:S(2)}) collective-permute-start(bf16[64,1024]{1,0:T(8,128)(2,1)S(1)} %get-tuple-element.42), channel_id=1, source_target_pairs={{0,14},{2,10},{4,12},{6,8},{8,6},{10,2},{12,4},{14,0},{16,30},{18,... | collective-permute-start | bytes 393224 | tf_op jit(solution)/shard_map/ppermute | solution.py:785
  24.6 2.8 %collective-permute-start.12 = (bf16[64,1024]{1,0:T(8,128)(2,1)S(1)}, bf16[64,1024]{1,0:T(8,128)(2,1)S(1)}, u32[]{:S(2)}, u32[]{:S(2)}) collective-permute-start(bf16[64,1024]{1,0:T(8,128)(2,1)S(1)} %get-tuple-element.38.ready_ref), channel_id=1, source_target_pairs={{0,0},{2,4},{4,2},{6,6},{8,8},{10,12},{12,10},{14,14},{16,16},{18,... | collective-permute-start | bytes 393224 | tf_op jit(solution)/shard_map/ppermute | solution.py:785
  27.5 1.3 %collective-permute-start.9 = (bf16[64,1024]{1,0:T(8,128)(2,1)S(1)}, bf16[64,1024]{1,0:T(8,128)(2,1)S(1)}, u32[]{:S(2)}, u32[]{:S(2)}) collective-permute-start(bf16[64,1024]{1,0:T(8,128)(2,1)S(1)} %get-tuple-element.40), channel_id=1, source_target_pairs={{0,30},{2,26},{4,28},{6,24},{8,22},{10,18},{12,20},{14,16},{16,14}... | collective-permute-start | bytes 393224 | tf_op jit(solution)/shard_map/ppermute | solution.py:785
  28.9 3.7 %spread_rows.1 = (bf16[512,128]{1,0:T(8,128)(2,1)S(1)}, bf16[128,512]{1,0:T(8,128)(2,1)S(1)}, f32[512,128]{1,0:T(8,128)S(1)}, f32[512,128]{1,0:T(8,128)S(1)}, f3...) custom-call(s32[8,3]{1,0:T(8,128)S(1)} %copy.17.shape_ref, s32[16]{0:T(128)S(1)} %copy-done.4, ...), custom_call_target="tpu_custom_call" | custom-call | tf_op jit(solution)/shard_map/spread_rows/pallas_call | solution.py:544
  32.7 5.0 %collective-permute-done.9.refs_0_ = bf16[64,1024]{1,0:T(8,128)(2,1)S(1)} collective-permute-done((bf16[64,1024]{1,0:T(8,128)(2,1)S(1)}, bf16[64,1024]{1,0:T(8,128)(2,1)S(1)}, u32[]{:S(2)}, u32[]{:S(2)}) %collective-permute-start.9) | collective-permute-done | bytes 131104 | tf_op jit(solution)/shard_map/ppermute | solution.py:785
  38.3 0.9 %collective-permute-start.13 = (bf16[2,72,1152]{2,1,0:T(8,128)(2,1)S(1)}, bf16[2,72,1152]{2,1,0:T(8,128)(2,1)S(1)}, u32[]{:S(2)}, u32[]{:S(2)}) collective-permute-start(bf16[2,72,1152]{2,1,0:T(8,128)(2,1)S(1)} %get-tuple-element.44.mine_ref), channel_id=1, source_target_pairs={{0,2},{2,0},{4,6},{6,4},{8,10},{10,8},{12,14},{14,12},{16,18},{18,... | collective-permute-start | bytes 995336 | tf_op jit(solution)/shard_map/ppermute | solution.py:39
  39.1 1.2 %collective-permute-start.14 = (bf16[72,128]{1,0:T(8,128)(2,1)S(1)}, bf16[72,128]{1,0:T(8,128)(2,1)S(1)}, u32[]{:S(2)}, u32[]{:S(2)}) collective-permute-start(bf16[72,128]{1,0:T(8,128)(2,1)S(1)} %get-tuple-element.54), channel_id=1, source_target_pairs={{0,1},{1,0},{2,3},{3,2},{4,5},{5,4},{6,7},{7,6},{8,9},{9,8},{10,11... | collective-permute-start | bytes 55304 | tf_op jit(solution)/shard_map/ppermute | solution.py:807
  40.9 2.3 %heads_rows.1 = (f32[256,1280]{1,0:T(8,128)S(1)}, bf16[512,1280]{1,0:T(8,128)(2,1)S(1)}, bf16[512,1280]{1,0:T(8,128)(2,1)S(1)}) custom-call(s32[16]{0:T(128)S(1)} %copy-done.4, bf16[512,128]{1,0:T(8,128)(2,1)S(1)} %get-tuple-element.39.refs_5_.left_ref, bf16[2,72,1152]{2,1,0:T(8,128)(2,1)S(1)} %get-tuple-element.44.mine_ref, ...), custom_call_target="tpu_custom_call" | custom-call | tf_op jit(solution)/shard_map/heads_rows/pallas_call | solution.py:627
  43.6 3.3 %attend_rows.1 = bf16[256,1280]{1,0:T(8,128)(2,1)} custom-call(s32[16]{0:T(128)S(1)} %copy-done.4, f32[256,1280]{1,0:T(8,128)S(1)} %get-tuple-element.49.q_ref, bf16[512,1280]{1,0:T(8,128)(2,1)S(1)} %get-tuple-element.50.k_ref, bf16[512,1280]{1,0:T(8,128)(2,1)S(1)} %get-tuple-element.51.v_ref, bf16[512,128]{1,0:T(8,128)(2,1)S(1)} %get-tuple-element.39.refs_5_.left_ref, ...), custom_call_target="tpu_custom_call" | custom-call | tf_op jit(solution)/shard_map/attend_rows/pallas_call | solution.py:705
  (43 shorter events, 1.9 us)
Async XLA Ops:
  0.0 5.9 %copy-start = (bf16[64,1280]{1,0:T(8,128)(2,1)S(1)}, bf16[64,1280]{1,0:T(8,128)(2,1)}, u32[]{:S(2)}) copy-start(bf16[64,1280]{1,0:T(8,128)(2,1)} %weight_ref.1) | copy-start | bytes 491524
  0.0 5.9 %copy-start.1 = (f32[8,2,1280]{2,1,0:T(2,128)S(1)}, f32[8,2,1280]{2,1,0:T(2,128)}, u32[]{:S(2)}) copy-start(f32[8,2,1280]{2,1,0:T(2,128)} %time_ref.1) | copy-start | bytes 245764
  0.0 5.9 %copy-start.2 = (f32[2,1280]{1,0:T(2,128)S(1)}, f32[2,1280]{1,0:T(2,128)}, u32[]{:S(2)}) copy-start(f32[2,1280]{1,0:T(2,128)} %block_ref.1) | copy-start | bytes 30724
  1.6 4.3 %collective-permute-start = (bf16[1200,128]{1,0:T(8,128)(2,1)S(1)}, bf16[1200,128]{1,0:T(8,128)(2,1)S(1)}, u32[]{:S(2)}, u32[]{:S(2)}) collective-permute-start(bf16[1200,128]{1,0:T(8,128)(2,1)S(1)} %get-tuple-element.30.refs_5_), channel_id=1, source_target_pairs={{0,2},{2,0},{4,6},{6,4},{8,10},{10,8},{12,14},{14,12},{16,18},{18,... | collective-permute-start | bytes 921608 | tf_op jit(solution)/shard_map/ppermute | solution.py:39
  2.3 12.3 %collective-permute-start.6 = (bf16[1200,128]{1,0:T(8,128)(2,1)S(1)}, bf16[1200,128]{1,0:T(8,128)(2,1)S(1)}, u32[]{:S(2)}, u32[]{:S(2)}) collective-permute-start(bf16[1200,128]{1,0:T(8,128)(2,1)S(1)} %get-tuple-element.37), channel_id=1, source_target_pairs={{0,4},{2,6},{4,0},{6,2},{8,12},{10,14},{12,8},{14,10},{16,20},{18,... | collective-permute-start | bytes 921608 | tf_op jit(solution)/shard_map/ppermute | solution.py:39
  3.6 12.9 %collective-permute-start.4 = (bf16[1200,128]{1,0:T(8,128)(2,1)S(1)}, bf16[1200,128]{1,0:T(8,128)(2,1)S(1)}, u32[]{:S(2)}, u32[]{:S(2)}) collective-permute-start(bf16[1200,128]{1,0:T(8,128)(2,1)S(1)} %get-tuple-element.36), channel_id=1, source_target_pairs={{0,8},{2,10},{4,12},{6,14},{8,0},{10,2},{12,4},{14,6},{16,24},{18,... | collective-permute-start | bytes 921608 | tf_op jit(solution)/shard_map/ppermute | solution.py:39
  4.9 13.7 %collective-permute-start.3 = (bf16[1200,128]{1,0:T(8,128)(2,1)S(1)}, bf16[1200,128]{1,0:T(8,128)(2,1)S(1)}, u32[]{:S(2)}, u32[]{:S(2)}) collective-permute-start(bf16[1200,128]{1,0:T(8,128)(2,1)S(1)} %get-tuple-element.35), channel_id=1, source_target_pairs={{0,12},{2,14},{4,8},{6,10},{8,4},{10,6},{12,0},{14,2},{16,28},{18,... | collective-permute-start | bytes 921608 | tf_op jit(solution)/shard_map/ppermute | solution.py:39
  6.0 7.5 %collective-permute-start.2 = (bf16[112,1280]{1,0:T(8,128)(2,1)S(1)}, bf16[112,1280]{1,0:T(8,128)(2,1)S(1)}, u32[]{:S(2)}, u32[]{:S(2)}) collective-permute-start(bf16[112,1280]{1,0:T(8,128)(2,1)S(1)} %get-tuple-element.32.own_ref.own_part_ref.here_ref), channel_id=1, source_target_pairs={{0,1},{1,0},{2,3},{3,2},{4,5},{5,4},{6,7},{7,6},{8,9},{9,8},{10,11... | collective-permute-start | bytes 860168 | tf_op jit(solution)/shard_map/ppermute | solution.py:754
  7.3 7.3 %collective-permute-start.1 = (bf16[256,64]{1,0:T(8,128)(2,1)S(1)}, bf16[256,64]{1,0:T(8,128)(2,1)S(1)}, u32[]{:S(2)}, u32[]{:S(2)}) collective-permute-start(bf16[256,64]{1,0:T(8,128)(2,1)S(1)} %get-tuple-element.31.mine_ref), channel_id=1, source_target_pairs={{0,2},{2,0},{4,6},{6,4},{8,10},{10,8},{12,14},{14,12},{16,18},{18,... | collective-permute-start | bytes 98312 | tf_op jit(solution)/shard_map/ppermute | solution.py:39
  14.6 5.2 %collective-permute-start.7 = (bf16[1200,128]{1,0:T(8,128)(2,1)S(1)}, bf16[1200,128]{1,0:T(8,128)(2,1)S(1)}, u32[]{:S(2)}, u32[]{:S(2)}) collective-permute-start(bf16[1200,128]{1,0:T(8,128)(2,1)S(1)} %after.5.refs_3_), channel_id=1, source_target_pairs={{0,2},{2,0},{4,6},{6,4},{8,10},{10,8},{12,14},{14,12},{16,18},{18,... | collective-permute-start | bytes 921608 | tf_op jit(solution)/shard_map/ppermute | solution.py:39
  16.5 3.3 %collective-permute-start.5 = (bf16[1200,128]{1,0:T(8,128)(2,1)S(1)}, bf16[1200,128]{1,0:T(8,128)(2,1)S(1)}, u32[]{:S(2)}, u32[]{:S(2)}) collective-permute-start(bf16[1200,128]{1,0:T(8,128)(2,1)S(1)} %after.4.refs_1_), channel_id=1, source_target_pairs={{0,2},{2,0},{4,6},{6,4},{8,10},{10,8},{12,14},{14,12},{16,18},{18,... | collective-permute-start | bytes 921608 | tf_op jit(solution)/shard_map/ppermute | solution.py:39
  18.6 3.1 %collective-permute-start.8 = (bf16[1200,128]{1,0:T(8,128)(2,1)S(1)}, bf16[1200,128]{1,0:T(8,128)(2,1)S(1)}, u32[]{:S(2)}, u32[]{:S(2)}) collective-permute-start(bf16[1200,128]{1,0:T(8,128)(2,1)S(1)} %after.3.refs_0_), channel_id=1, source_target_pairs={{0,2},{2,0},{4,6},{6,4},{8,10},{10,8},{12,14},{14,12},{16,18},{18,... | collective-permute-start | bytes 921608 | tf_op jit(solution)/shard_map/ppermute | solution.py:39
  21.7 7.1 %copy-start.5 = (f32[2560]{0:T(1024)S(1)}, f32[2560]{0:T(1024)}, u32[]{:S(2)}) copy-start(f32[2560]{0:T(1024)} %param.22) | copy-start | bytes 30724
  21.7 7.1 %copy-start.7 = (f32[1280]{0:T(1024)S(1)}, f32[1280]{0:T(1024)}, u32[]{:S(2)}) copy-start(f32[1280]{0:T(1024)} %param.20) | copy-start | bytes 15364
  21.7 7.1 %copy-start.8 = (s32[8,3]{0,1:T(4,128)S(1)}, s32[8,3]{0,1:T(4,128)}, u32[]{:S(2)}) copy-start(s32[8,3]{0,1:T(4,128)} %param.13) | copy-start | bytes 292
  21.7 7.2 %copy-start.3 = (f32[2,1280]{1,0:T(2,128)S(1)}, f32[2,1280]{1,0:T(2,128)}, u32[]{:S(2)}) copy-start(f32[2,1280]{1,0:T(2,128)} %gain_ref.1) | copy-start | bytes 30724
  21.7 7.2 %copy-start.4 = (s32[16]{0:T(128)S(1)}, s32[16]{0:T(128)}, u32[]{:S(2)}) copy-start(s32[16]{0:T(128)} %counts_ref.5) | copy-start | bytes 196
  22.4 10.3 %collective-permute-start.10 = (bf16[64,1024]{1,0:T(8,128)(2,1)S(1)}, bf16[64,1024]{1,0:T(8,128)(2,1)S(1)}, u32[]{:S(2)}, u32[]{:S(2)}) collective-permute-start(bf16[64,1024]{1,0:T(8,128)(2,1)S(1)} %get-tuple-element.41), channel_id=1, source_target_pairs={{0,16},{2,20},{4,18},{6,22},{8,24},{10,28},{12,26},{14,30},{16,0},... | collective-permute-start | bytes 393224 | tf_op jit(solution)/shard_map/ppermute | solution.py:785
  23.3 9.4 %collective-permute-start.11 = (bf16[64,1024]{1,0:T(8,128)(2,1)S(1)}, bf16[64,1024]{1,0:T(8,128)(2,1)S(1)}, u32[]{:S(2)}, u32[]{:S(2)}) collective-permute-start(bf16[64,1024]{1,0:T(8,128)(2,1)S(1)} %get-tuple-element.42), channel_id=1, source_target_pairs={{0,14},{2,10},{4,12},{6,8},{8,6},{10,2},{12,4},{14,0},{16,30},{18,... | collective-permute-start | bytes 393224 | tf_op jit(solution)/shard_map/ppermute | solution.py:785
  24.6 8.1 %collective-permute-start.12 = (bf16[64,1024]{1,0:T(8,128)(2,1)S(1)}, bf16[64,1024]{1,0:T(8,128)(2,1)S(1)}, u32[]{:S(2)}, u32[]{:S(2)}) collective-permute-start(bf16[64,1024]{1,0:T(8,128)(2,1)S(1)} %get-tuple-element.38.ready_ref), channel_id=1, source_target_pairs={{0,0},{2,4},{4,2},{6,6},{8,8},{10,12},{12,10},{14,14},{16,16},{18,... | collective-permute-start | bytes 393224 | tf_op jit(solution)/shard_map/ppermute | solution.py:785
  27.5 10.3 %collective-permute-start.9 = (bf16[64,1024]{1,0:T(8,128)(2,1)S(1)}, bf16[64,1024]{1,0:T(8,128)(2,1)S(1)}, u32[]{:S(2)}, u32[]{:S(2)}) collective-permute-start(bf16[64,1024]{1,0:T(8,128)(2,1)S(1)} %get-tuple-element.40), channel_id=1, source_target_pairs={{0,30},{2,26},{4,28},{6,24},{8,22},{10,18},{12,20},{14,16},{16,14}... | collective-permute-start | bytes 393224 | tf_op jit(solution)/shard_map/ppermute | solution.py:785
  38.3 2.6 %collective-permute-start.13 = (bf16[2,72,1152]{2,1,0:T(8,128)(2,1)S(1)}, bf16[2,72,1152]{2,1,0:T(8,128)(2,1)S(1)}, u32[]{:S(2)}, u32[]{:S(2)}) collective-permute-start(bf16[2,72,1152]{2,1,0:T(8,128)(2,1)S(1)} %get-tuple-element.44.mine_ref), channel_id=1, source_target_pairs={{0,2},{2,0},{4,6},{6,4},{8,10},{10,8},{12,14},{14,12},{16,18},{18,... | collective-permute-start | bytes 995336 | tf_op jit(solution)/shard_map/ppermute | solution.py:39
  39.1 4.0 %collective-permute-start.14 = (bf16[72,128]{1,0:T(8,128)(2,1)S(1)}, bf16[72,128]{1,0:T(8,128)(2,1)S(1)}, u32[]{:S(2)}, u32[]{:S(2)}) collective-permute-start(bf16[72,128]{1,0:T(8,128)(2,1)S(1)} %get-tuple-element.54), channel_id=1, source_target_pairs={{0,1},{1,0},{2,3},{3,2},{4,5},{5,4},{6,7},{7,6},{8,9},{9,8},{10,11... | collective-permute-start | bytes 55304 | tf_op jit(solution)/shard_map/ppermute | solution.py:807
  40.4 3.2 %collective-permute-start.15 = (bf16[72,128]{1,0:T(8,128)(2,1)S(1)}, bf16[72,128]{1,0:T(8,128)(2,1)S(1)}, u32[]{:S(2)}, u32[]{:S(2)}) collective-permute-start(bf16[72,128]{1,0:T(8,128)(2,1)S(1)} %get-tuple-element.54), channel_id=1, source_target_pairs={{0,3},{1,2},{2,1},{3,0},{4,7},{5,6},{6,5},{7,4},{8,11},{9,10},{10,... | collective-permute-start | bytes 55304 | tf_op jit(solution)/shard_map/ppermute | solution.py:808
  (1 other events, 5.9 us)

commit v4 on v2

--- a/solution.py
+++ b/solution.py
@@ -771,7 +771,7 @@
 
     products = product_rows(rows_here, early, placed, clips_sent, padded)
     arrived = {}
-    for flip in reversed(range(clips_sent)):
+    for flip in [0, *range(2, clips_sent - 1), 1, clips_sent - 1]:
         pairs = []
         for source in range(count):
             rest, second, core = source // 4, source // 2 % 2, source % 2

time: 46.2 us -> 46.2 us (level)
  no operation moved by 1% of the time
where the time goes in v4:
time: 46.2 us; the launch traced here: 46 us
  starting transfers between devices  17.9 us (39%)
  Pallas kernels  13.8 us (30%)
  waiting for transfers between devices  13.1 us (28%)
  local copies, waits for them, and re-layouts  1.02 us (2%)
    ppermute x9, starting transfers between devices, swap_bits(): lax.ppermute(value, 'seq', [(source, source ^ mask) for source in range(c...  8.26 us
    ppermute x4, starting transfers between devices, shards(): arrived[flip] = lax.ppermute(products[flip], 'seq', pairs)  6.63 us
    ppermute x4, waiting for transfers between devices, shards(): arrived[flip] = lax.ppermute(products[flip], 'seq', pairs)  5.2 us
    ppermute x1, waiting for transfers between devices, shards(): lax.ppermute(own, 'mp', [(i, (i + 1) % halves) for i in range(halves)])  5.04 us
    pallas_call x1, Pallas kernels, spread_rows(): pl.pallas_call(spread_kernel, out_shape=[jax.ShapeDtypeStruct((2 * tokens...  3.73 us
    pallas_call x1, Pallas kernels, attend_rows(): pl.pallas_call(functools.partial(attend_kernel, heads_here), out_shape=ja...  3.32 us
    ppermute x9, waiting for transfers between devices, swap_bits(): lax.ppermute(value, 'seq', [(source, source ^ mask) for source in range(c...  2.41 us
    pallas_call x1, Pallas kernels, heads_rows(): pl.pallas_call(functools.partial(heads_kernel, heads_here), out_shape=[ja...  2.26 us
  transfers between devices with their start and end apart: 16, of which 5 were waited for; matrix products, arithmetic and copies ran while one was open for 2% of the time, Pallas kernels for 17%

profile of v4, /device:TPU:17, one launch (start us, length us, event | category | flops | bytes accessed | tf_op | source)
XLA Modules:
  0.0 46.0 jit_solution(3161366319959227500)
XLA Ops:
  0.0 1.5 %pack_weights.1 = (bf16[1200,128]{1,0:T(8,128)(2,1)S(1)}, bf16[1200,128]{1,0:T(8,128)(2,1)S(1)}, bf16[1200,128]{1,0:T(8,128)(2,1)S(1)}, bf16[1200,128]{1,0:T(8,128)(2,1)S(1)}) custom-call(bf16[160,1280]{1,0:T(8,128)(2,1)} %wq_ref.1, bf16[160,2560]{1,0:T(8,128)(2,1)} %wkv_ref.1), custom_call_target="tpu_custom_call" | custom-call | tf_op jit(solution)/shard_map/pack_weights/pallas_call | solution.py:166
  1.6 0.7 %collective-permute-start = (bf16[1200,128]{1,0:T(8,128)(2,1)S(1)}, bf16[1200,128]{1,0:T(8,128)(2,1)S(1)}, u32[]{:S(2)}, u32[]{:S(2)}) collective-permute-start(bf16[1200,128]{1,0:T(8,128)(2,1)S(1)} %get-tuple-element.28.refs_5_), channel_id=1, source_target_pairs={{0,2},{2,0},{4,6},{6,4},{8,10},{10,8},{12,14},{14,12},{16,18},{18,... | collective-permute-start | bytes 921608 | tf_op jit(solution)/shard_map/ppermute | solution.py:39
  2.3 1.2 %collective-permute-start.6 = (bf16[1200,128]{1,0:T(8,128)(2,1)S(1)}, bf16[1200,128]{1,0:T(8,128)(2,1)S(1)}, u32[]{:S(2)}, u32[]{:S(2)}) collective-permute-start(bf16[1200,128]{1,0:T(8,128)(2,1)S(1)} %get-tuple-element.33), channel_id=1, source_target_pairs={{0,4},{2,6},{4,0},{6,2},{8,12},{10,14},{12,8},{14,10},{16,20},{18,... | collective-permute-start | bytes 921608 | tf_op jit(solution)/shard_map/ppermute | solution.py:39
  3.6 1.3 %collective-permute-start.4 = (bf16[1200,128]{1,0:T(8,128)(2,1)S(1)}, bf16[1200,128]{1,0:T(8,128)(2,1)S(1)}, u32[]{:S(2)}, u32[]{:S(2)}) collective-permute-start(bf16[1200,128]{1,0:T(8,128)(2,1)S(1)} %get-tuple-element.32), channel_id=1, source_target_pairs={{0,8},{2,10},{4,12},{6,14},{8,0},{10,2},{12,4},{14,6},{16,24},{18,... | collective-permute-start | bytes 921608 | tf_op jit(solution)/shard_map/ppermute | solution.py:39
  5.0 0.9 %copy.16.patches_ref = bf16[256,64]{1,0:T(8,128)(2,1)S(1)} copy(bf16[256,64]{0,1:T(8,128)(2,1)} %param.12) | data formatting | bytes 65536 | tf_op args[0]
  6.0 1.3 %collective-permute-start.2 = (bf16[112,1280]{1,0:T(8,128)(2,1)S(1)}, bf16[112,1280]{1,0:T(8,128)(2,1)S(1)}, u32[]{:S(2)}, u32[]{:S(2)}) collective-permute-start(bf16[112,1280]{1,0:T(8,128)(2,1)S(1)} %get-tuple-element.30.own_ref.own_part_ref.here_ref), channel_id=1, source_target_pairs={{0,1},{1,0},{2,3},{3,2},{4,5},{5,4},{6,7},{7,6},{8,9},{9,8},{10,11... | collective-permute-start | bytes 860168 | tf_op jit(solution)/shard_map/ppermute | solution.py:749
  7.3 1.2 %collective-permute-start.1 = (bf16[256,64]{1,0:T(8,128)(2,1)S(1)}, bf16[256,64]{1,0:T(8,128)(2,1)S(1)}, u32[]{:S(2)}, u32[]{:S(2)}) collective-permute-start(bf16[256,64]{1,0:T(8,128)(2,1)S(1)} %get-tuple-element.29.mine_ref), channel_id=1, source_target_pairs={{0,2},{2,0},{4,6},{6,4},{8,10},{10,8},{12,14},{14,12},{16,18},{18,... | collective-permute-start | bytes 98312 | tf_op jit(solution)/shard_map/ppermute | solution.py:39
  8.5 5.0 %collective-permute-done.2.other_ref.other_part_ref.there_ref = bf16[112,1280]{1,0:T(8,128)(2,1)S(1)} collective-permute-done((bf16[112,1280]{1,0:T(8,128)(2,1)S(1)}, bf16[112,1280]{1,0:T(8,128)(2,1)S(1)}, u32[]{:S(2)}, u32[]{:S(2)}) %collective-permute-start.2) | collective-permute-done | bytes 286752 | tf_op jit(solution)/shard_map/ppermute | solution.py:749
  13.5 0.8 %modulated_rows.1.refs_1_.rows_ref = bf16[320,1280]{1,0:T(8,128)(2,1)S(1)} custom-call(bf16[112,1280]{1,0:T(8,128)(2,1)S(1)} %get-tuple-element.30.own_ref.own_part_ref.here_ref, bf16[112,1280]{1,0:T(8,128)(2,1)S(1)} %collective-permute-done.2.other_ref.other_part_ref.there_ref, bf16[112,1280]{1,0:T(8,128)(2,1)S(1)} %get-tuple-element.30.own_ref.own_part_ref.here_ref, ...), custom_call_target="tpu_custom_call" | custom-call | tf_op jit(solution)/shard_map/modulated_rows/pallas_call | solution.py:232
  14.4 1.9 %collective-permute-start.7 = (bf16[1200,128]{1,0:T(8,128)(2,1)S(1)}, bf16[1200,128]{1,0:T(8,128)(2,1)S(1)}, u32[]{:S(2)}, u32[]{:S(2)}) collective-permute-start(bf16[1200,128]{1,0:T(8,128)(2,1)S(1)} %after.5.refs_3_), channel_id=1, source_target_pairs={{0,2},{2,0},{4,6},{6,4},{8,10},{10,8},{12,14},{14,12},{16,18},{18,... | collective-permute-start | bytes 921608 | tf_op jit(solution)/shard_map/ppermute | solution.py:39
  16.4 2.3 %collective-permute-done.3.refs_0_ = bf16[1200,128]{1,0:T(8,128)(2,1)S(1)} collective-permute-done((bf16[1200,128]{1,0:T(8,128)(2,1)S(1)}, bf16[1200,128]{1,0:T(8,128)(2,1)S(1)}, u32[]{:S(2)}, u32[]{:S(2)}) %collective-permute-start.3) | collective-permute-done | bytes 307232 | tf_op jit(solution)/shard_map/ppermute | solution.py:39
  18.6 1.2 %collective-permute-start.8 = (bf16[1200,128]{1,0:T(8,128)(2,1)S(1)}, bf16[1200,128]{1,0:T(8,128)(2,1)S(1)}, u32[]{:S(2)}, u32[]{:S(2)}) collective-permute-start(bf16[1200,128]{1,0:T(8,128)(2,1)S(1)} %after.3.refs_0_), channel_id=1, source_target_pairs={{0,2},{2,0},{4,6},{6,4},{8,10},{10,8},{12,14},{14,12},{16,18},{18,... | collective-permute-start | bytes 921608 | tf_op jit(solution)/shard_map/ppermute | solution.py:39
  19.8 1.0 %early_rows.1.early_ref = f32[320,1024]{1,0:T(8,128)S(1)} custom-call(bf16[320,1280]{1,0:T(8,128)(2,1)S(1)} %modulated_rows.1.refs_1_.rows_ref, bf16[1200,128]{1,0:T(8,128)(2,1)S(1)} %after.3.refs_0_, bf16[1200,128]{1,0:T(8,128)(2,1)S(1)} %after.4.refs_1_, bf16[1200,128]{1,0:T(8,128)(2,1)S(1)} %collective-permute-done.5.refs_2_, ...), custom_call_target="tpu_custom_call" | custom-call | tf_op jit(solution)/shard_map/early_rows/pallas_call | solution.py:279
  21.5 1.3 %collective-permute-start.10 = (bf16[64,1024]{1,0:T(8,128)(2,1)S(1)}, bf16[64,1024]{1,0:T(8,128)(2,1)S(1)}, u32[]{:S(2)}, u32[]{:S(2)}) collective-permute-start(bf16[64,1024]{1,0:T(8,128)(2,1)S(1)} %get-tuple-element.36), channel_id=1, source_target_pairs={{0,16},{2,20},{4,18},{6,22},{8,24},{10,28},{12,26},{14,30},{16,0},... | collective-permute-start | bytes 393224 | tf_op jit(solution)/shard_map/ppermute | solution.py:780
  22.8 1.3 %collective-permute-start.11 = (bf16[64,1024]{1,0:T(8,128)(2,1)S(1)}, bf16[64,1024]{1,0:T(8,128)(2,1)S(1)}, u32[]{:S(2)}, u32[]{:S(2)}) collective-permute-start(bf16[64,1024]{1,0:T(8,128)(2,1)S(1)} %get-tuple-element.37), channel_id=1, source_target_pairs={{0,14},{2,10},{4,12},{6,8},{8,6},{10,2},{12,4},{14,0},{16,30},{18,... | collective-permute-start | bytes 393224 | tf_op jit(solution)/shard_map/ppermute | solution.py:780
  24.1 1.3 %collective-permute-start.12 = (bf16[64,1024]{1,0:T(8,128)(2,1)S(1)}, bf16[64,1024]{1,0:T(8,128)(2,1)S(1)}, u32[]{:S(2)}, u32[]{:S(2)}) collective-permute-start(bf16[64,1024]{1,0:T(8,128)(2,1)S(1)} %get-tuple-element.38), channel_id=1, source_target_pairs={{0,30},{2,26},{4,28},{6,24},{8,22},{10,18},{12,20},{14,16},{16,14}... | collective-permute-start | bytes 393224 | tf_op jit(solution)/shard_map/ppermute | solution.py:780
  25.4 2.7 %collective-permute-start.9 = (bf16[64,1024]{1,0:T(8,128)(2,1)S(1)}, bf16[64,1024]{1,0:T(8,128)(2,1)S(1)}, u32[]{:S(2)}, u32[]{:S(2)}) collective-permute-start(bf16[64,1024]{1,0:T(8,128)(2,1)S(1)} %get-tuple-element.34.ready_ref), channel_id=1, source_target_pairs={{0,0},{2,4},{4,2},{6,6},{8,8},{10,12},{12,10},{14,14},{16,16},{18,... | collective-permute-start | bytes 393224 | tf_op jit(solution)/shard_map/ppermute | solution.py:780
  28.2 3.7 %spread_rows.1 = (bf16[512,128]{1,0:T(8,128)(2,1)S(1)}, bf16[128,512]{1,0:T(8,128)(2,1)S(1)}, f32[512,128]{1,0:T(8,128)S(1)}, f32[512,128]{1,0:T(8,128)S(1)}, f3...) custom-call(s32[8,3]{1,0:T(8,128)S(1)} %copy.17.shape_ref, s32[16]{0:T(128)S(1)} %copy-done.4, ...), custom_call_target="tpu_custom_call" | custom-call | tf_op jit(solution)/shard_map/spread_rows/pallas_call | solution.py:539
  32.0 5.2 %collective-permute-done.12.refs_3_ = bf16[64,1024]{1,0:T(8,128)(2,1)S(1)} collective-permute-done((bf16[64,1024]{1,0:T(8,128)(2,1)S(1)}, bf16[64,1024]{1,0:T(8,128)(2,1)S(1)}, u32[]{:S(2)}, u32[]{:S(2)}) %collective-permute-start.12) | collective-permute-done | bytes 131104 | tf_op jit(solution)/shard_map/ppermute | solution.py:780
  37.2 0.5 %sum_rows.1 = (bf16[2,72,1152]{2,1,0:T(8,128)(2,1)S(1)}, f32[72,128]{1,0:T(8,128)S(1)}, bf16[72,128]{1,0:T(8,128)(2,1)S(1)}) custom-call(bf16[64,1024]{1,0:T(8,128)(2,1)S(1)} %collective-permute-done.9.refs_0_, bf16[64,1024]{1,0:T(8,128)(2,1)S(1)} %collective-permute-done.10.refs_1_, bf16[64,1024]{1,0:T(8,128)(2,1)S(1)} %collective-permute-done.11.refs_2_, ...), custom_call_target="tpu_custom_call" | custom-call | tf_op jit(solution)/shard_map/sum_rows/pallas_call | solution.py:413
  37.7 0.5 %collective-permute-start.13 = (bf16[2,72,1152]{2,1,0:T(8,128)(2,1)S(1)}, bf16[2,72,1152]{2,1,0:T(8,128)(2,1)S(1)}, u32[]{:S(2)}, u32[]{:S(2)}) collective-permute-start(bf16[2,72,1152]{2,1,0:T(8,128)(2,1)S(1)} %get-tuple-element.40.mine_ref), channel_id=1, source_target_pairs={{0,2},{2,0},{4,6},{6,4},{8,10},{10,8},{12,14},{14,12},{16,18},{18,... | collective-permute-start | bytes 995336 | tf_op jit(solution)/shard_map/ppermute | solution.py:39
  38.2 1.2 %collective-permute-start.14 = (bf16[72,128]{1,0:T(8,128)(2,1)S(1)}, bf16[72,128]{1,0:T(8,128)(2,1)S(1)}, u32[]{:S(2)}, u32[]{:S(2)}) collective-permute-start(bf16[72,128]{1,0:T(8,128)(2,1)S(1)} %get-tuple-element.50), channel_id=1, source_target_pairs={{0,1},{1,0},{2,3},{3,2},{4,5},{5,4},{6,7},{7,6},{8,9},{9,8},{10,11... | collective-permute-start | bytes 55304 | tf_op jit(solution)/shard_map/ppermute | solution.py:802
  40.0 2.3 %heads_rows.1 = (f32[256,1280]{1,0:T(8,128)S(1)}, bf16[512,1280]{1,0:T(8,128)(2,1)S(1)}, bf16[512,1280]{1,0:T(8,128)(2,1)S(1)}) custom-call(s32[16]{0:T(128)S(1)} %copy-done.4, bf16[512,128]{1,0:T(8,128)(2,1)S(1)} %get-tuple-element.35.refs_5_.left_ref, bf16[2,72,1152]{2,1,0:T(8,128)(2,1)S(1)} %get-tuple-element.40.mine_ref, ...), custom_call_target="tpu_custom_call" | custom-call | tf_op jit(solution)/shard_map/heads_rows/pallas_call | solution.py:622
  42.7 3.3 %attend_rows.1 = bf16[256,1280]{1,0:T(8,128)(2,1)} custom-call(s32[16]{0:T(128)S(1)} %copy-done.4, f32[256,1280]{1,0:T(8,128)S(1)} %get-tuple-element.45.q_ref, bf16[512,1280]{1,0:T(8,128)(2,1)S(1)} %get-tuple-element.46.k_ref, bf16[512,1280]{1,0:T(8,128)(2,1)S(1)} %get-tuple-element.47.v_ref, bf16[512,128]{1,0:T(8,128)(2,1)S(1)} %get-tuple-element.35.refs_5_.left_ref, ...), custom_call_target="tpu_custom_call" | custom-call | tf_op jit(solution)/shard_map/attend_rows/pallas_call | solution.py:700
  (43 shorter events, 2.0 us)
Async XLA Ops:
  0.0 5.9 %copy-start = (bf16[64,1280]{1,0:T(8,128)(2,1)S(1)}, bf16[64,1280]{1,0:T(8,128)(2,1)}, u32[]{:S(2)}) copy-start(bf16[64,1280]{1,0:T(8,128)(2,1)} %weight_ref.1) | copy-start | bytes 491524
  0.0 5.9 %copy-start.1 = (f32[8,2,1280]{2,1,0:T(2,128)S(1)}, f32[8,2,1280]{2,1,0:T(2,128)}, u32[]{:S(2)}) copy-start(f32[8,2,1280]{2,1,0:T(2,128)} %time_ref.1) | copy-start | bytes 245764
  0.0 5.9 %copy-start.2 = (f32[2,1280]{1,0:T(2,128)S(1)}, f32[2,1280]{1,0:T(2,128)}, u32[]{:S(2)}) copy-start(f32[2,1280]{1,0:T(2,128)} %block_ref.1) | copy-start | bytes 30724
  1.6 4.3 %collective-permute-start = (bf16[1200,128]{1,0:T(8,128)(2,1)S(1)}, bf16[1200,128]{1,0:T(8,128)(2,1)S(1)}, u32[]{:S(2)}, u32[]{:S(2)}) collective-permute-start(bf16[1200,128]{1,0:T(8,128)(2,1)S(1)} %get-tuple-element.28.refs_5_), channel_id=1, source_target_pairs={{0,2},{2,0},{4,6},{6,4},{8,10},{10,8},{12,14},{14,12},{16,18},{18,... | collective-permute-start | bytes 921608 | tf_op jit(solution)/shard_map/ppermute | solution.py:39
  2.3 12.0 %collective-permute-start.6 = (bf16[1200,128]{1,0:T(8,128)(2,1)S(1)}, bf16[1200,128]{1,0:T(8,128)(2,1)S(1)}, u32[]{:S(2)}, u32[]{:S(2)}) collective-permute-start(bf16[1200,128]{1,0:T(8,128)(2,1)S(1)} %get-tuple-element.33), channel_id=1, source_target_pairs={{0,4},{2,6},{4,0},{6,2},{8,12},{10,14},{12,8},{14,10},{16,20},{18,... | collective-permute-start | bytes 921608 | tf_op jit(solution)/shard_map/ppermute | solution.py:39
  3.6 12.7 %collective-permute-start.4 = (bf16[1200,128]{1,0:T(8,128)(2,1)S(1)}, bf16[1200,128]{1,0:T(8,128)(2,1)S(1)}, u32[]{:S(2)}, u32[]{:S(2)}) collective-permute-start(bf16[1200,128]{1,0:T(8,128)(2,1)S(1)} %get-tuple-element.32), channel_id=1, source_target_pairs={{0,8},{2,10},{4,12},{6,14},{8,0},{10,2},{12,4},{14,6},{16,24},{18,... | collective-permute-start | bytes 921608 | tf_op jit(solution)/shard_map/ppermute | solution.py:39
  4.9 13.7 %collective-permute-start.3 = (bf16[1200,128]{1,0:T(8,128)(2,1)S(1)}, bf16[1200,128]{1,0:T(8,128)(2,1)S(1)}, u32[]{:S(2)}, u32[]{:S(2)}) collective-permute-start(bf16[1200,128]{1,0:T(8,128)(2,1)S(1)} %get-tuple-element.31), channel_id=1, source_target_pairs={{0,12},{2,14},{4,8},{6,10},{8,4},{10,6},{12,0},{14,2},{16,28},{18,... | collective-permute-start | bytes 921608 | tf_op jit(solution)/shard_map/ppermute | solution.py:39
  6.0 7.5 %collective-permute-start.2 = (bf16[112,1280]{1,0:T(8,128)(2,1)S(1)}, bf16[112,1280]{1,0:T(8,128)(2,1)S(1)}, u32[]{:S(2)}, u32[]{:S(2)}) collective-permute-start(bf16[112,1280]{1,0:T(8,128)(2,1)S(1)} %get-tuple-element.30.own_ref.own_part_ref.here_ref), channel_id=1, source_target_pairs={{0,1},{1,0},{2,3},{3,2},{4,5},{5,4},{6,7},{7,6},{8,9},{9,8},{10,11... | collective-permute-start | bytes 860168 | tf_op jit(solution)/shard_map/ppermute | solution.py:749
  7.3 7.1 %collective-permute-start.1 = (bf16[256,64]{1,0:T(8,128)(2,1)S(1)}, bf16[256,64]{1,0:T(8,128)(2,1)S(1)}, u32[]{:S(2)}, u32[]{:S(2)}) collective-permute-start(bf16[256,64]{1,0:T(8,128)(2,1)S(1)} %get-tuple-element.29.mine_ref), channel_id=1, source_target_pairs={{0,2},{2,0},{4,6},{6,4},{8,10},{10,8},{12,14},{14,12},{16,18},{18,... | collective-permute-start | bytes 98312 | tf_op jit(solution)/shard_map/ppermute | solution.py:39
  14.4 5.4 %collective-permute-start.7 = (bf16[1200,128]{1,0:T(8,128)(2,1)S(1)}, bf16[1200,128]{1,0:T(8,128)(2,1)S(1)}, u32[]{:S(2)}, u32[]{:S(2)}) collective-permute-start(bf16[1200,128]{1,0:T(8,128)(2,1)S(1)} %after.5.refs_3_), channel_id=1, source_target_pairs={{0,2},{2,0},{4,6},{6,4},{8,10},{10,8},{12,14},{14,12},{16,18},{18,... | collective-permute-start | bytes 921608 | tf_op jit(solution)/shard_map/ppermute | solution.py:39
  16.3 3.5 %collective-permute-start.5 = (bf16[1200,128]{1,0:T(8,128)(2,1)S(1)}, bf16[1200,128]{1,0:T(8,128)(2,1)S(1)}, u32[]{:S(2)}, u32[]{:S(2)}) collective-permute-start(bf16[1200,128]{1,0:T(8,128)(2,1)S(1)} %after.4.refs_1_), channel_id=1, source_target_pairs={{0,2},{2,0},{4,6},{6,4},{8,10},{10,8},{12,14},{14,12},{16,18},{18,... | collective-permute-start | bytes 921608 | tf_op jit(solution)/shard_map/ppermute | solution.py:39
  18.6 2.4 %collective-permute-start.8 = (bf16[1200,128]{1,0:T(8,128)(2,1)S(1)}, bf16[1200,128]{1,0:T(8,128)(2,1)S(1)}, u32[]{:S(2)}, u32[]{:S(2)}) collective-permute-start(bf16[1200,128]{1,0:T(8,128)(2,1)S(1)} %after.3.refs_0_), channel_id=1, source_target_pairs={{0,2},{2,0},{4,6},{6,4},{8,10},{10,8},{12,14},{14,12},{16,18},{18,... | collective-permute-start | bytes 921608 | tf_op jit(solution)/shard_map/ppermute | solution.py:39
  20.8 7.3 %copy-start.5 = (f32[2560]{0:T(1024)S(1)}, f32[2560]{0:T(1024)}, u32[]{:S(2)}) copy-start(f32[2560]{0:T(1024)} %param.22) | copy-start | bytes 30724
  20.8 7.3 %copy-start.7 = (f32[1280]{0:T(1024)S(1)}, f32[1280]{0:T(1024)}, u32[]{:S(2)}) copy-start(f32[1280]{0:T(1024)} %param.20) | copy-start | bytes 15364
  20.8 7.3 %copy-start.8 = (s32[8,3]{0,1:T(4,128)S(1)}, s32[8,3]{0,1:T(4,128)}, u32[]{:S(2)}) copy-start(s32[8,3]{0,1:T(4,128)} %param.13) | copy-start | bytes 292
  20.9 7.4 %copy-start.3 = (f32[2,1280]{1,0:T(2,128)S(1)}, f32[2,1280]{1,0:T(2,128)}, u32[]{:S(2)}) copy-start(f32[2,1280]{1,0:T(2,128)} %gain_ref.1) | copy-start | bytes 30724
  20.9 7.4 %copy-start.4 = (s32[16]{0:T(128)S(1)}, s32[16]{0:T(128)}, u32[]{:S(2)}) copy-start(s32[16]{0:T(128)} %counts_ref.5) | copy-start | bytes 196
  21.5 10.5 %collective-permute-start.10 = (bf16[64,1024]{1,0:T(8,128)(2,1)S(1)}, bf16[64,1024]{1,0:T(8,128)(2,1)S(1)}, u32[]{:S(2)}, u32[]{:S(2)}) collective-permute-start(bf16[64,1024]{1,0:T(8,128)(2,1)S(1)} %get-tuple-element.36), channel_id=1, source_target_pairs={{0,16},{2,20},{4,18},{6,22},{8,24},{10,28},{12,26},{14,30},{16,0},... | collective-permute-start | bytes 393224 | tf_op jit(solution)/shard_map/ppermute | solution.py:780
  22.8 9.2 %collective-permute-start.11 = (bf16[64,1024]{1,0:T(8,128)(2,1)S(1)}, bf16[64,1024]{1,0:T(8,128)(2,1)S(1)}, u32[]{:S(2)}, u32[]{:S(2)}) collective-permute-start(bf16[64,1024]{1,0:T(8,128)(2,1)S(1)} %get-tuple-element.37), channel_id=1, source_target_pairs={{0,14},{2,10},{4,12},{6,8},{8,6},{10,2},{12,4},{14,0},{16,30},{18,... | collective-permute-start | bytes 393224 | tf_op jit(solution)/shard_map/ppermute | solution.py:780
  24.1 13.1 %collective-permute-start.12 = (bf16[64,1024]{1,0:T(8,128)(2,1)S(1)}, bf16[64,1024]{1,0:T(8,128)(2,1)S(1)}, u32[]{:S(2)}, u32[]{:S(2)}) collective-permute-start(bf16[64,1024]{1,0:T(8,128)(2,1)S(1)} %get-tuple-element.38), channel_id=1, source_target_pairs={{0,30},{2,26},{4,28},{6,24},{8,22},{10,18},{12,20},{14,16},{16,14}... | collective-permute-start | bytes 393224 | tf_op jit(solution)/shard_map/ppermute | solution.py:780
  25.4 11.8 %collective-permute-start.9 = (bf16[64,1024]{1,0:T(8,128)(2,1)S(1)}, bf16[64,1024]{1,0:T(8,128)(2,1)S(1)}, u32[]{:S(2)}, u32[]{:S(2)}) collective-permute-start(bf16[64,1024]{1,0:T(8,128)(2,1)S(1)} %get-tuple-element.34.ready_ref), channel_id=1, source_target_pairs={{0,0},{2,4},{4,2},{6,6},{8,8},{10,12},{12,10},{14,14},{16,16},{18,... | collective-permute-start | bytes 393224 | tf_op jit(solution)/shard_map/ppermute | solution.py:780
  37.7 2.2 %collective-permute-start.13 = (bf16[2,72,1152]{2,1,0:T(8,128)(2,1)S(1)}, bf16[2,72,1152]{2,1,0:T(8,128)(2,1)S(1)}, u32[]{:S(2)}, u32[]{:S(2)}) collective-permute-start(bf16[2,72,1152]{2,1,0:T(8,128)(2,1)S(1)} %get-tuple-element.40.mine_ref), channel_id=1, source_target_pairs={{0,2},{2,0},{4,6},{6,4},{8,10},{10,8},{12,14},{14,12},{16,18},{18,... | collective-permute-start | bytes 995336 | tf_op jit(solution)/shard_map/ppermute | solution.py:39
  38.2 4.0 %collective-permute-start.14 = (bf16[72,128]{1,0:T(8,128)(2,1)S(1)}, bf16[72,128]{1,0:T(8,128)(2,1)S(1)}, u32[]{:S(2)}, u32[]{:S(2)}) collective-permute-start(bf16[72,128]{1,0:T(8,128)(2,1)S(1)} %get-tuple-element.50), channel_id=1, source_target_pairs={{0,1},{1,0},{2,3},{3,2},{4,5},{5,4},{6,7},{7,6},{8,9},{9,8},{10,11... | collective-permute-start | bytes 55304 | tf_op jit(solution)/shard_map/ppermute | solution.py:802
  39.5 3.2 %collective-permute-start.15 = (bf16[72,128]{1,0:T(8,128)(2,1)S(1)}, bf16[72,128]{1,0:T(8,128)(2,1)S(1)}, u32[]{:S(2)}, u32[]{:S(2)}) collective-permute-start(bf16[72,128]{1,0:T(8,128)(2,1)S(1)} %get-tuple-element.50), channel_id=1, source_target_pairs={{0,3},{1,2},{2,1},{3,0},{4,7},{5,6},{6,5},{7,4},{8,11},{9,10},{10,... | collective-permute-start | bytes 55304 | tf_op jit(solution)/shard_map/ppermute | solution.py:803
  (1 other events, 5.9 us)
